TPU v7x, 32 devices: a whole 2x2x4 slice. The times are simulated.
32 devices in a mesh: region: 4 (over z), tile: 8 (over y, x, core).
Axes of the slice: x: 2, y: 2, z: 4, core: 2. Of those that a mesh axis runs over, the one named last changes fastest.
Arguments:
- global_deriv: bfloat16 [6144, 32, 128], P(('region', 'tile')), may hold values from -0.15625 to 0.15625
- local_deriv: bfloat16 [6144, 5, 32], P(('region', 'tile')), may hold values from -4 to 4
- hit_weight: bfloat16 [6144, 32], P(('region', 'tile')), may hold values from 0.25 to 4
- hit_resid: bfloat16 [6144, 32], P(('region', 'tile')), may hold values from -6 to 6
- block_ids: int32 [6144, 32], P(('region', 'tile')), may hold values from 0 to 7
- hit_count: int32 [6144], P(('region', 'tile')), may hold values from 4 to 32
- track_region: int32 [6144, 1], P(('region', 'tile')), may hold values from 0 to 3; in each aligned block of 192 rows (0 to 191, 192 to 383, ...) at most 96 rows name the same one
- block_place: int32 [8], replicated, may hold values from 0 to 7, each once
Outputs:
- normal_matrix: float32 [4, 1024, 1024], P('region', 'tile')
- right_side: float32 [4, 1024], P('region', 'tile')
Inputs may be any that keep to these rules, and one draw needn't show every extreme that they name: `track_region`: among the tracks of one device at most 96 share a region, and in every draw some device has exactly 96 tracks in some region. `block_place`: each position appears once.
All inputs are finite; a program needn't handle non-finite values.
Results may differ from a plain program's by a relative error of at most 0.0029.
Values may be sent and summed in bfloat16 or wider, within the bound.
No kernel may reach another device: no remote copies, remote signals or barrier semaphores. Data moves between devices by JAX's collectives and lax.ppermute only.
A program may use at most 128 MiB of HBM per device.

v0:
```python
import functools
import jax
import jax.numpy as jnp
from jax import lax
from jax.experimental import pallas as pl
from jax.experimental.pallas import tpu as pltpu
from jax.sharding import PartitionSpec as P

F32 = jnp.float32
BF16 = jnp.bfloat16
GROUP = 8
PAIR = 2 * GROUP
DEPTH = 256

NT = (((1,), (1,)), ((), ()))


def iota(shape, axis):
    return lax.broadcasted_iota(jnp.int32, shape, axis)


def fit(ld, weight, resid, counts):
    hits = weight.shape[0]
    live = iota(weight.shape, 0) < counts.astype(jnp.int32)
    masked_w = jnp.where(live, weight, 0.0)
    weighted_l = [v * masked_w for v in ld]
    gamma = [[None] * 5 for _ in range(5)]
    for a in range(5):
        for b in range(a + 1):
            gamma[a][b] = jnp.sum(weighted_l[a] * ld[b], axis=0, keepdims=True)
            if a == b:
                gamma[a][b] = gamma[a][b] + 1.0
    beta = [jnp.sum(weighted_l[a] * resid, axis=0, keepdims=True) for a in range(5)]
    factor = [[None] * 5 for _ in range(5)]
    inverse = [None] * 5
    for j in range(5):
        center = gamma[j][j]
        for k in range(j):
            center = center - factor[j][k] * factor[j][k]
        factor[j][j] = jnp.sqrt(center)
        inverse[j] = 1.0 / factor[j][j]
        for i in range(j + 1, 5):
            offdiag = gamma[i][j]
            for k in range(j):
                offdiag = offdiag - factor[i][k] * factor[j][k]
            factor[i][j] = offdiag * inverse[j]
    solved, rhs = [], []
    for j in range(5):
        current, target = weighted_l[j], beta[j]
        for k in range(j):
            current = current - factor[j][k] * solved[k]
            target = target - factor[j][k] * rhs[k]
        solved.append(current * inverse[j])
        rhs.append(target * inverse[j])
    projection = solved[0] * rhs[0]
    for k in range(1, 5):
        projection = projection + solved[k] * rhs[k]
    return solved, masked_w * resid - projection, masked_w


def prepare(blocks, floats_ref, numbers_ref, scaled_ref, lanes_ref, column_ref, table_ref):
    tracks = floats_ref.shape[1]
    groups, _, depth = scaled_ref.shape
    slots = groups * GROUP
    hits = depth // GROUP
    count_row, region_row = (numbers_ref[hits + n : hits + n + 1, :] for n in range(2))
    rr = table_ref.shape[0] - 8
    member = (iota((rr, tracks), 0) == region_row).astype(F32)
    before = (iota((tracks, tracks), 0) < iota((tracks, tracks), 1)).astype(F32).astype(BF16)
    rank = jnp.dot(member.astype(BF16), before, preferred_element_type=F32)
    count = jnp.sum(member, axis=1, keepdims=True)
    room = (count.astype(jnp.int32) + (PAIR - 1)) & -PAIR
    room = jnp.broadcast_to(room.astype(F32), (rr, slots))
    lower = (iota((rr, rr), 1) < iota((rr, rr), 0)).astype(F32)
    start = jnp.zeros((rr, slots), F32)
    for g in range(rr):
        start = start + lower[:, g : g + 1] * room[g : g + 1, :]
    slot = jnp.sum(member * (rank + start[:, 0:1]), axis=0, keepdims=True)
    perm = (iota((slots, tracks), 0) == slot.astype(jnp.int32)).astype(F32).astype(BF16)
    numbers = jnp.where(
        iota((8, tracks), 0) == 0, iota((8, tracks), 1), jnp.broadcast_to(count_row, (8, tracks))
    )

    def sort(value):
        return lax.dot_general(value, perm, NT, preferred_element_type=F32)

    numbers = sort(numbers.astype(F32).astype(BF16))
    table_ref[0:8, :] = numbers.astype(jnp.int32)
    table_ref[8:, :] = jnp.where(
        iota((rr, slots), 1) == 0, start.astype(jnp.int32), (start + room).astype(jnp.int32)
    )
    flat = sort(floats_ref[...])
    flat = [flat[c * hits : (c + 1) * hits] for c in range(7)]
    solved, hit_factor, masked_w = fit(flat[:5], flat[5], flat[6], numbers[1:2])
    ids = sort(numbers_ref[:hits, :].astype(F32).astype(BF16))
    places = [numbers_ref[hits + 2 + b : hits + 3 + b, 0:1].astype(F32) for b in range(blocks)]
    position = jnp.zeros_like(ids)
    for b in range(blocks):
        position = jnp.where(ids == float(b), places[b], position)
    own = (iota((depth, slots), 0) // hits) == (iota((depth, slots), 1) % GROUP)

    def spread_out(value):
        return jnp.where(own, jnp.concatenate([value] * GROUP, axis=0), 0.0)

    grouping = (iota((groups, slots), 1) // GROUP == iota((groups, slots), 0)).astype(F32)
    for n, value in enumerate((masked_w, hit_factor)):
        lanes_ref[n] = lax.dot_general(
            grouping.astype(BF16), spread_out(value).astype(BF16), NT, preferred_element_type=F32
        )
    columns = column_ref.shape[1]
    grouping = (iota((columns, slots), 1) // GROUP == iota((columns, slots), 0)).astype(F32)
    column_ref[...] = lax.dot_general(
        spread_out(position).astype(BF16), grouping.astype(BF16), NT, preferred_element_type=F32
    )
    for c in range(5):
        scaled_ref[:, c * GROUP : (c + 1) * GROUP, :] = spread_out(solved[c]).T.reshape(
            groups, GROUP, depth
        )


def one_step(step, at, table_ref, g_ref, scaled_ref, lanes_ref, column_ref, g_s, direct_s, spread_s):
    hits, width = g_ref.shape[1:]
    depth = GROUP * hits
    blocks = spread_s.shape[1] // width
    rows = 5 * GROUP
    head = width + 8
    unit = (iota((width, width), 0) == iota((width, width), 1)).astype(F32).astype(BF16)
    lefts, values, positions = [], [], []
    for u in range(2):
        group = step * 2 + u
        for i in range(GROUP):
            g_s[u, i * hits : (i + 1) * hits, :] = g_ref[table_ref[0, group * GROUP + i]]
        g = g_s[u]
        chosen = jnp.full(column_ref.shape, group, jnp.int32)
        position = jnp.take_along_axis(column_ref[...], chosen, axis=1, mode="promise_in_bounds")
        turned = lax.dot_general(unit, g, NT, preferred_element_type=F32)
        weighted = turned * lanes_ref[0, pl.ds(group, 1), :]
        factor = jnp.where(iota((8, depth), 0) == 0, lanes_ref[1, pl.ds(group, 1), :], 0.0)
        scaled = scaled_ref[group]
        high = scaled.astype(BF16).astype(F32)
        left = jnp.concatenate(
            [weighted, factor, high, scaled - high, jnp.zeros((8, depth), F32)], axis=0
        )
        lefts.append(left.astype(BF16))
        values.append(g)
        positions.append(position.astype(BF16))
    for p in range(0, blocks, 2):
        columns = slice(p * width, (p + 2) * width)
        direct = direct_s[:, columns]
        for u in range(2):
            right = jnp.concatenate(
                [
                    jnp.where(positions[u] == jnp.bfloat16(q), values[u], jnp.bfloat16(0))
                    for q in (p, p + 1)
                ],
                axis=1,
            )
            total = jnp.dot(lefts[u], right, preferred_element_type=F32)
            direct = direct + total[:head]
            spread_s[pl.ds(pl.multiple_of(at + u * rows, GROUP), rows), columns] = (
                total[head : head + rows] + total[head + rows : head + 2 * rows]
            )
        direct_s[:, columns] = direct


EVEN = (0, 4, 2, 6)
ODD = (0, 2, 4, 6)


def lead_kernel(
    ks, sub, blocks, floats_ref, numbers_ref, g_ref,
    keep_ref, send_ref, scaled_ref, lanes_ref, column_ref, table_ref, table_s, sem, *scratch,
):
    prepare(blocks, floats_ref, numbers_ref, scaled_ref, lanes_ref, column_ref, table_ref)
    copy = pltpu.make_async_copy(table_ref, table_s, sem)
    copy.start()
    copy.wait()

    def region(n, carry):
        assemble_region(
            n, ks, sub, table_s, scaled_ref, lanes_ref, column_ref, g_ref, keep_ref, send_ref,
            *scratch,
        )
        return carry

    lax.fori_loop(0, len(ks), region, 0)


def follow_kernel(ks, sub, blocks, scaled_ref, lanes_ref, column_ref, table_ref, g_ref, *refs):
    def region(n, carry):
        assemble_region(n, ks, sub, table_ref, scaled_ref, lanes_ref, column_ref, g_ref, *refs)
        return carry

    if len(ks) == 1:
        region(0, 0)
    else:
        lax.fori_loop(0, len(ks), region, 0)


def assemble_region(
    number, ks, sub, table_ref, scaled_ref, lanes_ref, column_ref, g_ref,
    keep_ref, send_ref, g_s, direct_s, spread_s, wide_s, turned_s, acc_s,
):
    k = jnp.where(number == 0, ks[0], ks[-1])
    width = g_ref.shape[2]
    blocks = spread_s.shape[1] // width
    many = blocks // 2
    region = lax.axis_index("region") ^ k
    block = lax.axis_index("tile") // sub
    first = table_ref[8 + region, 0] // PAIR
    steps = table_ref[8 + region, 1] // PAIR - first
    direct_s[...] = jnp.zeros_like(direct_s)

    def group_step(n, carry):
        one_step(
            first + n, n * (10 * GROUP), table_ref, g_ref, scaled_ref, lanes_ref, column_ref,
            g_s, direct_s, spread_s,
        )
        return carry

    lax.fori_loop(0, steps, group_step, 0)
    used = steps * 10
    depth_tiles = DEPTH // 8
    chunks = jnp.maximum((used + depth_tiles - 1) // depth_tiles, 1)

    def clear(tile, carry):
        spread_s[pl.ds(pl.multiple_of(tile * 8, 8), 8), :] = jnp.zeros((8, blocks * width), F32)
        return carry

    lax.fori_loop(used, chunks * depth_tiles, clear, 0)

    unit = (iota((width, width), 0) == iota((width, width), 1)).astype(F32).astype(BF16)

    def chunk_step(chunk, carry):
        at = pl.multiple_of(chunk * DEPTH, DEPTH)
        wide_s[...] = spread_s[pl.ds(at, DEPTH), :].astype(BF16)
        for p in range(blocks):
            turned = lax.dot_general(
                unit, wide_s[:, p * width : (p + 1) * width], NT, preferred_element_type=F32
            )
            turned = (0.0 - turned).astype(BF16)
            turned_s[p * width : (p + 1) * width] = turned
            if p < many:
                turned_s[(blocks + p) * width : (blocks + p + 1) * width] = turned

        def products(add):
            for q in range(0, blocks, 2):
                upper = (q + blocks - many) % blocks
                value = jnp.dot(
                    turned_s[upper * width : (upper + many + 2) * width],
                    wide_s[:, q * width : (q + 2) * width],
                    preferred_element_type=F32,
                )
                for r in range(many + 2):
                    p = (upper + r) % blocks
                    for c in range(2):
                        d = many - r + c
                        if 0 <= d <= many and (d < many or p < many):
                            part = value[r * width : (r + 1) * width, c * width : (c + 1) * width]
                            columns = slice(d * width, (d + 1) * width)
                            acc_s[p, :, columns] = acc_s[p, :, columns] + part if add else part

        @pl.when(chunk == 0)
        def _():
            products(False)

        @pl.when(chunk > 0)
        def _():
            products(True)

        return carry

    lax.fori_loop(0, chunks, chunk_step, 0)
    half = width // 2
    for n in range(blocks // 2):
        for odd, out_ref in ((0, keep_ref), (1, send_ref)):
            p = block ^ (jnp.where(block % 2 == 1 - odd, ODD[n], EVEN[n]) + odd)
            columns = pl.ds(pl.multiple_of(p * width, width), width)
            parts = [direct_s[0:width, columns] + acc_s[p, :, 0:width]]
            parts += [acc_s[p, :, d * width : (d + 1) * width] for d in range(1, many)]
            upper = pl.multiple_of((p // many) * half, half)
            parts.append(acc_s[p % many, pl.ds(upper, half), many * width :])
            row = direct_s[width : width + 1, columns]
            high = row.astype(BF16).astype(F32)
            sub = iota((16, width), 0)
            parts.append(jnp.where(sub == 0, high, jnp.where(sub == 1, row - high, 0.0)))
            out_ref[n, number] = jnp.concatenate(parts, axis=0).astype(BF16)


def assemble(ks, sub, inputs, g, blocks, regions):
    tracks, hits, width = g.shape
    lead = len(inputs) == 2
    rows = width * (blocks // 2) + width // 2 + 16
    longest = -(-(-(-tracks // PAIR) * 5 * PAIR) // DEPTH) * DEPTH
    rr = -(-regions // 8) * 8
    slots = -(-(tracks + regions * (PAIR - 1)) // 128) * 128
    shared = [
        jax.ShapeDtypeStruct((slots // GROUP, 5 * GROUP, GROUP * hits), F32),
        jax.ShapeDtypeStruct((2, slots // GROUP, GROUP * hits), F32),
        jax.ShapeDtypeStruct((GROUP * hits, 128), F32),
        jax.ShapeDtypeStruct((8 + rr, slots), jnp.int32),
    ]
    out = jax.ShapeDtypeStruct((blocks // 2, len(ks), rows, width), BF16)
    vmem = pl.BlockSpec(memory_space=pltpu.VMEM)
    smem = pl.BlockSpec(memory_space=pltpu.SMEM)
    local_table = [pltpu.SMEM(shared[3].shape, jnp.int32), pltpu.SemaphoreType.DMA]
    return pl.pallas_call(
        functools.partial(lead_kernel if lead else follow_kernel, ks, sub, blocks),
        in_specs=[vmem] * 3 if lead else [vmem, vmem, vmem, smem, vmem],
        out_specs=[vmem] * (6 if lead else 2),
        out_shape=[out, out] + shared * lead,
        scratch_shapes=local_table * lead
        + [
            pltpu.VMEM((2, GROUP * hits, width), BF16),
            pltpu.VMEM((width + 8, blocks * width), F32),
            pltpu.VMEM((longest, blocks * width), F32),
            pltpu.VMEM((DEPTH, blocks * width), BF16),
            pltpu.VMEM(((blocks + blocks // 2) * width, DEPTH), BF16),
            pltpu.VMEM((blocks, width, (blocks // 2 + 1) * width), F32),
        ],
        compiler_params=pltpu.CompilerParams(vmem_limit_bytes=28 * 1024 * 1024),
        cost_estimate=pl.CostEstimate(
            flops=10**9 * len(ks), bytes_accessed=4 * 10**6, transcendentals=0
        ),
        name="assemble",
    )(*inputs, g)


def finish_kernel(sub, own_ref, r1_ref, r2_ref, r3_ref, e_ref, out_ref, vec_ref):
    width = own_ref.shape[1]
    p = lax.axis_index("tile") // sub
    blocks = out_ref.shape[1] // width
    many = blocks // 2

    def put(column, value):
        column = pl.multiple_of(((column + blocks) % blocks) * width, width)
        out_ref[:, pl.ds(column, width)] = value

    for d in range(many):
        put(p + d, own_ref[d * width : (d + 1) * width, :])
    for d, ref in ((1, r1_ref), (2, r2_ref), (3, r3_ref)):
        put(p - d, ref[...].astype(F32).T)
    tail = many * width + width // 2
    mine = own_ref[many * width : tail, :]
    other = e_ref[...].astype(F32)

    @pl.when(p < many)
    def _():
        put(p + many, jnp.concatenate([mine, other], axis=0))

    @pl.when(p >= many)
    def _():
        put(p + many, jnp.concatenate([other, mine], axis=0).T)

    vec_ref[...] = own_ref[tail : tail + 1, :] + own_ref[tail + 1 : tail + 2, :]


def finish(sub, own, r1, r2, r3, ext, blocks):
    width = own.shape[1]
    vmem = pl.BlockSpec(memory_space=pltpu.VMEM)
    return pl.pallas_call(
        functools.partial(finish_kernel, sub),
        in_specs=[vmem] * 5,
        out_specs=[vmem, vmem],
        out_shape=[
            jax.ShapeDtypeStruct((width, blocks * width), F32),
            jax.ShapeDtypeStruct((1, width), F32),
        ],
        compiler_params=pltpu.CompilerParams(vmem_limit_bytes=8 * 1024 * 1024),
        name="finish",
    )(own, r1, r2, r3, ext)


def local(
    tiles, global_deriv, local_deriv, hit_weight, hit_resid, block_ids, hit_count, track_region,
    block_place,
):
    regions = lax.axis_size("region")
    tracks, hits, width = global_deriv.shape
    blocks = block_place.shape[0]
    sub = tiles // blocks
    tile = lax.axis_index("tile")
    floats = [local_deriv.transpose(1, 2, 0).reshape(-1, tracks), hit_weight.T, hit_resid.T]
    numbers = [
        block_ids.T,
        hit_count.reshape(1, tracks),
        track_region.reshape(1, tracks),
        jnp.broadcast_to(block_place[:, None], (blocks, tracks)),
    ]
    inputs = (jnp.concatenate(floats, axis=0), jnp.concatenate(numbers, axis=0))

    def swap(value, even, odd):
        pairs = [(t, t ^ (sub * (odd if t // sub % 2 else even))) for t in range(tiles)]
        return lax.ppermute(value, "tile", pairs)

    def across(value, k):
        return lax.ppermute(value.astype(BF16), "region", [(r, r ^ k) for r in range(regions)])

    def near(keep, send):
        bit = 1
        while bit < sub:
            pairs = [(t, t ^ bit) for t in range(tiles)]
            keep, send = (v + lax.ppermute(v, "tile", pairs) for v in (keep, send))
            bit *= 2
        return keep, swap(send, 1, 1)

    def both(pair, part):
        return pair[0][part].astype(F32) + pair[1][part].astype(F32)

    low, top = slice(0, blocks // 4), slice(blocks // 4, blocks // 2)
    def upper(pair):
        return swap(both(pair, top).astype(BF16), 2, 4)

    def lower(pair, more):
        value = both(pair, low) + more.astype(F32)
        return value[0], swap(value[1].astype(BF16), 4, 2)

    groups = [(k + 1, k) for k in range(regions - 2, 0, -2)] + [(1,), (0,)]
    totals, cores, firsts, seconds = [None] * regions, [], [], []

    def after(value, other):
        return lax.optimization_barrier((value, other))[0]

    def settle(n):
        value = seconds[n][0] + seconds[n][1].astype(F32)
        for place, k in enumerate(groups[n]):
            totals[k] = value[place]

    last = len(groups) - 1
    for n, ks in enumerate(groups):
        keep, send, *made = assemble(ks, sub, inputs, global_deriv, blocks, regions)
        if n == 0:
            inputs = tuple(made)
            cores.append(near(keep, send))
            continue
        table = after(inputs[3], send)
        cores[n - 1] = after(cores[n - 1], send)
        if n > 1:
            firsts[n - 2] = after(firsts[n - 2], send)
            send = after(send, cores[n - 1][1])
            seconds.append(lower(cores[n - 2], firsts[n - 2]))
            settle(n - 2)
        if n < last:
            operand = both(cores[n - 1], top).astype(BF16)
            table = after(table, operand)
            firsts.append(swap(operand, 2, 4))
        inputs = inputs[:3] + (table,)
        cores.append(near(keep, send))
    operand = after(both(cores[last - 1], top).astype(BF16), cores[last][1])
    firsts.append(swap(operand, 2, 4))
    operand = both(cores[last], top).astype(BF16)
    firsts[last - 1] = after(firsts[last - 1], operand)
    value = both(cores[last - 1], low) + firsts[last - 1].astype(F32)
    half, more = value[0], value[1].astype(BF16)
    firsts.append(swap(operand, 2, 4))
    seconds.append((half, after(swap(more, 4, 2), firsts[last])))
    settle(last - 1)
    crossed = []
    for k in range(regions - 1, 1, -1):
        step = k & -k
        operand = totals[k].astype(BF16)
        if k == 2:
            firsts[last] = after(firsts[last], operand)
        value = across(operand, step)
        if k == 3:
            value = after(value, more)
        if k == step:
            crossed.append(value)
        else:
            totals[k - step] = totals[k - step] + value.astype(F32)
    seconds.append(lower(cores[last], firsts[last]))
    settle(last)
    own = totals[0]
    for value in crossed + [across(totals[1], 1)]:
        own = own + value.astype(F32)

    def onward(value, d):
        pairs = [
            (p * sub + s, ((p + d) % blocks) * sub + s) for p in range(blocks) for s in range(sub)
        ]
        return lax.ppermute(value.astype(BF16), "tile", pairs)

    matrix, vector = finish(
        sub,
        own,
        *(onward(own[d * width : (d + 1) * width], d) for d in range(1, blocks // 2)),
        onward(own[blocks // 2 * width : blocks // 2 * width + width // 2], blocks // 2),
        blocks,
    )
    if sub > 1:
        part = tile % sub
        rows = width // sub
        matrix = lax.dynamic_slice(matrix, (part * rows, 0), (rows, blocks * width))
        vector = lax.dynamic_slice(vector, (0, part * rows), (1, rows))
    return matrix[None], vector


def solution(mesh):
    return jax.shard_map(
        functools.partial(local, mesh.shape["tile"]),
        mesh=mesh,
        in_specs=(
            P(("region", "tile"), None, None),
            P(("region", "tile"), None, None),
            P(("region", "tile"), None),
            P(("region", "tile"), None),
            P(("region", "tile"), None),
            P(("region", "tile")),
            P(("region", "tile"), None),
            P(),
        ),
        out_specs=(P("region", "tile", None), P("region", "tile")),
        check_vma=False,
    )
```

profile of v0, /device:TPU:0, one launch (start us, length us, event | category | flops | bytes accessed | tf_op | source)
XLA Modules:
  0.0 66.0 jit_solution(13972720262112938880)
XLA Ops:
  0.6 0.7 %pad.3.clone = s32[42]{0:T(128)S(1)} pad(s32[8]{0:T(128)} %param.15, s32[]{:T(128)} %constant), padding=34_0 | pad | bytes 204 | tf_op jit(solution)/shard_map/concatenate | solution.py:390
  1.4 0.9 %pad_maximum_fusion.floats_ref = bf16[224,192]{1,0:T(8,128)(2,1)S(1)} fusion(bf16[32,192]{1,0:T(8,128)(2,1)} %bitcast.57, bf16[32,192]{1,0:T(8,128)(2,1)} %bitcast.58, bf16[160,192]{1,0:T(8,128)(2,1)} %bitcast.55), kind=kLoop, calls=%fused_computation.28 | loop fusion | flops 258048 | bytes 172032 | tf_op jit(solution)/shard_map/concatenate | solution.py:390
  2.3 0.9 %add_add_fusion.numbers_ref = s32[42,192]{1,0:T(8,128)S(1)} fusion(s32[1,192]{1,0:T(1,128)} %bitcast.59, s32[1,192]{1,0:T(1,128)} %bitcast.60, s32[32,192]{1,0:T(8,128)} %bitcast.56, s32[42]{0:T(128)S(1)} %pad.3.clone), kind=kLoop, calls=%fused_computation.29 | loop fusion | flops 24192 | bytes 58536 | tf_op jit(solution)/shard_map/concatenate | solution.py:390
  3.2 1.4 %copy-done = bf16[192,32,128]{2,1,0:T(8,128)(2,1)S(1)} copy-done((bf16[192,32,128]{2,1,0:T(8,128)(2,1)S(1)}, bf16[192,32,128]{2,1,0:T(8,128)(2,1)}, u32[]{:S(2)}) %copy-start) | copy-done | bytes 1572888
  4.6 8.8 %assemble.3 = (bf16[4,2,592,128]{3,2,1,0:T(8,128)(2,1)S(1)}, bf16[4,2,592,128]{3,2,1,0:T(8,128)(2,1)S(1)}, f32[32,40,256]{2,1,0:T(8,128)S(1)}, f32[2,32,256]{2,1...) custom-call(bf16[224,192]{1,0:T(8,128)(2,1)S(1)} %pad_maximum_fusion.floats_ref, ...), custom_call_target="tpu_custom_call" | custom-call | flops 2000000000 | bytes 4000000 | tf_op jit(solution)/shard_map/assemble/pallas_call | solution.py:307
  13.4 0.5 collective-permute-start
  13.9 3.1 %assemble.4 = (bf16[4,1,592,128]{3,2,1,0:T(8,128)(2,1)S(1)}, bf16[4,1,592,128]{3,2,1,0:T(8,128)(2,1)S(1)}) custom-call(f32[32,40,256]{2,1,0:T(8,128)S(1)} %get-tuple-element.27.scaled_ref, f32[2,32,256]{2,1,0:T(8,128)S(1)} %get-tuple-element.28.lanes_ref, f32[256,128]{1,0:T(8,128)S(1)} %get-tuple-element.29.column_ref, ...), custom_call_target="tpu_custom_call" | custom-call | flops 1000000000 | bytes 4000000 | tf_op jit(solution)/shard_map/assemble/pallas_call | solution.py:307
  17.1 0.1 collective-permute-start.1
  17.2 0.0 collective-permute-done
  17.2 0.2 add_convert_fusion
  17.3 3.5 %collective-permute-start.4 = (bf16[2,2,592,128]{3,2,1,0:T(8,128)(2,1)S(1)}, bf16[2,2,592,128]{3,2,1,0:T(8,128)(2,1)S(1)}, u32[]{:S(2)}, u32[]{:S(2)}) collective-permute-start(bf16[2,2,592,128]{3,2,1,0:T(8,128)(2,1)S(1)} %add_convert_fusion), channel_id=1, source_target_pairs={{0,2},{1,5},{2,0},{3,7},{4,6},{5,1},{6,4},{7,3},{8,10},{9,13},{10,... | collective-permute-start | bytes 1818632 | tf_op jit(solution)/shard_map/ppermute | solution.py:394
  20.9 3.6 %assemble.5 = (bf16[4,1,592,128]{3,2,1,0:T(8,128)(2,1)S(1)}, bf16[4,1,592,128]{3,2,1,0:T(8,128)(2,1)S(1)}) custom-call(f32[32,40,256]{2,1,0:T(8,128)S(1)} %get-tuple-element.27.scaled_ref, f32[2,32,256]{2,1,0:T(8,128)S(1)} %get-tuple-element.28.lanes_ref, f32[256,128]{1,0:T(8,128)S(1)} %get-tuple-element.29.column_ref, ...), custom_call_target="tpu_custom_call" | custom-call | flops 1000000000 | bytes 4000000 | tf_op jit(solution)/shard_map/assemble/pallas_call | solution.py:307
  24.5 0.0 collective-permute-done.1
  24.5 0.1 collective-permute-start.2
  24.6 4.3 %collective-permute-done.4 = bf16[2,2,592,128]{3,2,1,0:T(8,128)(2,1)S(1)} collective-permute-done((bf16[2,2,592,128]{3,2,1,0:T(8,128)(2,1)S(1)}, bf16[2,2,592,128]{3,2,1,0:T(8,128)(2,1)S(1)}, u32[]{:S(2)}, u32[]{:S(2)}) %collective-permute-start.4) | collective-permute-done | bytes 606240 | tf_op jit(solution)/shard_map/ppermute | solution.py:394
  28.9 0.2 convert_add_fusion
  29.1 1.5 %collective-permute-start.5 = (bf16[2,592,128]{2,1,0:T(8,128)(2,1)S(1)}, bf16[2,592,128]{2,1,0:T(8,128)(2,1)S(1)}, u32[]{:S(2)}, u32[]{:S(2)}) collective-permute-start(bf16[2,592,128]{2,1,0:T(8,128)(2,1)S(1)} %fusion.1), channel_id=1, source_target_pairs={{0,4},{1,3},{2,6},{3,1},{4,0},{5,7},{6,2},{7,5},{8,12},{9,11},{10,... | collective-permute-start | bytes 909320 | tf_op jit(solution)/shard_map/ppermute | solution.py:394
  30.6 0.1 add_convert_fusion.1
  30.7 0.0 collective-permute-done.2
  30.7 1.7 %collective-permute-start.7 = (bf16[2,1,592,128]{3,2,1,0:T(8,128)(2,1)S(1)}, bf16[2,1,592,128]{3,2,1,0:T(8,128)(2,1)S(1)}, u32[]{:S(2)}, u32[]{:S(2)}) collective-permute-start(bf16[2,1,592,128]{3,2,1,0:T(8,128)(2,1)S(1)} %add_convert_fusion.1), channel_id=1, source_target_pairs={{0,2},{1,5},{2,0},{3,7},{4,6},{5,1},{6,4},{7,3},{8,10},{9,13},{10,... | collective-permute-start | bytes 909320 | tf_op jit(solution)/shard_map/ppermute | solution.py:394
  32.4 0.1 add_convert_fusion.2
  32.5 0.5 collective-permute-start.3
  32.9 6.2 %collective-permute-done.5 = bf16[2,592,128]{2,1,0:T(8,128)(2,1)S(1)} collective-permute-done((bf16[2,592,128]{2,1,0:T(8,128)(2,1)S(1)}, bf16[2,592,128]{2,1,0:T(8,128)(2,1)S(1)}, u32[]{:S(2)}, u32[]{:S(2)}) %collective-permute-start.5) | collective-permute-done | bytes 303136 | tf_op jit(solution)/shard_map/ppermute | solution.py:394
  39.2 0.1 fusion
  39.3 2.5 %collective-permute-start.6 = (bf16[592,128]{1,0:T(8,128)(2,1)S(1)}, bf16[592,128]{1,0:T(8,128)(2,1)S(1)}, u32[]{:S(2)}, u32[]{:S(2)}) collective-permute-start(bf16[592,128]{1,0:T(8,128)(2,1)S(1)} %fusion.10), channel_id=1, source_target_pairs={{0,8},{8,0},{16,24},{24,16},{1,9},{9,1},{17,25},{25,17},{2,10},{10... | collective-permute-start | bytes 454664 | tf_op jit(solution)/shard_map/ppermute | solution.py:397
  41.8 0.0 collective-permute-done.7
  41.8 0.1 convert_add_fusion.2
  41.9 2.3 %collective-permute-start.10 = (bf16[1,592,128]{2,1,0:T(8,128)(2,1)S(1)}, bf16[1,592,128]{2,1,0:T(8,128)(2,1)S(1)}, u32[]{:S(2)}, u32[]{:S(2)}) collective-permute-start(bf16[1,592,128]{2,1,0:T(8,128)(2,1)S(1)} %fusion.11), channel_id=1, source_target_pairs={{0,4},{1,3},{2,6},{3,1},{4,0},{5,7},{6,2},{7,5},{8,12},{9,11},{10,... | collective-permute-start | bytes 454664 | tf_op jit(solution)/shard_map/ppermute | solution.py:394
  44.2 1.6 %collective-permute-done.6 = bf16[592,128]{1,0:T(8,128)(2,1)S(1)} collective-permute-done((bf16[592,128]{1,0:T(8,128)(2,1)S(1)}, bf16[592,128]{1,0:T(8,128)(2,1)S(1)}, u32[]{:S(2)}, u32[]{:S(2)}) %collective-permute-start.6) | collective-permute-done | bytes 151584 | tf_op jit(solution)/shard_map/ppermute | solution.py:397
  45.8 3.5 %collective-permute-start.9 = (bf16[592,128]{1,0:T(8,128)(2,1)S(1)}, bf16[592,128]{1,0:T(8,128)(2,1)S(1)}, u32[]{:S(2)}, u32[]{:S(2)}) collective-permute-start(bf16[592,128]{1,0:T(8,128)(2,1)S(1)} %fusion.9), channel_id=1, source_target_pairs={{0,16},{8,24},{16,0},{24,8},{1,17},{9,25},{17,1},{25,9},{2,18},{10... | collective-permute-start | bytes 454664 | tf_op jit(solution)/shard_map/ppermute | solution.py:397
  49.3 0.0 collective-permute-done.3
  49.3 0.1 convert_add_fusion.1
  49.4 2.4 %collective-permute-start.8 = (bf16[1,592,128]{2,1,0:T(8,128)(2,1)S(1)}, bf16[1,592,128]{2,1,0:T(8,128)(2,1)S(1)}, u32[]{:S(2)}, u32[]{:S(2)}) collective-permute-start(bf16[1,592,128]{2,1,0:T(8,128)(2,1)S(1)} %fusion.12), channel_id=1, source_target_pairs={{0,4},{1,3},{2,6},{3,1},{4,0},{5,7},{6,2},{7,5},{8,12},{9,11},{10,... | collective-permute-start | bytes 454664 | tf_op jit(solution)/shard_map/ppermute | solution.py:394
  51.8 0.0 collective-permute-done.10
  51.9 0.4 collective-permute-start.11
  52.2 2.8 %collective-permute-done.8 = bf16[1,592,128]{2,1,0:T(8,128)(2,1)S(1)} collective-permute-done((bf16[1,592,128]{2,1,0:T(8,128)(2,1)S(1)}, bf16[1,592,128]{2,1,0:T(8,128)(2,1)S(1)}, u32[]{:S(2)}, u32[]{:S(2)}) %collective-permute-start.8) | collective-permute-done | bytes 151584 | tf_op jit(solution)/shard_map/ppermute | solution.py:394
  55.0 0.0 collective-permute-done.9
  55.0 2.1 %collective-permute-done.11 = bf16[592,128]{1,0:T(8,128)(2,1)S(1)} collective-permute-done((bf16[592,128]{1,0:T(8,128)(2,1)S(1)}, bf16[592,128]{1,0:T(8,128)(2,1)S(1)}, u32[]{:S(2)}, u32[]{:S(2)}) %collective-permute-start.11) | collective-permute-done | bytes 151584 | tf_op jit(solution)/shard_map/ppermute | solution.py:397
  57.1 0.1 fusion.14
  57.2 0.1 collective-permute-start.12
  57.3 2.5 %collective-permute-start.13 = (bf16[128,128]{1,0:T(8,128)(2,1)S(1)}, bf16[128,128]{1,0:T(8,128)(2,1)S(1)}, u32[]{:S(2)}, u32[]{:S(2)}) collective-permute-start(bf16[128,128]{1,0:T(8,128)(2,1)S(1)} %get-tuple-element.55), channel_id=1, source_target_pairs={{0,2},{1,3},{2,4},{3,5},{4,6},{5,7},{6,0},{7,1},{8,10},{9,11},{10,... | collective-permute-start | bytes 98312 | tf_op jit(solution)/shard_map/ppermute | solution.py:481
  59.7 1.6 %collective-permute-start.14 = (bf16[128,128]{1,0:T(8,128)(2,1)S(1)}, bf16[128,128]{1,0:T(8,128)(2,1)S(1)}, u32[]{:S(2)}, u32[]{:S(2)}) collective-permute-start(bf16[128,128]{1,0:T(8,128)(2,1)S(1)} %get-tuple-element.54), channel_id=1, source_target_pairs={{0,3},{1,4},{2,5},{3,6},{4,7},{5,0},{6,1},{7,2},{8,11},{9,12},{10,... | collective-permute-start | bytes 98312 | tf_op jit(solution)/shard_map/ppermute | solution.py:481
  61.3 1.3 %collective-permute-start.15 = (bf16[64,128]{1,0:T(8,128)(2,1)S(1)}, bf16[64,128]{1,0:T(8,128)(2,1)S(1)}, u32[]{:S(2)}, u32[]{:S(2)}) collective-permute-start(bf16[64,128]{1,0:T(8,128)(2,1)S(1)} %slice.117), channel_id=1, source_target_pairs={{0,4},{1,5},{2,6},{3,7},{4,0},{5,1},{6,2},{7,3},{8,12},{9,13},{10,... | collective-permute-start | bytes 49160 | tf_op jit(solution)/shard_map/ppermute | solution.py:481
  62.6 2.5 %collective-permute-done.15.e_ref = bf16[64,128]{1,0:T(8,128)(2,1)S(1)} collective-permute-done((bf16[64,128]{1,0:T(8,128)(2,1)S(1)}, bf16[64,128]{1,0:T(8,128)(2,1)S(1)}, u32[]{:S(2)}, u32[]{:S(2)}) %collective-permute-start.15) | collective-permute-done | bytes 16416 | tf_op jit(solution)/shard_map/ppermute | solution.py:481
  65.1 0.0 collective-permute-done.12.r1_ref
  65.1 0.0 collective-permute-done.13.r2_ref
  65.1 0.0 collective-permute-done.14.r3_ref
  65.1 0.9 %finish.1 = (f32[128,1024]{1,0:T(8,128)}, f32[1,128]{1,0:T(1,128)}) custom-call(f32[592,128]{1,0:T(8,128)S(1)} %get-tuple-element.53.own_ref, bf16[128,128]{1,0:T(8,128)(2,1)S(1)} %collective-permute-done.12.r1_ref, bf16[128,128]{1,0:T(8,128)(2,1)S(1)} %collective-permute-done.13.r2_ref, bf16[128,128]{1,0:T(8,128)(2,1)S(1)} %collective-permute-done.14.r3_ref, ...), custom_call_target="tpu_custom_call" | custom-call | tf_op jit(solution)/shard_map/finish/pallas_call | solution.py:361
  (11 shorter events, 0.2 us)
Async XLA Ops:
  3.2 1.4 %copy-start = (bf16[192,32,128]{2,1,0:T(8,128)(2,1)S(1)}, bf16[192,32,128]{2,1,0:T(8,128)(2,1)}, u32[]{:S(2)}) copy-start(bf16[192,32,128]{2,1,0:T(8,128)(2,1)} %g_ref.5) | copy-start | bytes 4718596
  4.6 9.4 %copy-start.1 = (bf16[192,32,128]{2,1,0:T(8,128)(2,1)S(1)}, bf16[192,32,128]{2,1,0:T(8,128)(2,1)}, u32[]{:S(2)}) copy-start(bf16[192,32,128]{2,1,0:T(8,128)(2,1)} %g_ref.5) | copy-start | bytes 4718596
  13.4 3.8 %collective-permute-start = (bf16[4,2,592,128]{3,2,1,0:T(8,128)(2,1)S(1)}, bf16[4,2,592,128]{3,2,1,0:T(8,128)(2,1)S(1)}, u32[]{:S(2)}, u32[]{:S(2)}) collective-permute-start(bf16[4,2,592,128]{3,2,1,0:T(8,128)(2,1)S(1)} %get-tuple-element.34), channel_id=1, source_target_pairs={{0,1},{1,0},{2,3},{3,2},{4,5},{5,4},{6,7},{7,6},{8,9},{9,8},{10,11... | collective-permute-start | bytes 3637256 | tf_op jit(solution)/shard_map/ppermute | solution.py:394
  17.1 7.4 %collective-permute-start.1 = (bf16[4,1,592,128]{3,2,1,0:T(8,128)(2,1)S(1)}, bf16[4,1,592,128]{3,2,1,0:T(8,128)(2,1)S(1)}, u32[]{:S(2)}, u32[]{:S(2)}) collective-permute-start(bf16[4,1,592,128]{3,2,1,0:T(8,128)(2,1)S(1)} %get-tuple-element.31), channel_id=1, source_target_pairs={{0,1},{1,0},{2,3},{3,2},{4,5},{5,4},{6,7},{7,6},{8,9},{9,8},{10,11... | collective-permute-start | bytes 1818632 | tf_op jit(solution)/shard_map/ppermute | solution.py:394
  17.3 11.6 %collective-permute-start.4 = (bf16[2,2,592,128]{3,2,1,0:T(8,128)(2,1)S(1)}, bf16[2,2,592,128]{3,2,1,0:T(8,128)(2,1)S(1)}, u32[]{:S(2)}, u32[]{:S(2)}) collective-permute-start(bf16[2,2,592,128]{3,2,1,0:T(8,128)(2,1)S(1)} %add_convert_fusion), channel_id=1, source_target_pairs={{0,2},{1,5},{2,0},{3,7},{4,6},{5,1},{6,4},{7,3},{8,10},{9,13},{10,... | collective-permute-start | bytes 1818632 | tf_op jit(solution)/shard_map/ppermute | solution.py:394
  24.5 6.2 %collective-permute-start.2 = (bf16[4,1,592,128]{3,2,1,0:T(8,128)(2,1)S(1)}, bf16[4,1,592,128]{3,2,1,0:T(8,128)(2,1)S(1)}, u32[]{:S(2)}, u32[]{:S(2)}) collective-permute-start(bf16[4,1,592,128]{3,2,1,0:T(8,128)(2,1)S(1)} %get-tuple-element.42), channel_id=1, source_target_pairs={{0,1},{1,0},{2,3},{3,2},{4,5},{5,4},{6,7},{7,6},{8,9},{9,8},{10,11... | collective-permute-start | bytes 1818632 | tf_op jit(solution)/shard_map/ppermute | solution.py:394
  29.1 10.0 %collective-permute-start.5 = (bf16[2,592,128]{2,1,0:T(8,128)(2,1)S(1)}, bf16[2,592,128]{2,1,0:T(8,128)(2,1)S(1)}, u32[]{:S(2)}, u32[]{:S(2)}) collective-permute-start(bf16[2,592,128]{2,1,0:T(8,128)(2,1)S(1)} %fusion.1), channel_id=1, source_target_pairs={{0,4},{1,3},{2,6},{3,1},{4,0},{5,7},{6,2},{7,5},{8,12},{9,11},{10,... | collective-permute-start | bytes 909320 | tf_op jit(solution)/shard_map/ppermute | solution.py:394
  30.7 11.1 %collective-permute-start.7 = (bf16[2,1,592,128]{3,2,1,0:T(8,128)(2,1)S(1)}, bf16[2,1,592,128]{3,2,1,0:T(8,128)(2,1)S(1)}, u32[]{:S(2)}, u32[]{:S(2)}) collective-permute-start(bf16[2,1,592,128]{3,2,1,0:T(8,128)(2,1)S(1)} %add_convert_fusion.1), channel_id=1, source_target_pairs={{0,2},{1,5},{2,0},{3,7},{4,6},{5,1},{6,4},{7,3},{8,10},{9,13},{10,... | collective-permute-start | bytes 909320 | tf_op jit(solution)/shard_map/ppermute | solution.py:394
  32.5 16.8 %collective-permute-start.3 = (bf16[2,1,592,128]{3,2,1,0:T(8,128)(2,1)S(1)}, bf16[2,1,592,128]{3,2,1,0:T(8,128)(2,1)S(1)}, u32[]{:S(2)}, u32[]{:S(2)}) collective-permute-start(bf16[2,1,592,128]{3,2,1,0:T(8,128)(2,1)S(1)} %add_convert_fusion.2), channel_id=1, source_target_pairs={{0,2},{1,5},{2,0},{3,7},{4,6},{5,1},{6,4},{7,3},{8,10},{9,13},{10,... | collective-permute-start | bytes 909320 | tf_op jit(solution)/shard_map/ppermute | solution.py:394
  39.3 6.5 %collective-permute-start.6 = (bf16[592,128]{1,0:T(8,128)(2,1)S(1)}, bf16[592,128]{1,0:T(8,128)(2,1)S(1)}, u32[]{:S(2)}, u32[]{:S(2)}) collective-permute-start(bf16[592,128]{1,0:T(8,128)(2,1)S(1)} %fusion.10), channel_id=1, source_target_pairs={{0,8},{8,0},{16,24},{24,16},{1,9},{9,1},{17,25},{25,17},{2,10},{10... | collective-permute-start | bytes 454664 | tf_op jit(solution)/shard_map/ppermute | solution.py:397
  41.9 9.9 %collective-permute-start.10 = (bf16[1,592,128]{2,1,0:T(8,128)(2,1)S(1)}, bf16[1,592,128]{2,1,0:T(8,128)(2,1)S(1)}, u32[]{:S(2)}, u32[]{:S(2)}) collective-permute-start(bf16[1,592,128]{2,1,0:T(8,128)(2,1)S(1)} %fusion.11), channel_id=1, source_target_pairs={{0,4},{1,3},{2,6},{3,1},{4,0},{5,7},{6,2},{7,5},{8,12},{9,11},{10,... | collective-permute-start | bytes 454664 | tf_op jit(solution)/shard_map/ppermute | solution.py:394
  45.8 9.2 %collective-permute-start.9 = (bf16[592,128]{1,0:T(8,128)(2,1)S(1)}, bf16[592,128]{1,0:T(8,128)(2,1)S(1)}, u32[]{:S(2)}, u32[]{:S(2)}) collective-permute-start(bf16[592,128]{1,0:T(8,128)(2,1)S(1)} %fusion.9), channel_id=1, source_target_pairs={{0,16},{8,24},{16,0},{24,8},{1,17},{9,25},{17,1},{25,9},{2,18},{10... | collective-permute-start | bytes 454664 | tf_op jit(solution)/shard_map/ppermute | solution.py:397
  49.4 5.6 %collective-permute-start.8 = (bf16[1,592,128]{2,1,0:T(8,128)(2,1)S(1)}, bf16[1,592,128]{2,1,0:T(8,128)(2,1)S(1)}, u32[]{:S(2)}, u32[]{:S(2)}) collective-permute-start(bf16[1,592,128]{2,1,0:T(8,128)(2,1)S(1)} %fusion.12), channel_id=1, source_target_pairs={{0,4},{1,3},{2,6},{3,1},{4,0},{5,7},{6,2},{7,5},{8,12},{9,11},{10,... | collective-permute-start | bytes 454664 | tf_op jit(solution)/shard_map/ppermute | solution.py:394
  51.9 5.3 %collective-permute-start.11 = (bf16[592,128]{1,0:T(8,128)(2,1)S(1)}, bf16[592,128]{1,0:T(8,128)(2,1)S(1)}, u32[]{:S(2)}, u32[]{:S(2)}) collective-permute-start(bf16[592,128]{1,0:T(8,128)(2,1)S(1)} %fusion.13), channel_id=1, source_target_pairs={{0,8},{8,0},{16,24},{24,16},{1,9},{9,1},{17,25},{25,17},{2,10},{10... | collective-permute-start | bytes 454664 | tf_op jit(solution)/shard_map/ppermute | solution.py:397
  57.2 7.8 %collective-permute-start.12 = (bf16[128,128]{1,0:T(8,128)(2,1)S(1)}, bf16[128,128]{1,0:T(8,128)(2,1)S(1)}, u32[]{:S(2)}, u32[]{:S(2)}) collective-permute-start(bf16[128,128]{1,0:T(8,128)(2,1)S(1)} %get-tuple-element.56), channel_id=1, source_target_pairs={{0,1},{1,2},{2,3},{3,4},{4,5},{5,6},{6,7},{7,0},{8,9},{9,10},{10,1... | collective-permute-start | bytes 98312 | tf_op jit(solution)/shard_map/ppermute | solution.py:481
  57.3 7.8 %collective-permute-start.13 = (bf16[128,128]{1,0:T(8,128)(2,1)S(1)}, bf16[128,128]{1,0:T(8,128)(2,1)S(1)}, u32[]{:S(2)}, u32[]{:S(2)}) collective-permute-start(bf16[128,128]{1,0:T(8,128)(2,1)S(1)} %get-tuple-element.55), channel_id=1, source_target_pairs={{0,2},{1,3},{2,4},{3,5},{4,6},{5,7},{6,0},{7,1},{8,10},{9,11},{10,... | collective-permute-start | bytes 98312 | tf_op jit(solution)/shard_map/ppermute | solution.py:481
  59.7 5.3 %collective-permute-start.14 = (bf16[128,128]{1,0:T(8,128)(2,1)S(1)}, bf16[128,128]{1,0:T(8,128)(2,1)S(1)}, u32[]{:S(2)}, u32[]{:S(2)}) collective-permute-start(bf16[128,128]{1,0:T(8,128)(2,1)S(1)} %get-tuple-element.54), channel_id=1, source_target_pairs={{0,3},{1,4},{2,5},{3,6},{4,7},{5,0},{6,1},{7,2},{8,11},{9,12},{10,... | collective-permute-start | bytes 98312 | tf_op jit(solution)/shard_map/ppermute | solution.py:481
  61.3 3.7 %collective-permute-start.15 = (bf16[64,128]{1,0:T(8,128)(2,1)S(1)}, bf16[64,128]{1,0:T(8,128)(2,1)S(1)}, u32[]{:S(2)}, u32[]{:S(2)}) collective-permute-start(bf16[64,128]{1,0:T(8,128)(2,1)S(1)} %slice.117), channel_id=1, source_target_pairs={{0,4},{1,5},{2,6},{3,7},{4,0},{5,1},{6,2},{7,3},{8,12},{9,13},{10,... | collective-permute-start | bytes 49160 | tf_op jit(solution)/shard_map/ppermute | solution.py:481
where the time goes:
time: 65.8 us; the launch traced here: 66 us
  starting transfers between devices  24.3 us (37%)
  waiting for transfers between devices  19.5 us (30%)
  Pallas kernels  16.5 us (25%)
  other arithmetic  2.76 us (4%)
  local copies, waits for them, and re-layouts  2.25 us (3%)
  between operations  0.77 us (1%)
    pallas_call x3, Pallas kernels, assemble(): pl.pallas_call(functools.partial(lead_kernel if lead else follow_kernel,...  15.6 us
    ppermute x9, waiting for transfers between devices, swap(): return lax.ppermute(value, 'tile', pairs)  13.3 us
    ppermute x9, starting transfers between devices, swap(): return lax.ppermute(value, 'tile', pairs)  12.5 us
    ppermute x3, starting transfers between devices, across(): lax.ppermute(value.astype(BF16), 'region', [(r, r ^ k) for r in range(reg...  6.35 us
    ppermute x4, starting transfers between devices, onward(): return lax.ppermute(value.astype(BF16), 'tile', pairs)  5.37 us
    ppermute x3, waiting for transfers between devices, across(): lax.ppermute(value.astype(BF16), 'region', [(r, r ^ k) for r in range(reg...  3.68 us
    ppermute x4, waiting for transfers between devices, onward(): return lax.ppermute(value.astype(BF16), 'tile', pairs)  2.47 us
    concatenate x2, other arithmetic, local(): inputs = (jnp.concatenate(floats, axis=0), jnp.concatenate(numbers, axis=0))  1.81 us
  transfers between devices with their start and end apart: 16, of which 6 were waited for; matrix products, arithmetic and copies ran while one was open for 1% of the time, Pallas kernels for 10%

commit v1 on v0

--- a/solution.py
+++ b/solution.py
@@ -58,14 +58,18 @@
     return solved, masked_w * resid - projection, masked_w
 
 
-def prepare(blocks, floats_ref, numbers_ref, scaled_ref, lanes_ref, column_ref, table_ref):
-    tracks = floats_ref.shape[1]
-    groups, _, depth = scaled_ref.shape
-    slots = groups * GROUP
+def prepare(
+    place_ref, region_ref, count_ref, ld_ref, weight_ref, resid_ref, ids_ref, shared_ref, table_ref
+):
+    tracks = region_ref.shape[1]
+    slots = table_ref.shape[1]
+    groups = slots // GROUP
+    depth = shared_ref.shape[1]
     hits = depth // GROUP
-    count_row, region_row = (numbers_ref[hits + n : hits + n + 1, :] for n in range(2))
+    lanes_at, column_at = groups * 5 * GROUP, groups * (5 * GROUP + 2)
+    blocks = place_ref.shape[0]
     rr = table_ref.shape[0] - 8
-    member = (iota((rr, tracks), 0) == region_row).astype(F32)
+    member = (iota((rr, tracks), 0) == region_ref[...]).astype(F32)
     before = (iota((tracks, tracks), 0) < iota((tracks, tracks), 1)).astype(F32).astype(BF16)
     rank = jnp.dot(member.astype(BF16), before, preferred_element_type=F32)
     count = jnp.sum(member, axis=1, keepdims=True)
@@ -78,7 +82,7 @@
     slot = jnp.sum(member * (rank + start[:, 0:1]), axis=0, keepdims=True)
     perm = (iota((slots, tracks), 0) == slot.astype(jnp.int32)).astype(F32).astype(BF16)
     numbers = jnp.where(
-        iota((8, tracks), 0) == 0, iota((8, tracks), 1), jnp.broadcast_to(count_row, (8, tracks))
+        iota((8, tracks), 0) == 0, iota((8, tracks), 1), jnp.broadcast_to(count_ref[...], (8, tracks))
     )
 
     def sort(value):
@@ -89,14 +93,15 @@
     table_ref[8:, :] = jnp.where(
         iota((rr, slots), 1) == 0, start.astype(jnp.int32), (start + room).astype(jnp.int32)
     )
-    flat = sort(floats_ref[...])
-    flat = [flat[c * hits : (c + 1) * hits] for c in range(7)]
-    solved, hit_factor, masked_w = fit(flat[:5], flat[5], flat[6], numbers[1:2])
-    ids = sort(numbers_ref[:hits, :].astype(F32).astype(BF16))
-    places = [numbers_ref[hits + 2 + b : hits + 3 + b, 0:1].astype(F32) for b in range(blocks)]
+    flat = sort(ld_ref[...])
+    ld = [flat[c * hits : (c + 1) * hits] for c in range(5)]
+    solved, hit_factor, masked_w = fit(
+        ld, sort(weight_ref[...]), sort(resid_ref[...]), numbers[1:2]
+    )
+    ids = sort(ids_ref[...].astype(F32).astype(BF16))
     position = jnp.zeros_like(ids)
     for b in range(blocks):
-        position = jnp.where(ids == float(b), places[b], position)
+        position = jnp.where(ids == float(b), place_ref[b].astype(F32), position)
     own = (iota((depth, slots), 0) // hits) == (iota((depth, slots), 1) % GROUP)
 
     def spread_out(value):
@@ -104,26 +109,30 @@
 
     grouping = (iota((groups, slots), 1) // GROUP == iota((groups, slots), 0)).astype(F32)
     for n, value in enumerate((masked_w, hit_factor)):
-        lanes_ref[n] = lax.dot_general(
+        shared_ref[lanes_at + n * groups : lanes_at + (n + 1) * groups, :] = lax.dot_general(
             grouping.astype(BF16), spread_out(value).astype(BF16), NT, preferred_element_type=F32
         )
-    columns = column_ref.shape[1]
+    columns = 128
     grouping = (iota((columns, slots), 1) // GROUP == iota((columns, slots), 0)).astype(F32)
-    column_ref[...] = lax.dot_general(
+    shared_ref[column_at : column_at + depth, :columns] = lax.dot_general(
         spread_out(position).astype(BF16), grouping.astype(BF16), NT, preferred_element_type=F32
     )
     for c in range(5):
-        scaled_ref[:, c * GROUP : (c + 1) * GROUP, :] = spread_out(solved[c]).T.reshape(
-            groups, GROUP, depth
-        )
-
-
-def one_step(step, at, table_ref, g_ref, scaled_ref, lanes_ref, column_ref, g_s, direct_s, spread_s):
+        value = spread_out(solved[c]).T
+        for g in range(groups):
+            at = (g * 5 + c) * GROUP
+            shared_ref[at : at + GROUP, :] = value[g * GROUP : (g + 1) * GROUP, :]
+
+
+def one_step(step, at, table_ref, shared_ref, g_ref, g_s, direct_s, spread_s):
     hits, width = g_ref.shape[1:]
     depth = GROUP * hits
     blocks = spread_s.shape[1] // width
     rows = 5 * GROUP
     head = width + 8
+    groups = table_ref.shape[1] // GROUP
+    lanes_at, column_at = groups * rows, groups * (rows + 2)
+    column = shared_ref[column_at : column_at + depth, :128]
     unit = (iota((width, width), 0) == iota((width, width), 1)).astype(F32).astype(BF16)
     lefts, values, positions = [], [], []
     for u in range(2):
@@ -131,12 +140,12 @@
         for i in range(GROUP):
             g_s[u, i * hits : (i + 1) * hits, :] = g_ref[table_ref[0, group * GROUP + i]]
         g = g_s[u]
-        chosen = jnp.full(column_ref.shape, group, jnp.int32)
-        position = jnp.take_along_axis(column_ref[...], chosen, axis=1, mode="promise_in_bounds")
+        chosen = jnp.full(column.shape, group, jnp.int32)
+        position = jnp.take_along_axis(column, chosen, axis=1, mode="promise_in_bounds")
         turned = lax.dot_general(unit, g, NT, preferred_element_type=F32)
-        weighted = turned * lanes_ref[0, pl.ds(group, 1), :]
-        factor = jnp.where(iota((8, depth), 0) == 0, lanes_ref[1, pl.ds(group, 1), :], 0.0)
-        scaled = scaled_ref[group]
+        weighted = turned * shared_ref[pl.ds(lanes_at + group, 1), :]
+        factor = jnp.where(iota((8, depth), 0) == 0, shared_ref[pl.ds(lanes_at + groups + group, 1), :], 0.0)
+        scaled = shared_ref[pl.ds(pl.multiple_of(group * rows, GROUP), rows), :]
         high = scaled.astype(BF16).astype(F32)
         left = jnp.concatenate(
             [weighted, factor, high, scaled - high, jnp.zeros((8, depth), F32)], axis=0
@@ -167,28 +176,35 @@
 ODD = (0, 2, 4, 6)
 
 
-def lead_kernel(
-    ks, sub, blocks, floats_ref, numbers_ref, g_ref,
-    keep_ref, send_ref, scaled_ref, lanes_ref, column_ref, table_ref, table_s, sem, *scratch,
-):
-    prepare(blocks, floats_ref, numbers_ref, scaled_ref, lanes_ref, column_ref, table_ref)
-    copy = pltpu.make_async_copy(table_ref, table_s, sem)
+def lead_kernel(ks, sub, *refs):
+    small, g_hbm, (keep_ref, send_ref, shared_ref, table_ref) = refs[:7], refs[7], refs[8:12]
+    local_small, g_ref, table_s, sems, scratch = refs[12:19], refs[19], refs[20], refs[21], refs[22:]
+    copies = [
+        pltpu.make_async_copy(source, target, sems.at[n])
+        for n, (source, target) in enumerate([*zip(small, local_small), (g_hbm, g_ref)])
+    ]
+    for copy in copies:
+        copy.start()
+    for copy in copies[:-1]:
+        copy.wait()
+    prepare(*local_small, shared_ref, table_ref)
+    copy = pltpu.make_async_copy(table_ref, table_s, sems.at[0])
     copy.start()
     copy.wait()
+    copies[-1].wait()
 
     def region(n, carry):
         assemble_region(
-            n, ks, sub, table_s, scaled_ref, lanes_ref, column_ref, g_ref, keep_ref, send_ref,
-            *scratch,
+            n, ks, sub, table_s, shared_ref, g_ref, keep_ref, send_ref, *scratch
         )
         return carry
 
     lax.fori_loop(0, len(ks), region, 0)
 
 
-def follow_kernel(ks, sub, blocks, scaled_ref, lanes_ref, column_ref, table_ref, g_ref, *refs):
+def follow_kernel(ks, sub, shared_ref, table_ref, g_ref, *refs):
     def region(n, carry):
-        assemble_region(n, ks, sub, table_ref, scaled_ref, lanes_ref, column_ref, g_ref, *refs)
+        assemble_region(n, ks, sub, table_ref, shared_ref, g_ref, *refs)
         return carry
 
     if len(ks) == 1:
@@ -198,7 +214,7 @@
 
 
 def assemble_region(
-    number, ks, sub, table_ref, scaled_ref, lanes_ref, column_ref, g_ref,
+    number, ks, sub, table_ref, shared_ref, g_ref,
     keep_ref, send_ref, g_s, direct_s, spread_s, wide_s, turned_s, acc_s,
 ):
     k = jnp.where(number == 0, ks[0], ks[-1])
@@ -213,8 +229,7 @@
 
     def group_step(n, carry):
         one_step(
-            first + n, n * (10 * GROUP), table_ref, g_ref, scaled_ref, lanes_ref, column_ref,
-            g_s, direct_s, spread_s,
+            first + n, n * (10 * GROUP), table_ref, shared_ref, g_ref, g_s, direct_s, spread_s
         )
         return carry
 
@@ -245,16 +260,17 @@
 
         def products(add):
             for q in range(0, blocks, 2):
-                upper = (q + blocks - many) % blocks
+                reach = many if q >= many else many - 1
+                upper = (q + blocks - reach) % blocks
                 value = jnp.dot(
-                    turned_s[upper * width : (upper + many + 2) * width],
+                    turned_s[upper * width : (upper + reach + 2) * width],
                     wide_s[:, q * width : (q + 2) * width],
                     preferred_element_type=F32,
                 )
-                for r in range(many + 2):
+                for r in range(reach + 2):
                     p = (upper + r) % blocks
                     for c in range(2):
-                        d = many - r + c
+                        d = reach - r + c
                         if 0 <= d <= many and (d < many or p < many):
                             part = value[r * width : (r + 1) * width, c * width : (c + 1) * width]
                             columns = slice(d * width, (d + 1) * width)
@@ -289,27 +305,31 @@
 
 def assemble(ks, sub, inputs, g, blocks, regions):
     tracks, hits, width = g.shape
-    lead = len(inputs) == 2
+    lead = len(inputs) == 7
     rows = width * (blocks // 2) + width // 2 + 16
     longest = -(-(-(-tracks // PAIR) * 5 * PAIR) // DEPTH) * DEPTH
     rr = -(-regions // 8) * 8
     slots = -(-(tracks + regions * (PAIR - 1)) // 128) * 128
     shared = [
-        jax.ShapeDtypeStruct((slots // GROUP, 5 * GROUP, GROUP * hits), F32),
-        jax.ShapeDtypeStruct((2, slots // GROUP, GROUP * hits), F32),
-        jax.ShapeDtypeStruct((GROUP * hits, 128), F32),
+        jax.ShapeDtypeStruct((slots // GROUP * (5 * GROUP + 2) + GROUP * hits, GROUP * hits), F32),
         jax.ShapeDtypeStruct((8 + rr, slots), jnp.int32),
     ]
     out = jax.ShapeDtypeStruct((blocks // 2, len(ks), rows, width), BF16)
     vmem = pl.BlockSpec(memory_space=pltpu.VMEM)
     smem = pl.BlockSpec(memory_space=pltpu.SMEM)
-    local_table = [pltpu.SMEM(shared[3].shape, jnp.int32), pltpu.SemaphoreType.DMA]
+    copies = [pltpu.SMEM(inputs[0].shape, jnp.int32)]
+    copies += [pltpu.VMEM(value.shape, value.dtype) for value in inputs[1:]]
+    copies += [
+        pltpu.VMEM(g.shape, g.dtype),
+        pltpu.SMEM(shared[1].shape, jnp.int32),
+        pltpu.SemaphoreType.DMA((8,)),
+    ]
     return pl.pallas_call(
-        functools.partial(lead_kernel if lead else follow_kernel, ks, sub, blocks),
-        in_specs=[vmem] * 3 if lead else [vmem, vmem, vmem, smem, vmem],
-        out_specs=[vmem] * (6 if lead else 2),
+        functools.partial(lead_kernel if lead else follow_kernel, ks, sub),
+        in_specs=[pl.BlockSpec(memory_space=pltpu.HBM)] * 8 if lead else [vmem, smem, vmem],
+        out_specs=[vmem] * (4 if lead else 2),
         out_shape=[out, out] + shared * lead,
-        scratch_shapes=local_table * lead
+        scratch_shapes=copies * lead
         + [
             pltpu.VMEM((2, GROUP * hits, width), BF16),
             pltpu.VMEM((width + 8, blocks * width), F32),
@@ -318,7 +338,7 @@
             pltpu.VMEM(((blocks + blocks // 2) * width, DEPTH), BF16),
             pltpu.VMEM((blocks, width, (blocks // 2 + 1) * width), F32),
         ],
-        compiler_params=pltpu.CompilerParams(vmem_limit_bytes=28 * 1024 * 1024),
+        compiler_params=pltpu.CompilerParams(vmem_limit_bytes=(60 if lead else 28) * 1024 * 1024),
         cost_estimate=pl.CostEstimate(
             flops=10**9 * len(ks), bytes_accessed=4 * 10**6, transcendentals=0
         ),
@@ -380,14 +400,15 @@
     blocks = block_place.shape[0]
     sub = tiles // blocks
     tile = lax.axis_index("tile")
-    floats = [local_deriv.transpose(1, 2, 0).reshape(-1, tracks), hit_weight.T, hit_resid.T]
-    numbers = [
+    inputs = (
+        block_place,
+        track_region.reshape(1, tracks),
+        hit_count.reshape(1, tracks),
+        local_deriv.transpose(1, 2, 0).reshape(-1, tracks),
+        hit_weight.T,
+        hit_resid.T,
         block_ids.T,
-        hit_count.reshape(1, tracks),
-        track_region.reshape(1, tracks),
-        jnp.broadcast_to(block_place[:, None], (blocks, tracks)),
-    ]
-    inputs = (jnp.concatenate(floats, axis=0), jnp.concatenate(numbers, axis=0))
+    )
 
     def swap(value, even, odd):
         pairs = [(t, t ^ (sub * (odd if t // sub % 2 else even))) for t in range(tiles)]
@@ -430,22 +451,22 @@
     for n, ks in enumerate(groups):
         keep, send, *made = assemble(ks, sub, inputs, global_deriv, blocks, regions)
         if n == 0:
-            inputs = tuple(made)
             cores.append(near(keep, send))
+            operand = both(cores[0], top).astype(BF16)
+            inputs = made[0], after(made[1], operand)
+            firsts.append(swap(operand, 2, 4))
             continue
-        table = after(inputs[3], send)
-        cores[n - 1] = after(cores[n - 1], send)
         if n > 1:
+            cores[n - 1] = after(cores[n - 1], send)
             firsts[n - 2] = after(firsts[n - 2], send)
             send = after(send, cores[n - 1][1])
             seconds.append(lower(cores[n - 2], firsts[n - 2]))
             settle(n - 2)
-        if n < last:
-            operand = both(cores[n - 1], top).astype(BF16)
-            table = after(table, operand)
-            firsts.append(swap(operand, 2, 4))
-        inputs = inputs[:3] + (table,)
+        if 1 < n < last:
+            firsts.append(swap(both(cores[n - 1], top).astype(BF16), 2, 4))
+        inputs = inputs[0], after(inputs[1], send)
         cores.append(near(keep, send))
+    cores[last] = after(cores[last], seconds[-1][1])
     operand = after(both(cores[last - 1], top).astype(BF16), cores[last][1])
     firsts.append(swap(operand, 2, 4))
     operand = both(cores[last], top).astype(BF16)

time: 65.8 us -> 64.4 us (0.979); the launches traced: 66 us -> 63.8 us
  starting transfers between devices: 24.3 us -> 18.1 us
  Pallas kernels: 16.5 us -> 20.5 us
  waiting for transfers between devices: 19.5 us -> 20.9 us
  other arithmetic: 2.76 us -> 2.03 us
  local copies, waits for them, and re-layouts: 2.25 us -> 1.55 us
    pallas_call x3, Pallas kernels: 15.6 us -> 19.5 us  [assemble(): pl.pallas_call(functools.partial(lead_kernel if lead else follow_kernel,...]
    ppermute x4, starting transfers between devices: 5.37 us -> 2.19 us  [onward(): return lax.ppermute(value.astype(BF16), 'tile', pairs)]
    ppermute x3, starting transfers between devices: 6.35 us -> 3.31 us  [across(): lax.ppermute(value.astype(BF16), 'region', [(r, r ^ k) for r in range(reg...]
    ppermute x9, waiting for transfers between devices: 13.3 us -> 15.3 us  [swap(): return lax.ppermute(value, 'tile', pairs)]
    concatenate x2 -> x0, other arithmetic: 1.81 us -> none  [local(): inputs = (jnp.concatenate(floats, axis=0), jnp.concatenate(numbers, axis=0))]
    ppermute x3, waiting for transfers between devices: 3.68 us -> 2.14 us  [across(): lax.ppermute(value.astype(BF16), 'region', [(r, r ^ k) for r in range(reg...]
    convert_element_type x1, other arithmetic: 0.16 us -> 1.23 us  [local(): operand = both(cores[0], top).astype(BF16)]
    ppermute x4, waiting for transfers between devices: 2.47 us -> 3.46 us  [onward(): return lax.ppermute(value.astype(BF16), 'tile', pairs)]
  transfers between devices with their start and end apart: 16 -> 16, of which waited for: 6 -> 7; matrix products, arithmetic and copies ran while one was open for 1% -> 1% of each run, Pallas kernels for 10% -> 15%
where the time goes in v1:
time: 64.4 us; the launch traced here: 63.8 us
  waiting for transfers between devices  20.9 us (32%)
  Pallas kernels  20.5 us (32%)
  starting transfers between devices  18.1 us (28%)
  other arithmetic  2.03 us (3%)
  local copies, waits for them, and re-layouts  1.55 us (2%)
  between operations  0.8 us (1%)
    pallas_call x3, Pallas kernels, assemble(): pl.pallas_call(functools.partial(lead_kernel if lead else follow_kernel,...  19.5 us
    ppermute x9, waiting for transfers between devices, swap(): return lax.ppermute(value, 'tile', pairs)  15.3 us
    ppermute x9, starting transfers between devices, swap(): return lax.ppermute(value, 'tile', pairs)  12.6 us
    ppermute x4, waiting for transfers between devices, onward(): return lax.ppermute(value.astype(BF16), 'tile', pairs)  3.46 us
    ppermute x3, starting transfers between devices, across(): lax.ppermute(value.astype(BF16), 'region', [(r, r ^ k) for r in range(reg...  3.31 us
    ppermute x4, starting transfers between devices, onward(): return lax.ppermute(value.astype(BF16), 'tile', pairs)  2.19 us
    ppermute x3, waiting for transfers between devices, across(): lax.ppermute(value.astype(BF16), 'region', [(r, r ^ k) for r in range(reg...  2.14 us
    unnamed x8, local copies, waits for them, and re-layouts  1.45 us
  transfers between devices with their start and end apart: 16, of which 7 were waited for; matrix products, arithmetic and copies ran while one was open for 1% of the time, Pallas kernels for 15%

profile of v1, /device:TPU:0, one launch (start us, length us, event | category | flops | bytes accessed | tf_op | source)
XLA Modules:
  0.0 63.8 jit_solution(1929544560401187972)
XLA Ops:
  0.6 10.3 %assemble.3 = (bf16[4,2,592,128]{3,2,1,0:T(8,128)(2,1)}, bf16[4,2,592,128]{3,2,1,0:T(8,128)(2,1)}, f32[1600,256]{1,0:T(8,128)}, s32[16,256]{1,0:T(8,128)}) custom-call(s32[8]{0:T(128)} %refs_0_.1, s32[1,192]{1,0:T(1,128)} %bitcast.60, s32[1,192]{1,0:T(1,128)} %bitcast.61, bf16[160,192]{1,0:T(8,128)(2,1)} %bitcast.56, bf16[32,192]{1,0:T(8,128)(2,1)} %bitcast.58, ...), custom_call_target="tpu_custom_call" | custom-call | flops 2000000000 | bytes 4000000 | tf_op jit(solution)/shard_map/assemble/pallas_call | solution.py:327
  10.9 0.0 copy-start
  10.9 0.0 copy-start.2
  10.9 0.1 collective-permute-start
  11.0 3.1 %collective-permute-done = bf16[4,2,592,128]{3,2,1,0:T(8,128)(2,1)S(1)} collective-permute-done((bf16[4,2,592,128]{3,2,1,0:T(8,128)(2,1)}, bf16[4,2,592,128]{3,2,1,0:T(8,128)(2,1)S(1)}, u32[]{:S(2)}, u32[]{:S(2)}) %collective-permute-start) | collective-permute-done | bytes 1212448 | tf_op jit(solution)/shard_map/ppermute | solution.py:415
  14.1 1.2 %add_convert_fusion = bf16[2,2,592,128]{3,2,1,0:T(8,128)(2,1)S(1)} fusion(bf16[4,2,592,128]{3,2,1,0:T(8,128)(2,1)S(1)} %collective-permute-done, bf16[4,2,592,128]{3,2,1,0:T(8,128)(2,1)} %get-tuple-element.27), kind=kLoop, calls=%fused_computation.1 | loop fusion | flops 1212416 | bytes 1818624 | tf_op jit(solution)/shard_map/convert_element_type | solution.py:455
  15.3 3.0 %collective-permute-start.3 = (bf16[2,2,592,128]{3,2,1,0:T(8,128)(2,1)S(1)}, bf16[2,2,592,128]{3,2,1,0:T(8,128)(2,1)S(1)}, u32[]{:S(2)}, u32[]{:S(2)}) collective-permute-start(bf16[2,2,592,128]{3,2,1,0:T(8,128)(2,1)S(1)} %add_convert_fusion), channel_id=1, source_target_pairs={{0,2},{1,5},{2,0},{3,7},{4,6},{5,1},{6,4},{7,3},{8,10},{9,13},{10,... | collective-permute-start | bytes 1818632 | tf_op jit(solution)/shard_map/ppermute | solution.py:415
  18.3 0.0 copy-done
  18.3 1.4 %copy-done.1 = f32[1600,256]{1,0:T(8,128)S(1)} copy-done((f32[1600,256]{1,0:T(8,128)S(1)}, f32[1600,256]{1,0:T(8,128)}, u32[]{:S(2)}) %copy-start.1) | copy-done | bytes 1638424
  19.8 6.2 %assemble.4 = (bf16[4,1,592,128]{3,2,1,0:T(8,128)(2,1)S(1)}, bf16[4,1,592,128]{3,2,1,0:T(8,128)(2,1)S(1)}) custom-call(f32[1600,256]{1,0:T(8,128)S(1)} %copy-done.1, s32[16,256]{1,0:T(8,128)S(1)} %copy-done.2, bf16[192,32,128]{2,1,0:T(8,128)(2,1)S(1)} %copy-done), custom_call_target="tpu_custom_call" | custom-call | flops 1000000000 | bytes 4000000 | tf_op jit(solution)/shard_map/assemble/pallas_call | solution.py:327
  26.0 0.1 collective-permute-start.1
  26.0 3.1 %assemble.5 = (bf16[4,1,592,128]{3,2,1,0:T(8,128)(2,1)S(1)}, bf16[4,1,592,128]{3,2,1,0:T(8,128)(2,1)S(1)}) custom-call(f32[1600,256]{1,0:T(8,128)S(1)} %copy-done.1, s32[16,256]{1,0:T(8,128)S(1)} %copy-done.2, bf16[192,32,128]{2,1,0:T(8,128)(2,1)S(1)} %copy-done), custom_call_target="tpu_custom_call" | custom-call | flops 1000000000 | bytes 4000000 | tf_op jit(solution)/shard_map/assemble/pallas_call | solution.py:327
  29.1 0.0 collective-permute-done.3
  29.1 0.0 collective-permute-done.1
  29.1 1.1 %collective-permute-start.2 = (bf16[4,1,592,128]{3,2,1,0:T(8,128)(2,1)S(1)}, bf16[4,1,592,128]{3,2,1,0:T(8,128)(2,1)S(1)}, u32[]{:S(2)}, u32[]{:S(2)}) collective-permute-start(bf16[4,1,592,128]{3,2,1,0:T(8,128)(2,1)S(1)} %get-tuple-element.36), channel_id=1, source_target_pairs={{0,1},{1,0},{2,3},{3,2},{4,5},{5,4},{6,7},{7,6},{8,9},{9,8},{10,11... | collective-permute-start | bytes 1818632 | tf_op jit(solution)/shard_map/ppermute | solution.py:415
  30.2 0.2 convert_add_fusion
  30.5 2.1 %collective-permute-start.4 = (bf16[2,592,128]{2,1,0:T(8,128)(2,1)S(1)}, bf16[2,592,128]{2,1,0:T(8,128)(2,1)S(1)}, u32[]{:S(2)}, u32[]{:S(2)}) collective-permute-start(bf16[2,592,128]{2,1,0:T(8,128)(2,1)S(1)} %fusion.1), channel_id=1, source_target_pairs={{0,4},{1,3},{2,6},{3,1},{4,0},{5,7},{6,2},{7,5},{8,12},{9,11},{10,... | collective-permute-start | bytes 909320 | tf_op jit(solution)/shard_map/ppermute | solution.py:415
  32.6 0.1 add_convert_fusion.1
  32.6 4.7 %collective-permute-done.4 = bf16[2,592,128]{2,1,0:T(8,128)(2,1)S(1)} collective-permute-done((bf16[2,592,128]{2,1,0:T(8,128)(2,1)S(1)}, bf16[2,592,128]{2,1,0:T(8,128)(2,1)S(1)}, u32[]{:S(2)}, u32[]{:S(2)}) %collective-permute-start.4) | collective-permute-done | bytes 303136 | tf_op jit(solution)/shard_map/ppermute | solution.py:415
  37.3 0.1 fusion
  37.4 0.0 collective-permute-done.2
  37.4 0.9 %collective-permute-start.7 = (bf16[2,1,592,128]{3,2,1,0:T(8,128)(2,1)S(1)}, bf16[2,1,592,128]{3,2,1,0:T(8,128)(2,1)S(1)}, u32[]{:S(2)}, u32[]{:S(2)}) collective-permute-start(bf16[2,1,592,128]{3,2,1,0:T(8,128)(2,1)S(1)} %add_convert_fusion.1), channel_id=1, source_target_pairs={{0,2},{1,5},{2,0},{3,7},{4,6},{5,1},{6,4},{7,3},{8,10},{9,13},{10,... | collective-permute-start | bytes 909320 | tf_op jit(solution)/shard_map/ppermute | solution.py:415
  38.4 1.6 %collective-permute-start.6 = (bf16[592,128]{1,0:T(8,128)(2,1)S(1)}, bf16[592,128]{1,0:T(8,128)(2,1)S(1)}, u32[]{:S(2)}, u32[]{:S(2)}) collective-permute-start(bf16[592,128]{1,0:T(8,128)(2,1)S(1)} %fusion.10), channel_id=1, source_target_pairs={{0,8},{8,0},{16,24},{24,16},{1,9},{9,1},{17,25},{25,17},{2,10},{10... | collective-permute-start | bytes 454664 | tf_op jit(solution)/shard_map/ppermute | solution.py:418
  40.0 0.1 add_convert_fusion.2
  40.1 0.7 %collective-permute-start.5 = (bf16[2,1,592,128]{3,2,1,0:T(8,128)(2,1)S(1)}, bf16[2,1,592,128]{3,2,1,0:T(8,128)(2,1)S(1)}, u32[]{:S(2)}, u32[]{:S(2)}) collective-permute-start(bf16[2,1,592,128]{3,2,1,0:T(8,128)(2,1)S(1)} %add_convert_fusion.2), channel_id=1, source_target_pairs={{0,2},{1,5},{2,0},{3,7},{4,6},{5,1},{6,4},{7,3},{8,10},{9,13},{10,... | collective-permute-start | bytes 909320 | tf_op jit(solution)/shard_map/ppermute | solution.py:415
  40.9 3.5 %collective-permute-done.7 = bf16[2,1,592,128]{3,2,1,0:T(8,128)(2,1)S(1)} collective-permute-done((bf16[2,1,592,128]{3,2,1,0:T(8,128)(2,1)S(1)}, bf16[2,1,592,128]{3,2,1,0:T(8,128)(2,1)S(1)}, u32[]{:S(2)}, u32[]{:S(2)}) %collective-permute-start.7) | collective-permute-done | bytes 303136 | tf_op jit(solution)/shard_map/ppermute | solution.py:415
  44.3 0.1 convert_add_fusion.2
  44.4 2.1 %collective-permute-start.10 = (bf16[1,592,128]{2,1,0:T(8,128)(2,1)S(1)}, bf16[1,592,128]{2,1,0:T(8,128)(2,1)S(1)}, u32[]{:S(2)}, u32[]{:S(2)}) collective-permute-start(bf16[1,592,128]{2,1,0:T(8,128)(2,1)S(1)} %fusion.11), channel_id=1, source_target_pairs={{0,4},{1,3},{2,6},{3,1},{4,0},{5,7},{6,2},{7,5},{8,12},{9,11},{10,... | collective-permute-start | bytes 454664 | tf_op jit(solution)/shard_map/ppermute | solution.py:415
  46.5 0.0 collective-permute-done.6
  46.6 0.9 %collective-permute-start.9 = (bf16[592,128]{1,0:T(8,128)(2,1)S(1)}, bf16[592,128]{1,0:T(8,128)(2,1)S(1)}, u32[]{:S(2)}, u32[]{:S(2)}) collective-permute-start(bf16[592,128]{1,0:T(8,128)(2,1)S(1)} %fusion.9), channel_id=1, source_target_pairs={{0,16},{8,24},{16,0},{24,8},{1,17},{9,25},{17,1},{25,9},{2,18},{10... | collective-permute-start | bytes 454664 | tf_op jit(solution)/shard_map/ppermute | solution.py:418
  47.5 1.7 %collective-permute-done.5 = bf16[2,1,592,128]{3,2,1,0:T(8,128)(2,1)S(1)} collective-permute-done((bf16[2,1,592,128]{3,2,1,0:T(8,128)(2,1)S(1)}, bf16[2,1,592,128]{3,2,1,0:T(8,128)(2,1)S(1)}, u32[]{:S(2)}, u32[]{:S(2)}) %collective-permute-start.5) | collective-permute-done | bytes 303136 | tf_op jit(solution)/shard_map/ppermute | solution.py:415
  49.2 0.1 convert_add_fusion.1
  49.3 2.5 %collective-permute-start.8 = (bf16[1,592,128]{2,1,0:T(8,128)(2,1)S(1)}, bf16[1,592,128]{2,1,0:T(8,128)(2,1)S(1)}, u32[]{:S(2)}, u32[]{:S(2)}) collective-permute-start(bf16[1,592,128]{2,1,0:T(8,128)(2,1)S(1)} %fusion.12), channel_id=1, source_target_pairs={{0,4},{1,3},{2,6},{3,1},{4,0},{5,7},{6,2},{7,5},{8,12},{9,11},{10,... | collective-permute-start | bytes 454664 | tf_op jit(solution)/shard_map/ppermute | solution.py:415
  51.8 0.0 collective-permute-done.10
  51.9 0.8 %collective-permute-start.11 = (bf16[592,128]{1,0:T(8,128)(2,1)S(1)}, bf16[592,128]{1,0:T(8,128)(2,1)S(1)}, u32[]{:S(2)}, u32[]{:S(2)}) collective-permute-start(bf16[592,128]{1,0:T(8,128)(2,1)S(1)} %fusion.13), channel_id=1, source_target_pairs={{0,8},{8,0},{16,24},{24,16},{1,9},{9,1},{17,25},{25,17},{2,10},{10... | collective-permute-start | bytes 454664 | tf_op jit(solution)/shard_map/ppermute | solution.py:418
  52.7 2.3 %collective-permute-done.8 = bf16[1,592,128]{2,1,0:T(8,128)(2,1)S(1)} collective-permute-done((bf16[1,592,128]{2,1,0:T(8,128)(2,1)S(1)}, bf16[1,592,128]{2,1,0:T(8,128)(2,1)S(1)}, u32[]{:S(2)}, u32[]{:S(2)}) %collective-permute-start.8) | collective-permute-done | bytes 151584 | tf_op jit(solution)/shard_map/ppermute | solution.py:415
  55.0 0.0 collective-permute-done.9
  55.0 2.1 %collective-permute-done.11 = bf16[592,128]{1,0:T(8,128)(2,1)S(1)} collective-permute-done((bf16[592,128]{1,0:T(8,128)(2,1)S(1)}, bf16[592,128]{1,0:T(8,128)(2,1)S(1)}, u32[]{:S(2)}, u32[]{:S(2)}) %collective-permute-start.11) | collective-permute-done | bytes 151584 | tf_op jit(solution)/shard_map/ppermute | solution.py:418
  57.1 0.1 fusion.14
  57.2 0.1 collective-permute-start.14
  57.3 0.6 collective-permute-start.13
  58.0 0.8 %collective-permute-start.12 = (bf16[128,128]{1,0:T(8,128)(2,1)S(1)}, bf16[128,128]{1,0:T(8,128)(2,1)S(1)}, u32[]{:S(2)}, u32[]{:S(2)}) collective-permute-start(bf16[128,128]{1,0:T(8,128)(2,1)S(1)} %get-tuple-element.52), channel_id=1, source_target_pairs={{0,1},{1,2},{2,3},{3,4},{4,5},{5,6},{6,7},{7,0},{8,9},{9,10},{10,1... | collective-permute-start | bytes 98312 | tf_op jit(solution)/shard_map/ppermute | solution.py:502
  58.7 0.7 %collective-permute-start.15 = (bf16[64,128]{1,0:T(8,128)(2,1)S(1)}, bf16[64,128]{1,0:T(8,128)(2,1)S(1)}, u32[]{:S(2)}, u32[]{:S(2)}) collective-permute-start(bf16[64,128]{1,0:T(8,128)(2,1)S(1)} %slice.117), channel_id=1, source_target_pairs={{0,4},{1,5},{2,6},{3,7},{4,0},{5,1},{6,2},{7,3},{8,12},{9,13},{10,... | collective-permute-start | bytes 49160 | tf_op jit(solution)/shard_map/ppermute | solution.py:502
  59.5 3.5 %collective-permute-done.15.e_ref = bf16[64,128]{1,0:T(8,128)(2,1)S(1)} collective-permute-done((bf16[64,128]{1,0:T(8,128)(2,1)S(1)}, bf16[64,128]{1,0:T(8,128)(2,1)S(1)}, u32[]{:S(2)}, u32[]{:S(2)}) %collective-permute-start.15) | collective-permute-done | bytes 16416 | tf_op jit(solution)/shard_map/ppermute | solution.py:502
  62.9 0.0 collective-permute-done.14.r3_ref
  62.9 0.0 collective-permute-done.13.r2_ref
  62.9 0.0 collective-permute-done.12.r1_ref
  62.9 0.9 %finish.1 = (f32[128,1024]{1,0:T(8,128)}, f32[1,128]{1,0:T(1,128)}) custom-call(f32[592,128]{1,0:T(8,128)S(1)} %get-tuple-element.49.own_ref, bf16[128,128]{1,0:T(8,128)(2,1)S(1)} %collective-permute-done.12.r1_ref, bf16[128,128]{1,0:T(8,128)(2,1)S(1)} %collective-permute-done.13.r2_ref, bf16[128,128]{1,0:T(8,128)(2,1)S(1)} %collective-permute-done.14.r3_ref, ...), custom_call_target="tpu_custom_call" | custom-call | tf_op jit(solution)/shard_map/finish/pallas_call | solution.py:381
  (12 shorter events, 0.2 us)
Async XLA Ops:
  10.9 7.4 %copy-start = (bf16[192,32,128]{2,1,0:T(8,128)(2,1)S(1)}, bf16[192,32,128]{2,1,0:T(8,128)(2,1)}, u32[]{:S(2)}) copy-start(bf16[192,32,128]{2,1,0:T(8,128)(2,1)} %g_ref.3) | copy-start | bytes 4718596
  10.9 7.4 %copy-start.2 = (s32[16,256]{1,0:T(8,128)S(1)}, s32[16,256]{1,0:T(8,128)}, u32[]{:S(2)}) copy-start(s32[16,256]{1,0:T(8,128)} %get-tuple-element.31.table_ref) | copy-start | bytes 49156
  10.9 3.2 %collective-permute-start = (bf16[4,2,592,128]{3,2,1,0:T(8,128)(2,1)}, bf16[4,2,592,128]{3,2,1,0:T(8,128)(2,1)S(1)}, u32[]{:S(2)}, u32[]{:S(2)}) collective-permute-start(bf16[4,2,592,128]{3,2,1,0:T(8,128)(2,1)} %get-tuple-element.28), channel_id=1, source_target_pairs={{0,1},{1,0},{2,3},{3,2},{4,5},{5,4},{6,7},{7,6},{8,9},{9,8},{10,11... | collective-permute-start | bytes 3637256 | tf_op jit(solution)/shard_map/ppermute | solution.py:415
  15.3 13.8 %collective-permute-start.3 = (bf16[2,2,592,128]{3,2,1,0:T(8,128)(2,1)S(1)}, bf16[2,2,592,128]{3,2,1,0:T(8,128)(2,1)S(1)}, u32[]{:S(2)}, u32[]{:S(2)}) collective-permute-start(bf16[2,2,592,128]{3,2,1,0:T(8,128)(2,1)S(1)} %add_convert_fusion), channel_id=1, source_target_pairs={{0,2},{1,5},{2,0},{3,7},{4,6},{5,1},{6,4},{7,3},{8,10},{9,13},{10,... | collective-permute-start | bytes 1818632 | tf_op jit(solution)/shard_map/ppermute | solution.py:415
  18.3 1.4 %copy-start.1 = (f32[1600,256]{1,0:T(8,128)S(1)}, f32[1600,256]{1,0:T(8,128)}, u32[]{:S(2)}) copy-start(f32[1600,256]{1,0:T(8,128)} %get-tuple-element.25.shared_ref) | copy-start | bytes 4915204
  25.9 4.3 %copy-start.3 = (bf16[4,2,592,128]{3,2,1,0:T(8,128)(2,1)S(1)}, bf16[4,2,592,128]{3,2,1,0:T(8,128)(2,1)}, u32[]{:S(2)}) copy-start(bf16[4,2,592,128]{3,2,1,0:T(8,128)(2,1)} %get-tuple-element.27) | copy-start | bytes 3637252
  26.0 3.2 %collective-permute-start.1 = (bf16[4,1,592,128]{3,2,1,0:T(8,128)(2,1)S(1)}, bf16[4,1,592,128]{3,2,1,0:T(8,128)(2,1)S(1)}, u32[]{:S(2)}, u32[]{:S(2)}) collective-permute-start(bf16[4,1,592,128]{3,2,1,0:T(8,128)(2,1)S(1)} %get-tuple-element.30), channel_id=1, source_target_pairs={{0,1},{1,0},{2,3},{3,2},{4,5},{5,4},{6,7},{7,6},{8,9},{9,8},{10,11... | collective-permute-start | bytes 1818632 | tf_op jit(solution)/shard_map/ppermute | solution.py:415
  29.1 8.3 %collective-permute-start.2 = (bf16[4,1,592,128]{3,2,1,0:T(8,128)(2,1)S(1)}, bf16[4,1,592,128]{3,2,1,0:T(8,128)(2,1)S(1)}, u32[]{:S(2)}, u32[]{:S(2)}) collective-permute-start(bf16[4,1,592,128]{3,2,1,0:T(8,128)(2,1)S(1)} %get-tuple-element.36), channel_id=1, source_target_pairs={{0,1},{1,0},{2,3},{3,2},{4,5},{5,4},{6,7},{7,6},{8,9},{9,8},{10,11... | collective-permute-start | bytes 1818632 | tf_op jit(solution)/shard_map/ppermute | solution.py:415
  30.5 6.9 %collective-permute-start.4 = (bf16[2,592,128]{2,1,0:T(8,128)(2,1)S(1)}, bf16[2,592,128]{2,1,0:T(8,128)(2,1)S(1)}, u32[]{:S(2)}, u32[]{:S(2)}) collective-permute-start(bf16[2,592,128]{2,1,0:T(8,128)(2,1)S(1)} %fusion.1), channel_id=1, source_target_pairs={{0,4},{1,3},{2,6},{3,1},{4,0},{5,7},{6,2},{7,5},{8,12},{9,11},{10,... | collective-permute-start | bytes 909320 | tf_op jit(solution)/shard_map/ppermute | solution.py:415
  37.4 6.9 %collective-permute-start.7 = (bf16[2,1,592,128]{3,2,1,0:T(8,128)(2,1)S(1)}, bf16[2,1,592,128]{3,2,1,0:T(8,128)(2,1)S(1)}, u32[]{:S(2)}, u32[]{:S(2)}) collective-permute-start(bf16[2,1,592,128]{3,2,1,0:T(8,128)(2,1)S(1)} %add_convert_fusion.1), channel_id=1, source_target_pairs={{0,2},{1,5},{2,0},{3,7},{4,6},{5,1},{6,4},{7,3},{8,10},{9,13},{10,... | collective-permute-start | bytes 909320 | tf_op jit(solution)/shard_map/ppermute | solution.py:415
  38.4 8.1 %collective-permute-start.6 = (bf16[592,128]{1,0:T(8,128)(2,1)S(1)}, bf16[592,128]{1,0:T(8,128)(2,1)S(1)}, u32[]{:S(2)}, u32[]{:S(2)}) collective-permute-start(bf16[592,128]{1,0:T(8,128)(2,1)S(1)} %fusion.10), channel_id=1, source_target_pairs={{0,8},{8,0},{16,24},{24,16},{1,9},{9,1},{17,25},{25,17},{2,10},{10... | collective-permute-start | bytes 454664 | tf_op jit(solution)/shard_map/ppermute | solution.py:418
  40.1 9.0 %collective-permute-start.5 = (bf16[2,1,592,128]{3,2,1,0:T(8,128)(2,1)S(1)}, bf16[2,1,592,128]{3,2,1,0:T(8,128)(2,1)S(1)}, u32[]{:S(2)}, u32[]{:S(2)}) collective-permute-start(bf16[2,1,592,128]{3,2,1,0:T(8,128)(2,1)S(1)} %add_convert_fusion.2), channel_id=1, source_target_pairs={{0,2},{1,5},{2,0},{3,7},{4,6},{5,1},{6,4},{7,3},{8,10},{9,13},{10,... | collective-permute-start | bytes 909320 | tf_op jit(solution)/shard_map/ppermute | solution.py:415
  44.4 7.4 %collective-permute-start.10 = (bf16[1,592,128]{2,1,0:T(8,128)(2,1)S(1)}, bf16[1,592,128]{2,1,0:T(8,128)(2,1)S(1)}, u32[]{:S(2)}, u32[]{:S(2)}) collective-permute-start(bf16[1,592,128]{2,1,0:T(8,128)(2,1)S(1)} %fusion.11), channel_id=1, source_target_pairs={{0,4},{1,3},{2,6},{3,1},{4,0},{5,7},{6,2},{7,5},{8,12},{9,11},{10,... | collective-permute-start | bytes 454664 | tf_op jit(solution)/shard_map/ppermute | solution.py:415
  46.6 8.4 %collective-permute-start.9 = (bf16[592,128]{1,0:T(8,128)(2,1)S(1)}, bf16[592,128]{1,0:T(8,128)(2,1)S(1)}, u32[]{:S(2)}, u32[]{:S(2)}) collective-permute-start(bf16[592,128]{1,0:T(8,128)(2,1)S(1)} %fusion.9), channel_id=1, source_target_pairs={{0,16},{8,24},{16,0},{24,8},{1,17},{9,25},{17,1},{25,9},{2,18},{10... | collective-permute-start | bytes 454664 | tf_op jit(solution)/shard_map/ppermute | solution.py:418
  49.3 5.7 %collective-permute-start.8 = (bf16[1,592,128]{2,1,0:T(8,128)(2,1)S(1)}, bf16[1,592,128]{2,1,0:T(8,128)(2,1)S(1)}, u32[]{:S(2)}, u32[]{:S(2)}) collective-permute-start(bf16[1,592,128]{2,1,0:T(8,128)(2,1)S(1)} %fusion.12), channel_id=1, source_target_pairs={{0,4},{1,3},{2,6},{3,1},{4,0},{5,7},{6,2},{7,5},{8,12},{9,11},{10,... | collective-permute-start | bytes 454664 | tf_op jit(solution)/shard_map/ppermute | solution.py:415
  51.9 5.3 %collective-permute-start.11 = (bf16[592,128]{1,0:T(8,128)(2,1)S(1)}, bf16[592,128]{1,0:T(8,128)(2,1)S(1)}, u32[]{:S(2)}, u32[]{:S(2)}) collective-permute-start(bf16[592,128]{1,0:T(8,128)(2,1)S(1)} %fusion.13), channel_id=1, source_target_pairs={{0,8},{8,0},{16,24},{24,16},{1,9},{9,1},{17,25},{25,17},{2,10},{10... | collective-permute-start | bytes 454664 | tf_op jit(solution)/shard_map/ppermute | solution.py:418
  57.2 5.7 %collective-permute-start.14 = (bf16[128,128]{1,0:T(8,128)(2,1)S(1)}, bf16[128,128]{1,0:T(8,128)(2,1)S(1)}, u32[]{:S(2)}, u32[]{:S(2)}) collective-permute-start(bf16[128,128]{1,0:T(8,128)(2,1)S(1)} %get-tuple-element.50), channel_id=1, source_target_pairs={{0,3},{1,4},{2,5},{3,6},{4,7},{5,0},{6,1},{7,2},{8,11},{9,12},{10,... | collective-permute-start | bytes 98312 | tf_op jit(solution)/shard_map/ppermute | solution.py:502
  57.3 5.6 %collective-permute-start.13 = (bf16[128,128]{1,0:T(8,128)(2,1)S(1)}, bf16[128,128]{1,0:T(8,128)(2,1)S(1)}, u32[]{:S(2)}, u32[]{:S(2)}) collective-permute-start(bf16[128,128]{1,0:T(8,128)(2,1)S(1)} %get-tuple-element.51), channel_id=1, source_target_pairs={{0,2},{1,3},{2,4},{3,5},{4,6},{5,7},{6,0},{7,1},{8,10},{9,11},{10,... | collective-permute-start | bytes 98312 | tf_op jit(solution)/shard_map/ppermute | solution.py:502
  58.0 5.0 %collective-permute-start.12 = (bf16[128,128]{1,0:T(8,128)(2,1)S(1)}, bf16[128,128]{1,0:T(8,128)(2,1)S(1)}, u32[]{:S(2)}, u32[]{:S(2)}) collective-permute-start(bf16[128,128]{1,0:T(8,128)(2,1)S(1)} %get-tuple-element.52), channel_id=1, source_target_pairs={{0,1},{1,2},{2,3},{3,4},{4,5},{5,6},{6,7},{7,0},{8,9},{9,10},{10,1... | collective-permute-start | bytes 98312 | tf_op jit(solution)/shard_map/ppermute | solution.py:502
  58.7 4.2 %collective-permute-start.15 = (bf16[64,128]{1,0:T(8,128)(2,1)S(1)}, bf16[64,128]{1,0:T(8,128)(2,1)S(1)}, u32[]{:S(2)}, u32[]{:S(2)}) collective-permute-start(bf16[64,128]{1,0:T(8,128)(2,1)S(1)} %slice.117), channel_id=1, source_target_pairs={{0,4},{1,5},{2,6},{3,7},{4,0},{5,1},{6,2},{7,3},{8,12},{9,13},{10,... | collective-permute-start | bytes 49160 | tf_op jit(solution)/shard_map/ppermute | solution.py:502

commit v2 on v1

--- a/solution.py
+++ b/solution.py
@@ -133,7 +133,6 @@
     groups = table_ref.shape[1] // GROUP
     lanes_at, column_at = groups * rows, groups * (rows + 2)
     column = shared_ref[column_at : column_at + depth, :128]
-    unit = (iota((width, width), 0) == iota((width, width), 1)).astype(F32).astype(BF16)
     lefts, values, positions = [], [], []
     for u in range(2):
         group = step * 2 + u
@@ -142,7 +141,7 @@
         g = g_s[u]
         chosen = jnp.full(column.shape, group, jnp.int32)
         position = jnp.take_along_axis(column, chosen, axis=1, mode="promise_in_bounds")
-        turned = lax.dot_general(unit, g, NT, preferred_element_type=F32)
+        turned = g.T.astype(F32)
         weighted = turned * shared_ref[pl.ds(lanes_at + group, 1), :]
         factor = jnp.where(iota((8, depth), 0) == 0, shared_ref[pl.ds(lanes_at + groups + group, 1), :], 0.0)
         scaled = shared_ref[pl.ds(pl.multiple_of(group * rows, GROUP), rows), :]
@@ -437,44 +436,51 @@
         return value[0], swap(value[1].astype(BF16), 4, 2)
 
     groups = [(k + 1, k) for k in range(regions - 2, 0, -2)] + [(1,), (0,)]
-    totals, cores, firsts, seconds = [None] * regions, [], [], []
-
     def after(value, other):
         return lax.optimization_barrier((value, other))[0]
+
+    last = len(groups) - 1
+    totals = [None] * regions
+    cores, firsts, seconds = ([None] * (last + 1) for _ in range(3))
 
     def settle(n):
         value = seconds[n][0] + seconds[n][1].astype(F32)
         for place, k in enumerate(groups[n]):
             totals[k] = value[place]
 
-    last = len(groups) - 1
     for n, ks in enumerate(groups):
         keep, send, *made = assemble(ks, sub, inputs, global_deriv, blocks, regions)
         if n == 0:
-            cores.append(near(keep, send))
+            cores[0] = near(keep, send)
             operand = both(cores[0], top).astype(BF16)
             inputs = made[0], after(made[1], operand)
-            firsts.append(swap(operand, 2, 4))
-            continue
-        if n > 1:
+            firsts[0] = swap(operand, 2, 4)
+        elif n < last - 1:
+            inputs = inputs[0], after(inputs[1], send)
+            cores[n] = near(keep, send)
+            firsts[n] = swap(both(cores[n], top).astype(BF16), 2, 4)
+            seconds[n] = lower(cores[n], firsts[n])
+            settle(n)
+        elif n < last:
+            firsts[0] = after(firsts[0], send)
+            value = both(cores[0], low) + firsts[0].astype(F32)
+            operand = value[1].astype(BF16)
+            inputs = inputs[0], after(inputs[1], (send, operand))
+            seconds[0] = value[0], swap(operand, 4, 2)
+            cores[n] = near(keep, send)
+        else:
             cores[n - 1] = after(cores[n - 1], send)
-            firsts[n - 2] = after(firsts[n - 2], send)
             send = after(send, cores[n - 1][1])
-            seconds.append(lower(cores[n - 2], firsts[n - 2]))
-            settle(n - 2)
-        if 1 < n < last:
-            firsts.append(swap(both(cores[n - 1], top).astype(BF16), 2, 4))
-        inputs = inputs[0], after(inputs[1], send)
-        cores.append(near(keep, send))
-    cores[last] = after(cores[last], seconds[-1][1])
-    operand = after(both(cores[last - 1], top).astype(BF16), cores[last][1])
-    firsts.append(swap(operand, 2, 4))
+            cores[n] = near(keep, send)
+            seconds[0] = seconds[0][0], after(seconds[0][1], send)
+            settle(0)
+    firsts[last - 1] = upper(cores[last - 1])
     operand = both(cores[last], top).astype(BF16)
     firsts[last - 1] = after(firsts[last - 1], operand)
     value = both(cores[last - 1], low) + firsts[last - 1].astype(F32)
     half, more = value[0], value[1].astype(BF16)
-    firsts.append(swap(operand, 2, 4))
-    seconds.append((half, after(swap(more, 4, 2), firsts[last])))
+    firsts[last] = swap(operand, 2, 4)
+    seconds[last - 1] = half, after(swap(more, 4, 2), firsts[last])
     settle(last - 1)
     crossed = []
     for k in range(regions - 1, 1, -1):
@@ -489,7 +495,7 @@
             crossed.append(value)
         else:
             totals[k - step] = totals[k - step] + value.astype(F32)
-    seconds.append(lower(cores[last], firsts[last]))
+    seconds[last] = lower(cores[last], firsts[last])
     settle(last)
     own = totals[0]
     for value in crossed + [across(totals[1], 1)]:

time: 64.4 us -> 62.9 us (0.977)
  Pallas kernels: 20.5 us -> 19.2 us
    ppermute x3, waiting for transfers between devices: 2.14 us -> 7.5 us  [across(): lax.ppermute(value.astype(BF16), 'region', [(r, r ^ k) for r in range(reg...]
    ppermute x9, waiting for transfers between devices: 15.3 us -> 10.7 us  [swap(): return lax.ppermute(value, 'tile', pairs)]
    ppermute x9, starting transfers between devices: 12.6 us -> 11.2 us  [swap(): return lax.ppermute(value, 'tile', pairs)]
    pallas_call x3, Pallas kernels: 19.5 us -> 18.3 us  [assemble(): pl.pallas_call(functools.partial(lead_kernel if lead else follow_kernel,...]
    ppermute x4, starting transfers between devices: 2.19 us -> 3.16 us  [onward(): return lax.ppermute(value.astype(BF16), 'tile', pairs)]
  transfers between devices with their start and end apart: 16 -> 16, of which waited for: 7 -> 9; matrix products, arithmetic and copies ran while one was open for 1% -> 1% of each run, Pallas kernels for 15% -> 10%
where the time goes in v2:
time: 62.9 us; the launch traced here: 62.8 us
  waiting for transfers between devices  21.1 us (34%)
  Pallas kernels  19.2 us (31%)
  starting transfers between devices  18.1 us (29%)
  other arithmetic  2.02 us (3%)
  local copies, waits for them, and re-layouts  1.55 us (2%)
  between operations  0.78 us (1%)
    pallas_call x3, Pallas kernels, assemble(): pl.pallas_call(functools.partial(lead_kernel if lead else follow_kernel,...  18.3 us
    ppermute x9, starting transfers between devices, swap(): return lax.ppermute(value, 'tile', pairs)  11.2 us
    ppermute x9, waiting for transfers between devices, swap(): return lax.ppermute(value, 'tile', pairs)  10.7 us
    ppermute x3, waiting for transfers between devices, across(): lax.ppermute(value.astype(BF16), 'region', [(r, r ^ k) for r in range(reg...  7.5 us
    ppermute x3, starting transfers between devices, across(): lax.ppermute(value.astype(BF16), 'region', [(r, r ^ k) for r in range(reg...  3.76 us
    ppermute x4, starting transfers between devices, onward(): return lax.ppermute(value.astype(BF16), 'tile', pairs)  3.16 us
    ppermute x4, waiting for transfers between devices, onward(): return lax.ppermute(value.astype(BF16), 'tile', pairs)  2.89 us
    unnamed x8, local copies, waits for them, and re-layouts  1.45 us
  transfers between devices with their start and end apart: 16, of which 9 were waited for; matrix products, arithmetic and copies ran while one was open for 1% of the time, Pallas kernels for 10%

profile of v2, /device:TPU:0, one launch (start us, length us, event | category | flops | bytes accessed | tf_op | source)
XLA Modules:
  0.0 62.8 jit_solution(9846660158973234156)
XLA Ops:
  0.6 11.9 %assemble.3 = (bf16[4,2,592,128]{3,2,1,0:T(8,128)(2,1)}, bf16[4,2,592,128]{3,2,1,0:T(8,128)(2,1)}, f32[1600,256]{1,0:T(8,128)}, s32[16,256]{1,0:T(8,128)}) custom-call(s32[8]{0:T(128)} %refs_0_.1, s32[1,192]{1,0:T(1,128)} %bitcast.60, s32[1,192]{1,0:T(1,128)} %bitcast.61, bf16[160,192]{1,0:T(8,128)(2,1)} %bitcast.56, bf16[32,192]{1,0:T(8,128)(2,1)} %bitcast.58, ...), custom_call_target="tpu_custom_call" | custom-call | flops 2000000000 | bytes 4000000 | tf_op jit(solution)/shard_map/assemble/pallas_call | solution.py:326
  12.5 0.0 copy-start
  12.5 0.0 copy-start.2
  12.5 0.1 collective-permute-start
  12.6 3.1 %collective-permute-done = bf16[4,2,592,128]{3,2,1,0:T(8,128)(2,1)S(1)} collective-permute-done((bf16[4,2,592,128]{3,2,1,0:T(8,128)(2,1)}, bf16[4,2,592,128]{3,2,1,0:T(8,128)(2,1)S(1)}, u32[]{:S(2)}, u32[]{:S(2)}) %collective-permute-start) | collective-permute-done | bytes 1212448 | tf_op jit(solution)/shard_map/ppermute | solution.py:414
  15.7 1.2 %add_convert_fusion = bf16[2,2,592,128]{3,2,1,0:T(8,128)(2,1)S(1)} fusion(bf16[4,2,592,128]{3,2,1,0:T(8,128)(2,1)S(1)} %collective-permute-done, bf16[4,2,592,128]{3,2,1,0:T(8,128)(2,1)} %get-tuple-element.25), kind=kLoop, calls=%fused_computation.1 | loop fusion | flops 1212416 | bytes 1818624 | tf_op jit(solution)/shard_map/convert_element_type | solution.py:455
  16.9 4.5 %collective-permute-start.1 = (bf16[2,2,592,128]{3,2,1,0:T(8,128)(2,1)S(1)}, bf16[2,2,592,128]{3,2,1,0:T(8,128)(2,1)S(1)}, u32[]{:S(2)}, u32[]{:S(2)}) collective-permute-start(bf16[2,2,592,128]{3,2,1,0:T(8,128)(2,1)S(1)} %add_convert_fusion), channel_id=1, source_target_pairs={{0,2},{1,5},{2,0},{3,7},{4,6},{5,1},{6,4},{7,3},{8,10},{9,13},{10,... | collective-permute-start | bytes 1818632 | tf_op jit(solution)/shard_map/ppermute | solution.py:414
  21.4 0.0 copy-done
  21.4 1.4 %copy-done.1 = f32[1600,256]{1,0:T(8,128)S(1)} copy-done((f32[1600,256]{1,0:T(8,128)S(1)}, f32[1600,256]{1,0:T(8,128)}, u32[]{:S(2)}) %copy-start.1) | copy-done | bytes 1638424
  22.9 3.4 %assemble.4 = (bf16[4,1,592,128]{3,2,1,0:T(8,128)(2,1)S(1)}, bf16[4,1,592,128]{3,2,1,0:T(8,128)(2,1)S(1)}) custom-call(f32[1600,256]{1,0:T(8,128)S(1)} %copy-done.1, s32[16,256]{1,0:T(8,128)S(1)} %copy-done.2, bf16[192,32,128]{2,1,0:T(8,128)(2,1)S(1)} %copy-done), custom_call_target="tpu_custom_call" | custom-call | flops 1000000000 | bytes 4000000 | tf_op jit(solution)/shard_map/assemble/pallas_call | solution.py:326
  26.3 0.1 collective-permute-start.2
  26.4 3.1 %collective-permute-done.1 = bf16[2,2,592,128]{3,2,1,0:T(8,128)(2,1)S(1)} collective-permute-done((bf16[2,2,592,128]{3,2,1,0:T(8,128)(2,1)S(1)}, bf16[2,2,592,128]{3,2,1,0:T(8,128)(2,1)S(1)}, u32[]{:S(2)}, u32[]{:S(2)}) %collective-permute-start.1) | collective-permute-done | bytes 606240 | tf_op jit(solution)/shard_map/ppermute | solution.py:414
  29.5 0.2 convert_add_fusion
  29.7 0.2 collective-permute-start.5
  29.9 3.0 %assemble.5 = (bf16[4,1,592,128]{3,2,1,0:T(8,128)(2,1)S(1)}, bf16[4,1,592,128]{3,2,1,0:T(8,128)(2,1)S(1)}) custom-call(f32[1600,256]{1,0:T(8,128)S(1)} %copy-done.1, s32[16,256]{1,0:T(8,128)S(1)} %copy-done.2, bf16[192,32,128]{2,1,0:T(8,128)(2,1)S(1)} %copy-done), custom_call_target="tpu_custom_call" | custom-call | flops 1000000000 | bytes 4000000 | tf_op jit(solution)/shard_map/assemble/pallas_call | solution.py:326
  32.9 0.0 collective-permute-done.2
  32.9 1.0 %collective-permute-start.3 = (bf16[4,1,592,128]{3,2,1,0:T(8,128)(2,1)S(1)}, bf16[4,1,592,128]{3,2,1,0:T(8,128)(2,1)S(1)}, u32[]{:S(2)}, u32[]{:S(2)}) collective-permute-start(bf16[4,1,592,128]{3,2,1,0:T(8,128)(2,1)S(1)} %get-tuple-element.35), channel_id=1, source_target_pairs={{0,1},{1,0},{2,3},{3,2},{4,5},{5,4},{6,7},{7,6},{8,9},{9,8},{10,11... | collective-permute-start | bytes 1818632 | tf_op jit(solution)/shard_map/ppermute | solution.py:414
  33.9 0.1 add_convert_fusion.1
  33.9 1.1 %collective-permute-start.7 = (bf16[2,1,592,128]{3,2,1,0:T(8,128)(2,1)S(1)}, bf16[2,1,592,128]{3,2,1,0:T(8,128)(2,1)S(1)}, u32[]{:S(2)}, u32[]{:S(2)}) collective-permute-start(bf16[2,1,592,128]{3,2,1,0:T(8,128)(2,1)S(1)} %add_convert_fusion.1), channel_id=1, source_target_pairs={{0,2},{1,5},{2,0},{3,7},{4,6},{5,1},{6,4},{7,3},{8,10},{9,13},{10,... | collective-permute-start | bytes 909320 | tf_op jit(solution)/shard_map/ppermute | solution.py:414
  35.1 1.5 %collective-permute-done.5 = bf16[2,592,128]{2,1,0:T(8,128)(2,1)S(1)} collective-permute-done((bf16[2,592,128]{2,1,0:T(8,128)(2,1)S(1)}, bf16[2,592,128]{2,1,0:T(8,128)(2,1)S(1)}, u32[]{:S(2)}, u32[]{:S(2)}) %collective-permute-start.5) | collective-permute-done | bytes 303136 | tf_op jit(solution)/shard_map/ppermute | solution.py:414
  36.6 0.1 fusion
  36.7 0.2 collective-permute-start.6
  36.9 0.0 collective-permute-done.3
  36.9 0.1 add_convert_fusion.2
  37.0 2.1 %collective-permute-start.4 = (bf16[2,1,592,128]{3,2,1,0:T(8,128)(2,1)S(1)}, bf16[2,1,592,128]{3,2,1,0:T(8,128)(2,1)S(1)}, u32[]{:S(2)}, u32[]{:S(2)}) collective-permute-start(bf16[2,1,592,128]{3,2,1,0:T(8,128)(2,1)S(1)} %add_convert_fusion.2), channel_id=1, source_target_pairs={{0,2},{1,5},{2,0},{3,7},{4,6},{5,1},{6,4},{7,3},{8,10},{9,13},{10,... | collective-permute-start | bytes 909320 | tf_op jit(solution)/shard_map/ppermute | solution.py:414
  39.1 1.7 %collective-permute-done.7 = bf16[2,1,592,128]{3,2,1,0:T(8,128)(2,1)S(1)} collective-permute-done((bf16[2,1,592,128]{3,2,1,0:T(8,128)(2,1)S(1)}, bf16[2,1,592,128]{3,2,1,0:T(8,128)(2,1)S(1)}, u32[]{:S(2)}, u32[]{:S(2)}) %collective-permute-start.7) | collective-permute-done | bytes 303136 | tf_op jit(solution)/shard_map/ppermute | solution.py:414
  40.8 0.1 convert_add_fusion.2
  41.0 1.1 %collective-permute-start.10 = (bf16[1,592,128]{2,1,0:T(8,128)(2,1)S(1)}, bf16[1,592,128]{2,1,0:T(8,128)(2,1)S(1)}, u32[]{:S(2)}, u32[]{:S(2)}) collective-permute-start(bf16[1,592,128]{2,1,0:T(8,128)(2,1)S(1)} %fusion.11), channel_id=1, source_target_pairs={{0,4},{1,3},{2,6},{3,1},{4,0},{5,7},{6,2},{7,5},{8,12},{9,11},{10,... | collective-permute-start | bytes 454664 | tf_op jit(solution)/shard_map/ppermute | solution.py:414
  42.1 0.0 collective-permute-done.6
  42.1 2.9 %collective-permute-start.9 = (bf16[592,128]{1,0:T(8,128)(2,1)S(1)}, bf16[592,128]{1,0:T(8,128)(2,1)S(1)}, u32[]{:S(2)}, u32[]{:S(2)}) collective-permute-start(bf16[592,128]{1,0:T(8,128)(2,1)S(1)} %fusion.9), channel_id=1, source_target_pairs={{0,16},{8,24},{16,0},{24,8},{1,17},{9,25},{17,1},{25,9},{2,18},{10... | collective-permute-start | bytes 454664 | tf_op jit(solution)/shard_map/ppermute | solution.py:417
  45.0 1.2 %collective-permute-done.10 = bf16[1,592,128]{2,1,0:T(8,128)(2,1)S(1)} collective-permute-done((bf16[1,592,128]{2,1,0:T(8,128)(2,1)S(1)}, bf16[1,592,128]{2,1,0:T(8,128)(2,1)S(1)}, u32[]{:S(2)}, u32[]{:S(2)}) %collective-permute-start.10) | collective-permute-done | bytes 151584 | tf_op jit(solution)/shard_map/ppermute | solution.py:414
  46.2 0.0 collective-permute-done.4
  46.3 0.1 convert_add_fusion.1
  46.4 1.1 %collective-permute-start.8 = (bf16[1,592,128]{2,1,0:T(8,128)(2,1)S(1)}, bf16[1,592,128]{2,1,0:T(8,128)(2,1)S(1)}, u32[]{:S(2)}, u32[]{:S(2)}) collective-permute-start(bf16[1,592,128]{2,1,0:T(8,128)(2,1)S(1)} %fusion.12), channel_id=1, source_target_pairs={{0,4},{1,3},{2,6},{3,1},{4,0},{5,7},{6,2},{7,5},{8,12},{9,11},{10,... | collective-permute-start | bytes 454664 | tf_op jit(solution)/shard_map/ppermute | solution.py:414
  47.5 0.7 %collective-permute-start.11 = (bf16[592,128]{1,0:T(8,128)(2,1)S(1)}, bf16[592,128]{1,0:T(8,128)(2,1)S(1)}, u32[]{:S(2)}, u32[]{:S(2)}) collective-permute-start(bf16[592,128]{1,0:T(8,128)(2,1)S(1)} %fusion.13), channel_id=1, source_target_pairs={{0,8},{8,0},{16,24},{24,16},{1,9},{9,1},{17,25},{25,17},{2,10},{10... | collective-permute-start | bytes 454664 | tf_op jit(solution)/shard_map/ppermute | solution.py:417
  48.2 4.4 %collective-permute-done.9 = bf16[592,128]{1,0:T(8,128)(2,1)S(1)} collective-permute-done((bf16[592,128]{1,0:T(8,128)(2,1)S(1)}, bf16[592,128]{1,0:T(8,128)(2,1)S(1)}, u32[]{:S(2)}, u32[]{:S(2)}) %collective-permute-start.9) | collective-permute-done | bytes 151584 | tf_op jit(solution)/shard_map/ppermute | solution.py:417
  52.5 0.0 collective-permute-done.8
  52.5 3.1 %collective-permute-done.11 = bf16[592,128]{1,0:T(8,128)(2,1)S(1)} collective-permute-done((bf16[592,128]{1,0:T(8,128)(2,1)S(1)}, bf16[592,128]{1,0:T(8,128)(2,1)S(1)}, u32[]{:S(2)}, u32[]{:S(2)}) %collective-permute-start.11) | collective-permute-done | bytes 151584 | tf_op jit(solution)/shard_map/ppermute | solution.py:417
  55.7 0.1 fusion.14
  55.8 0.4 collective-permute-start.14
  56.2 1.4 %collective-permute-start.13 = (bf16[128,128]{1,0:T(8,128)(2,1)S(1)}, bf16[128,128]{1,0:T(8,128)(2,1)S(1)}, u32[]{:S(2)}, u32[]{:S(2)}) collective-permute-start(bf16[128,128]{1,0:T(8,128)(2,1)S(1)} %get-tuple-element.47), channel_id=1, source_target_pairs={{0,2},{1,3},{2,4},{3,5},{4,6},{5,7},{6,0},{7,1},{8,10},{9,11},{10,... | collective-permute-start | bytes 98312 | tf_op jit(solution)/shard_map/ppermute | solution.py:508
  57.6 0.0 collective-permute-start.12
  57.6 1.4 %collective-permute-start.15 = (bf16[64,128]{1,0:T(8,128)(2,1)S(1)}, bf16[64,128]{1,0:T(8,128)(2,1)S(1)}, u32[]{:S(2)}, u32[]{:S(2)}) collective-permute-start(bf16[64,128]{1,0:T(8,128)(2,1)S(1)} %slice.119), channel_id=1, source_target_pairs={{0,4},{1,5},{2,6},{3,7},{4,0},{5,1},{6,2},{7,3},{8,12},{9,13},{10,... | collective-permute-start | bytes 49160 | tf_op jit(solution)/shard_map/ppermute | solution.py:508
  58.9 2.6 %collective-permute-done.15.e_ref = bf16[64,128]{1,0:T(8,128)(2,1)S(1)} collective-permute-done((bf16[64,128]{1,0:T(8,128)(2,1)S(1)}, bf16[64,128]{1,0:T(8,128)(2,1)S(1)}, u32[]{:S(2)}, u32[]{:S(2)}) %collective-permute-start.15) | collective-permute-done | bytes 16416 | tf_op jit(solution)/shard_map/ppermute | solution.py:508
  61.5 0.0 collective-permute-done.14.r3_ref
  61.5 0.0 collective-permute-done.13.r2_ref
  61.5 0.3 collective-permute-done.12.r1_ref
  61.8 0.9 %finish.1 = (f32[128,1024]{1,0:T(8,128)}, f32[1,128]{1,0:T(1,128)}) custom-call(f32[592,128]{1,0:T(8,128)S(1)} %get-tuple-element.45.own_ref, bf16[128,128]{1,0:T(8,128)(2,1)S(1)} %collective-permute-done.12.r1_ref, bf16[128,128]{1,0:T(8,128)(2,1)S(1)} %collective-permute-done.13.r2_ref, bf16[128,128]{1,0:T(8,128)(2,1)S(1)} %collective-permute-done.14.r3_ref, ...), custom_call_target="tpu_custom_call" | custom-call | tf_op jit(solution)/shard_map/finish/pallas_call | solution.py:380
  (12 shorter events, 0.2 us)
Async XLA Ops:
  12.5 8.9 %copy-start = (bf16[192,32,128]{2,1,0:T(8,128)(2,1)S(1)}, bf16[192,32,128]{2,1,0:T(8,128)(2,1)}, u32[]{:S(2)}) copy-start(bf16[192,32,128]{2,1,0:T(8,128)(2,1)} %g_ref.3) | copy-start | bytes 4718596
  12.5 8.9 %copy-start.2 = (s32[16,256]{1,0:T(8,128)S(1)}, s32[16,256]{1,0:T(8,128)}, u32[]{:S(2)}) copy-start(s32[16,256]{1,0:T(8,128)} %get-tuple-element.30.table_ref) | copy-start | bytes 49156
  12.5 3.2 %collective-permute-start = (bf16[4,2,592,128]{3,2,1,0:T(8,128)(2,1)}, bf16[4,2,592,128]{3,2,1,0:T(8,128)(2,1)S(1)}, u32[]{:S(2)}, u32[]{:S(2)}) collective-permute-start(bf16[4,2,592,128]{3,2,1,0:T(8,128)(2,1)} %get-tuple-element.26), channel_id=1, source_target_pairs={{0,1},{1,0},{2,3},{3,2},{4,5},{5,4},{6,7},{7,6},{8,9},{9,8},{10,11... | collective-permute-start | bytes 3637256 | tf_op jit(solution)/shard_map/ppermute | solution.py:414
  16.9 12.5 %collective-permute-start.1 = (bf16[2,2,592,128]{3,2,1,0:T(8,128)(2,1)S(1)}, bf16[2,2,592,128]{3,2,1,0:T(8,128)(2,1)S(1)}, u32[]{:S(2)}, u32[]{:S(2)}) collective-permute-start(bf16[2,2,592,128]{3,2,1,0:T(8,128)(2,1)S(1)} %add_convert_fusion), channel_id=1, source_target_pairs={{0,2},{1,5},{2,0},{3,7},{4,6},{5,1},{6,4},{7,3},{8,10},{9,13},{10,... | collective-permute-start | bytes 1818632 | tf_op jit(solution)/shard_map/ppermute | solution.py:414
  21.4 1.4 %copy-start.1 = (f32[1600,256]{1,0:T(8,128)S(1)}, f32[1600,256]{1,0:T(8,128)}, u32[]{:S(2)}) copy-start(f32[1600,256]{1,0:T(8,128)} %get-tuple-element.23.shared_ref) | copy-start | bytes 4915204
  22.9 6.6 %copy-start.3 = (bf16[4,2,592,128]{3,2,1,0:T(8,128)(2,1)S(1)}, bf16[4,2,592,128]{3,2,1,0:T(8,128)(2,1)}, u32[]{:S(2)}) copy-start(bf16[4,2,592,128]{3,2,1,0:T(8,128)(2,1)} %get-tuple-element.25) | copy-start | bytes 3637252
  26.3 6.6 %collective-permute-start.2 = (bf16[4,1,592,128]{3,2,1,0:T(8,128)(2,1)S(1)}, bf16[4,1,592,128]{3,2,1,0:T(8,128)(2,1)S(1)}, u32[]{:S(2)}, u32[]{:S(2)}) collective-permute-start(bf16[4,1,592,128]{3,2,1,0:T(8,128)(2,1)S(1)} %get-tuple-element.28), channel_id=1, source_target_pairs={{0,1},{1,0},{2,3},{3,2},{4,5},{5,4},{6,7},{7,6},{8,9},{9,8},{10,11... | collective-permute-start | bytes 1818632 | tf_op jit(solution)/shard_map/ppermute | solution.py:414
  29.7 6.9 %collective-permute-start.5 = (bf16[2,592,128]{2,1,0:T(8,128)(2,1)S(1)}, bf16[2,592,128]{2,1,0:T(8,128)(2,1)S(1)}, u32[]{:S(2)}, u32[]{:S(2)}) collective-permute-start(bf16[2,592,128]{2,1,0:T(8,128)(2,1)S(1)} %fusion.1), channel_id=1, source_target_pairs={{0,4},{1,3},{2,6},{3,1},{4,0},{5,7},{6,2},{7,5},{8,12},{9,11},{10,... | collective-permute-start | bytes 909320 | tf_op jit(solution)/shard_map/ppermute | solution.py:414
  32.9 4.0 %collective-permute-start.3 = (bf16[4,1,592,128]{3,2,1,0:T(8,128)(2,1)S(1)}, bf16[4,1,592,128]{3,2,1,0:T(8,128)(2,1)S(1)}, u32[]{:S(2)}, u32[]{:S(2)}) collective-permute-start(bf16[4,1,592,128]{3,2,1,0:T(8,128)(2,1)S(1)} %get-tuple-element.35), channel_id=1, source_target_pairs={{0,1},{1,0},{2,3},{3,2},{4,5},{5,4},{6,7},{7,6},{8,9},{9,8},{10,11... | collective-permute-start | bytes 1818632 | tf_op jit(solution)/shard_map/ppermute | solution.py:414
  33.9 6.9 %collective-permute-start.7 = (bf16[2,1,592,128]{3,2,1,0:T(8,128)(2,1)S(1)}, bf16[2,1,592,128]{3,2,1,0:T(8,128)(2,1)S(1)}, u32[]{:S(2)}, u32[]{:S(2)}) collective-permute-start(bf16[2,1,592,128]{3,2,1,0:T(8,128)(2,1)S(1)} %add_convert_fusion.1), channel_id=1, source_target_pairs={{0,2},{1,5},{2,0},{3,7},{4,6},{5,1},{6,4},{7,3},{8,10},{9,13},{10,... | collective-permute-start | bytes 909320 | tf_op jit(solution)/shard_map/ppermute | solution.py:414
  36.7 5.4 %collective-permute-start.6 = (bf16[592,128]{1,0:T(8,128)(2,1)S(1)}, bf16[592,128]{1,0:T(8,128)(2,1)S(1)}, u32[]{:S(2)}, u32[]{:S(2)}) collective-permute-start(bf16[592,128]{1,0:T(8,128)(2,1)S(1)} %fusion.10), channel_id=1, source_target_pairs={{0,8},{8,0},{16,24},{24,16},{1,9},{9,1},{17,25},{25,17},{2,10},{10... | collective-permute-start | bytes 454664 | tf_op jit(solution)/shard_map/ppermute | solution.py:417
  37.0 9.2 %collective-permute-start.4 = (bf16[2,1,592,128]{3,2,1,0:T(8,128)(2,1)S(1)}, bf16[2,1,592,128]{3,2,1,0:T(8,128)(2,1)S(1)}, u32[]{:S(2)}, u32[]{:S(2)}) collective-permute-start(bf16[2,1,592,128]{3,2,1,0:T(8,128)(2,1)S(1)} %add_convert_fusion.2), channel_id=1, source_target_pairs={{0,2},{1,5},{2,0},{3,7},{4,6},{5,1},{6,4},{7,3},{8,10},{9,13},{10,... | collective-permute-start | bytes 909320 | tf_op jit(solution)/shard_map/ppermute | solution.py:414
  41.0 5.3 %collective-permute-start.10 = (bf16[1,592,128]{2,1,0:T(8,128)(2,1)S(1)}, bf16[1,592,128]{2,1,0:T(8,128)(2,1)S(1)}, u32[]{:S(2)}, u32[]{:S(2)}) collective-permute-start(bf16[1,592,128]{2,1,0:T(8,128)(2,1)S(1)} %fusion.11), channel_id=1, source_target_pairs={{0,4},{1,3},{2,6},{3,1},{4,0},{5,7},{6,2},{7,5},{8,12},{9,11},{10,... | collective-permute-start | bytes 454664 | tf_op jit(solution)/shard_map/ppermute | solution.py:414
  42.1 10.4 %collective-permute-start.9 = (bf16[592,128]{1,0:T(8,128)(2,1)S(1)}, bf16[592,128]{1,0:T(8,128)(2,1)S(1)}, u32[]{:S(2)}, u32[]{:S(2)}) collective-permute-start(bf16[592,128]{1,0:T(8,128)(2,1)S(1)} %fusion.9), channel_id=1, source_target_pairs={{0,16},{8,24},{16,0},{24,8},{1,17},{9,25},{17,1},{25,9},{2,18},{10... | collective-permute-start | bytes 454664 | tf_op jit(solution)/shard_map/ppermute | solution.py:417
  46.4 6.1 %collective-permute-start.8 = (bf16[1,592,128]{2,1,0:T(8,128)(2,1)S(1)}, bf16[1,592,128]{2,1,0:T(8,128)(2,1)S(1)}, u32[]{:S(2)}, u32[]{:S(2)}) collective-permute-start(bf16[1,592,128]{2,1,0:T(8,128)(2,1)S(1)} %fusion.12), channel_id=1, source_target_pairs={{0,4},{1,3},{2,6},{3,1},{4,0},{5,7},{6,2},{7,5},{8,12},{9,11},{10,... | collective-permute-start | bytes 454664 | tf_op jit(solution)/shard_map/ppermute | solution.py:414
  47.5 8.2 %collective-permute-start.11 = (bf16[592,128]{1,0:T(8,128)(2,1)S(1)}, bf16[592,128]{1,0:T(8,128)(2,1)S(1)}, u32[]{:S(2)}, u32[]{:S(2)}) collective-permute-start(bf16[592,128]{1,0:T(8,128)(2,1)S(1)} %fusion.13), channel_id=1, source_target_pairs={{0,8},{8,0},{16,24},{24,16},{1,9},{9,1},{17,25},{25,17},{2,10},{10... | collective-permute-start | bytes 454664 | tf_op jit(solution)/shard_map/ppermute | solution.py:417
  55.8 5.7 %collective-permute-start.14 = (bf16[128,128]{1,0:T(8,128)(2,1)S(1)}, bf16[128,128]{1,0:T(8,128)(2,1)S(1)}, u32[]{:S(2)}, u32[]{:S(2)}) collective-permute-start(bf16[128,128]{1,0:T(8,128)(2,1)S(1)} %get-tuple-element.46), channel_id=1, source_target_pairs={{0,3},{1,4},{2,5},{3,6},{4,7},{5,0},{6,1},{7,2},{8,11},{9,12},{10,... | collective-permute-start | bytes 98312 | tf_op jit(solution)/shard_map/ppermute | solution.py:508
  56.2 5.3 %collective-permute-start.13 = (bf16[128,128]{1,0:T(8,128)(2,1)S(1)}, bf16[128,128]{1,0:T(8,128)(2,1)S(1)}, u32[]{:S(2)}, u32[]{:S(2)}) collective-permute-start(bf16[128,128]{1,0:T(8,128)(2,1)S(1)} %get-tuple-element.47), channel_id=1, source_target_pairs={{0,2},{1,3},{2,4},{3,5},{4,6},{5,7},{6,0},{7,1},{8,10},{9,11},{10,... | collective-permute-start | bytes 98312 | tf_op jit(solution)/shard_map/ppermute | solution.py:508
  57.6 4.3 %collective-permute-start.12 = (bf16[128,128]{1,0:T(8,128)(2,1)S(1)}, bf16[128,128]{1,0:T(8,128)(2,1)S(1)}, u32[]{:S(2)}, u32[]{:S(2)}) collective-permute-start(bf16[128,128]{1,0:T(8,128)(2,1)S(1)} %get-tuple-element.48), channel_id=1, source_target_pairs={{0,1},{1,2},{2,3},{3,4},{4,5},{5,6},{6,7},{7,0},{8,9},{9,10},{10,1... | collective-permute-start | bytes 98312 | tf_op jit(solution)/shard_map/ppermute | solution.py:508
  57.6 3.9 %collective-permute-start.15 = (bf16[64,128]{1,0:T(8,128)(2,1)S(1)}, bf16[64,128]{1,0:T(8,128)(2,1)S(1)}, u32[]{:S(2)}, u32[]{:S(2)}) collective-permute-start(bf16[64,128]{1,0:T(8,128)(2,1)S(1)} %slice.119), channel_id=1, source_target_pairs={{0,4},{1,5},{2,6},{3,7},{4,0},{5,1},{6,2},{7,3},{8,12},{9,13},{10,... | collective-permute-start | bytes 49160 | tf_op jit(solution)/shard_map/ppermute | solution.py:508

commit v3 on v2

--- a/solution.py
+++ b/solution.py
@@ -243,16 +243,11 @@
 
     lax.fori_loop(used, chunks * depth_tiles, clear, 0)
 
-    unit = (iota((width, width), 0) == iota((width, width), 1)).astype(F32).astype(BF16)
-
     def chunk_step(chunk, carry):
         at = pl.multiple_of(chunk * DEPTH, DEPTH)
         wide_s[...] = spread_s[pl.ds(at, DEPTH), :].astype(BF16)
         for p in range(blocks):
-            turned = lax.dot_general(
-                unit, wide_s[:, p * width : (p + 1) * width], NT, preferred_element_type=F32
-            )
-            turned = (0.0 - turned).astype(BF16)
+            turned = -wide_s[:, p * width : (p + 1) * width].T
             turned_s[p * width : (p + 1) * width] = turned
             if p < many:
                 turned_s[(blocks + p) * width : (blocks + p + 1) * width] = turned
@@ -451,29 +446,31 @@
     for n, ks in enumerate(groups):
         keep, send, *made = assemble(ks, sub, inputs, global_deriv, blocks, regions)
         if n == 0:
+            inputs = tuple(made)
             cores[0] = near(keep, send)
+            continue
+        if n == 1:
+            cores[0] = after(cores[0], send)
             operand = both(cores[0], top).astype(BF16)
-            inputs = made[0], after(made[1], operand)
             firsts[0] = swap(operand, 2, 4)
-        elif n < last - 1:
-            inputs = inputs[0], after(inputs[1], send)
+            send = after(send, operand)
+        if n < last - 1:
             cores[n] = near(keep, send)
             firsts[n] = swap(both(cores[n], top).astype(BF16), 2, 4)
             seconds[n] = lower(cores[n], firsts[n])
             settle(n)
+            inputs = inputs[0], after(inputs[1], send)
         elif n < last:
-            firsts[0] = after(firsts[0], send)
-            value = both(cores[0], low) + firsts[0].astype(F32)
-            operand = value[1].astype(BF16)
-            inputs = inputs[0], after(inputs[1], (send, operand))
-            seconds[0] = value[0], swap(operand, 4, 2)
+            inputs = inputs[0], after(inputs[1], send)
             cores[n] = near(keep, send)
         else:
+            firsts[0] = after(firsts[0], send)
+            seconds[0] = lower(cores[0], firsts[0])
+            settle(0)
             cores[n - 1] = after(cores[n - 1], send)
             send = after(send, cores[n - 1][1])
-            cores[n] = near(keep, send)
-            seconds[0] = seconds[0][0], after(seconds[0][1], send)
-            settle(0)
+            cores[n] = after(near(keep, send), seconds[0][1])
+            cores[n - 1] = after(cores[n - 1], cores[n][1])
     firsts[last - 1] = upper(cores[last - 1])
     operand = both(cores[last], top).astype(BF16)
     firsts[last - 1] = after(firsts[last - 1], operand)

time: 62.9 us -> 65 us (1.033); the launches traced: 62.8 us -> 64.2 us
  waiting for transfers between devices: 21.1 us -> 24 us
  starting transfers between devices: 18.1 us -> 16.4 us
  other arithmetic: 2.02 us -> 0.96 us
  local copies, waits for them, and re-layouts: 1.55 us -> 2.26 us
    ppermute x9, waiting for transfers between devices: 10.7 us -> 16.9 us  [swap(): return lax.ppermute(value, 'tile', pairs)]
    ppermute x3, waiting for transfers between devices: 7.5 us -> 4.07 us  [across(): lax.ppermute(value.astype(BF16), 'region', [(r, r ^ k) for r in range(reg...]
    ppermute x3, starting transfers between devices: 3.76 us -> 1.9 us  [across(): lax.ppermute(value.astype(BF16), 'region', [(r, r ^ k) for r in range(reg...]
    ppermute x9, starting transfers between devices: 11.2 us -> 12.4 us  [swap(): return lax.ppermute(value, 'tile', pairs)]
    convert_element_type x1, other arithmetic: 1.23 us -> 0.16 us  [local(): operand = both(cores[0], top).astype(BF16)]
    ppermute x4, starting transfers between devices: 3.16 us -> 2.19 us  [onward(): return lax.ppermute(value.astype(BF16), 'tile', pairs)]
    unnamed x8, local copies, waits for them, and re-layouts: 1.45 us -> 2.16 us
  transfers between devices with their start and end apart: 16 -> 16, of which waited for: 9 -> 8; matrix products, arithmetic and copies ran while one was open for 1% -> 1% of each run, Pallas kernels for 10% -> 12%
where the time goes in v3:
time: 65 us; the launch traced here: 64.2 us
  waiting for transfers between devices  24 us (37%)
  Pallas kernels  19.7 us (30%)
  starting transfers between devices  16.4 us (25%)
  local copies, waits for them, and re-layouts  2.26 us (3%)
  other arithmetic  0.96 us (1%)
  between operations  0.81 us (1%)
    pallas_call x3, Pallas kernels, assemble(): pl.pallas_call(functools.partial(lead_kernel if lead else follow_kernel,...  18.8 us
    ppermute x9, waiting for transfers between devices, swap(): return lax.ppermute(value, 'tile', pairs)  16.9 us
    ppermute x9, starting transfers between devices, swap(): return lax.ppermute(value, 'tile', pairs)  12.4 us
    ppermute x3, waiting for transfers between devices, across(): lax.ppermute(value.astype(BF16), 'region', [(r, r ^ k) for r in range(reg...  4.07 us
    ppermute x4, waiting for transfers between devices, onward(): return lax.ppermute(value.astype(BF16), 'tile', pairs)  3.09 us
    ppermute x4, starting transfers between devices, onward(): return lax.ppermute(value.astype(BF16), 'tile', pairs)  2.19 us
    unnamed x8, local copies, waits for them, and re-layouts  2.16 us
    ppermute x3, starting transfers between devices, across(): lax.ppermute(value.astype(BF16), 'region', [(r, r ^ k) for r in range(reg...  1.9 us
  transfers between devices with their start and end apart: 16, of which 8 were waited for; matrix products, arithmetic and copies ran while one was open for 1% of the time, Pallas kernels for 12%

profile of v3, /device:TPU:0, one launch (start us, length us, event | category | flops | bytes accessed | tf_op | source)
XLA Modules:
  0.0 64.2 jit_solution(825491222487666230)
XLA Ops:
  0.6 0.0 copy-start
  0.6 11.2 %assemble.3 = (bf16[4,2,592,128]{3,2,1,0:T(8,128)(2,1)}, bf16[4,2,592,128]{3,2,1,0:T(8,128)(2,1)}, f32[1600,256]{1,0:T(8,128)}, s32[16,256]{1,0:T(8,128)}) custom-call(s32[8]{0:T(128)} %refs_0_.1, s32[1,192]{1,0:T(1,128)} %bitcast.60, s32[1,192]{1,0:T(1,128)} %bitcast.61, bf16[160,192]{1,0:T(8,128)(2,1)} %bitcast.56, bf16[32,192]{1,0:T(8,128)(2,1)} %bitcast.58, ...), custom_call_target="tpu_custom_call" | custom-call | flops 2000000000 | bytes 4000000 | tf_op jit(solution)/shard_map/assemble/pallas_call | solution.py:321
  11.9 0.5 collective-permute-start
  12.4 0.0 copy-done
  12.4 1.4 %copy-done.1 = f32[1600,256]{1,0:T(8,128)S(1)} copy-done((f32[1600,256]{1,0:T(8,128)S(1)}, f32[1600,256]{1,0:T(8,128)}, u32[]{:S(2)}) %copy-start.1) | copy-done | bytes 1638424
  13.8 0.7 %copy-done.2 = s32[16,256]{1,0:T(8,128)S(1)} copy-done((s32[16,256]{1,0:T(8,128)S(1)}, s32[16,256]{1,0:T(8,128)}, u32[]{:S(2)}) %copy-start.2) | copy-done | bytes 16408
  14.5 4.7 %assemble.4 = (bf16[4,1,592,128]{3,2,1,0:T(8,128)(2,1)S(1)}, bf16[4,1,592,128]{3,2,1,0:T(8,128)(2,1)S(1)}) custom-call(f32[1600,256]{1,0:T(8,128)S(1)} %copy-done.1, s32[16,256]{1,0:T(8,128)S(1)} %copy-done.2, bf16[192,32,128]{2,1,0:T(8,128)(2,1)S(1)} %copy-done), custom_call_target="tpu_custom_call" | custom-call | flops 1000000000 | bytes 4000000 | tf_op jit(solution)/shard_map/assemble/pallas_call | solution.py:321
  19.2 0.0 collective-permute-done
  19.3 0.2 add_convert_fusion
  19.4 0.1 collective-permute-start.1
  19.5 2.0 %collective-permute-start.3 = (bf16[2,2,592,128]{3,2,1,0:T(8,128)(2,1)S(1)}, bf16[2,2,592,128]{3,2,1,0:T(8,128)(2,1)S(1)}, u32[]{:S(2)}, u32[]{:S(2)}) collective-permute-start(bf16[2,2,592,128]{3,2,1,0:T(8,128)(2,1)S(1)} %add_convert_fusion), channel_id=1, source_target_pairs={{0,2},{1,5},{2,0},{3,7},{4,6},{5,1},{6,4},{7,3},{8,10},{9,13},{10,... | collective-permute-start | bytes 1818632 | tf_op jit(solution)/shard_map/ppermute | solution.py:409
  21.5 2.9 %assemble.5 = (bf16[4,1,592,128]{3,2,1,0:T(8,128)(2,1)S(1)}, bf16[4,1,592,128]{3,2,1,0:T(8,128)(2,1)S(1)}) custom-call(f32[1600,256]{1,0:T(8,128)S(1)} %copy-done.1, s32[16,256]{1,0:T(8,128)S(1)} %copy-done.2, bf16[192,32,128]{2,1,0:T(8,128)(2,1)S(1)} %copy-done), custom_call_target="tpu_custom_call" | custom-call | flops 1000000000 | bytes 4000000 | tf_op jit(solution)/shard_map/assemble/pallas_call | solution.py:321
  24.4 0.0 collective-permute-done.1
  24.4 1.1 %collective-permute-start.2 = (bf16[4,1,592,128]{3,2,1,0:T(8,128)(2,1)S(1)}, bf16[4,1,592,128]{3,2,1,0:T(8,128)(2,1)S(1)}, u32[]{:S(2)}, u32[]{:S(2)}) collective-permute-start(bf16[4,1,592,128]{3,2,1,0:T(8,128)(2,1)S(1)} %get-tuple-element.41), channel_id=1, source_target_pairs={{0,1},{1,0},{2,3},{3,2},{4,5},{5,4},{6,7},{7,6},{8,9},{9,8},{10,11... | collective-permute-start | bytes 1818632 | tf_op jit(solution)/shard_map/ppermute | solution.py:409
  25.4 4.2 %collective-permute-done.3 = bf16[2,2,592,128]{3,2,1,0:T(8,128)(2,1)S(1)} collective-permute-done((bf16[2,2,592,128]{3,2,1,0:T(8,128)(2,1)S(1)}, bf16[2,2,592,128]{3,2,1,0:T(8,128)(2,1)S(1)}, u32[]{:S(2)}, u32[]{:S(2)}) %collective-permute-start.3) | collective-permute-done | bytes 606240 | tf_op jit(solution)/shard_map/ppermute | solution.py:409
  29.6 0.2 convert_add_fusion
  29.9 2.8 %collective-permute-start.4 = (bf16[2,592,128]{2,1,0:T(8,128)(2,1)S(1)}, bf16[2,592,128]{2,1,0:T(8,128)(2,1)S(1)}, u32[]{:S(2)}, u32[]{:S(2)}) collective-permute-start(bf16[2,592,128]{2,1,0:T(8,128)(2,1)S(1)} %fusion.1), channel_id=1, source_target_pairs={{0,4},{1,3},{2,6},{3,1},{4,0},{5,7},{6,2},{7,5},{8,12},{9,11},{10,... | collective-permute-start | bytes 909320 | tf_op jit(solution)/shard_map/ppermute | solution.py:409
  32.7 4.8 %collective-permute-done.4 = bf16[2,592,128]{2,1,0:T(8,128)(2,1)S(1)} collective-permute-done((bf16[2,592,128]{2,1,0:T(8,128)(2,1)S(1)}, bf16[2,592,128]{2,1,0:T(8,128)(2,1)S(1)}, u32[]{:S(2)}, u32[]{:S(2)}) %collective-permute-start.4) | collective-permute-done | bytes 303136 | tf_op jit(solution)/shard_map/ppermute | solution.py:409
  37.5 0.1 fusion
  37.6 0.0 collective-permute-done.2
  37.6 0.1 add_convert_fusion.1
  37.7 1.2 %collective-permute-start.7 = (bf16[2,1,592,128]{3,2,1,0:T(8,128)(2,1)S(1)}, bf16[2,1,592,128]{3,2,1,0:T(8,128)(2,1)S(1)}, u32[]{:S(2)}, u32[]{:S(2)}) collective-permute-start(bf16[2,1,592,128]{3,2,1,0:T(8,128)(2,1)S(1)} %add_convert_fusion.1), channel_id=1, source_target_pairs={{0,2},{1,5},{2,0},{3,7},{4,6},{5,1},{6,4},{7,3},{8,10},{9,13},{10,... | collective-permute-start | bytes 909320 | tf_op jit(solution)/shard_map/ppermute | solution.py:409
  39.0 1.2 %collective-permute-start.6 = (bf16[592,128]{1,0:T(8,128)(2,1)S(1)}, bf16[592,128]{1,0:T(8,128)(2,1)S(1)}, u32[]{:S(2)}, u32[]{:S(2)}) collective-permute-start(bf16[592,128]{1,0:T(8,128)(2,1)S(1)} %fusion.10), channel_id=1, source_target_pairs={{0,8},{8,0},{16,24},{24,16},{1,9},{9,1},{17,25},{25,17},{2,10},{10... | collective-permute-start | bytes 454664 | tf_op jit(solution)/shard_map/ppermute | solution.py:412
  40.2 0.1 add_convert_fusion.2
  40.2 0.1 collective-permute-start.5
  40.4 4.2 %collective-permute-done.7 = bf16[2,1,592,128]{3,2,1,0:T(8,128)(2,1)S(1)} collective-permute-done((bf16[2,1,592,128]{3,2,1,0:T(8,128)(2,1)S(1)}, bf16[2,1,592,128]{3,2,1,0:T(8,128)(2,1)S(1)}, u32[]{:S(2)}, u32[]{:S(2)}) %collective-permute-start.7) | collective-permute-done | bytes 303136 | tf_op jit(solution)/shard_map/ppermute | solution.py:409
  44.6 0.1 convert_add_fusion.2
  44.7 2.1 %collective-permute-start.10 = (bf16[1,592,128]{2,1,0:T(8,128)(2,1)S(1)}, bf16[1,592,128]{2,1,0:T(8,128)(2,1)S(1)}, u32[]{:S(2)}, u32[]{:S(2)}) collective-permute-start(bf16[1,592,128]{2,1,0:T(8,128)(2,1)S(1)} %fusion.11), channel_id=1, source_target_pairs={{0,4},{1,3},{2,6},{3,1},{4,0},{5,7},{6,2},{7,5},{8,12},{9,11},{10,... | collective-permute-start | bytes 454664 | tf_op jit(solution)/shard_map/ppermute | solution.py:409
  46.8 0.0 collective-permute-done.6
  46.8 0.6 collective-permute-start.9
  47.5 2.6 %collective-permute-done.5 = bf16[2,1,592,128]{3,2,1,0:T(8,128)(2,1)S(1)} collective-permute-done((bf16[2,1,592,128]{3,2,1,0:T(8,128)(2,1)S(1)}, bf16[2,1,592,128]{3,2,1,0:T(8,128)(2,1)S(1)}, u32[]{:S(2)}, u32[]{:S(2)}) %collective-permute-start.5) | collective-permute-done | bytes 303136 | tf_op jit(solution)/shard_map/ppermute | solution.py:409
  50.1 0.1 convert_add_fusion.1
  50.2 2.4 %collective-permute-start.8 = (bf16[1,592,128]{2,1,0:T(8,128)(2,1)S(1)}, bf16[1,592,128]{2,1,0:T(8,128)(2,1)S(1)}, u32[]{:S(2)}, u32[]{:S(2)}) collective-permute-start(bf16[1,592,128]{2,1,0:T(8,128)(2,1)S(1)} %fusion.12), channel_id=1, source_target_pairs={{0,4},{1,3},{2,6},{3,1},{4,0},{5,7},{6,2},{7,5},{8,12},{9,11},{10,... | collective-permute-start | bytes 454664 | tf_op jit(solution)/shard_map/ppermute | solution.py:409
  52.6 0.0 collective-permute-done.10
  52.6 0.1 collective-permute-start.11
  52.7 1.9 %collective-permute-done.9 = bf16[592,128]{1,0:T(8,128)(2,1)S(1)} collective-permute-done((bf16[592,128]{1,0:T(8,128)(2,1)S(1)}, bf16[592,128]{1,0:T(8,128)(2,1)S(1)}, u32[]{:S(2)}, u32[]{:S(2)}) %collective-permute-start.9) | collective-permute-done | bytes 151584 | tf_op jit(solution)/shard_map/ppermute | solution.py:412
  54.6 1.1 %collective-permute-done.8 = bf16[1,592,128]{2,1,0:T(8,128)(2,1)S(1)} collective-permute-done((bf16[1,592,128]{2,1,0:T(8,128)(2,1)S(1)}, bf16[1,592,128]{2,1,0:T(8,128)(2,1)S(1)}, u32[]{:S(2)}, u32[]{:S(2)}) %collective-permute-start.8) | collective-permute-done | bytes 151584 | tf_op jit(solution)/shard_map/ppermute | solution.py:409
  55.7 2.1 %collective-permute-done.11 = bf16[592,128]{1,0:T(8,128)(2,1)S(1)} collective-permute-done((bf16[592,128]{1,0:T(8,128)(2,1)S(1)}, bf16[592,128]{1,0:T(8,128)(2,1)S(1)}, u32[]{:S(2)}, u32[]{:S(2)}) %collective-permute-start.11) | collective-permute-done | bytes 151584 | tf_op jit(solution)/shard_map/ppermute | solution.py:412
  57.9 0.1 fusion.14
  58.0 0.1 collective-permute-start.14
  58.0 0.2 collective-permute-start.13
  58.2 1.1 %collective-permute-start.12 = (bf16[128,128]{1,0:T(8,128)(2,1)S(1)}, bf16[128,128]{1,0:T(8,128)(2,1)S(1)}, u32[]{:S(2)}, u32[]{:S(2)}) collective-permute-start(bf16[128,128]{1,0:T(8,128)(2,1)S(1)} %get-tuple-element.58), channel_id=1, source_target_pairs={{0,1},{1,2},{2,3},{3,4},{4,5},{5,6},{6,7},{7,0},{8,9},{9,10},{10,1... | collective-permute-start | bytes 98312 | tf_op jit(solution)/shard_map/ppermute | solution.py:505
  59.4 0.8 %collective-permute-start.15 = (bf16[64,128]{1,0:T(8,128)(2,1)S(1)}, bf16[64,128]{1,0:T(8,128)(2,1)S(1)}, u32[]{:S(2)}, u32[]{:S(2)}) collective-permute-start(bf16[64,128]{1,0:T(8,128)(2,1)S(1)} %slice.115), channel_id=1, source_target_pairs={{0,4},{1,5},{2,6},{3,7},{4,0},{5,1},{6,2},{7,3},{8,12},{9,13},{10,... | collective-permute-start | bytes 49160 | tf_op jit(solution)/shard_map/ppermute | solution.py:505
  60.2 3.1 %collective-permute-done.15.e_ref = bf16[64,128]{1,0:T(8,128)(2,1)S(1)} collective-permute-done((bf16[64,128]{1,0:T(8,128)(2,1)S(1)}, bf16[64,128]{1,0:T(8,128)(2,1)S(1)}, u32[]{:S(2)}, u32[]{:S(2)}) %collective-permute-start.15) | collective-permute-done | bytes 16416 | tf_op jit(solution)/shard_map/ppermute | solution.py:505
  63.2 0.0 collective-permute-done.14.r3_ref
  63.2 0.0 collective-permute-done.13.r2_ref
  63.2 0.0 collective-permute-done.12.r1_ref
  63.3 0.9 %finish.1 = (f32[128,1024]{1,0:T(8,128)}, f32[1,128]{1,0:T(1,128)}) custom-call(f32[592,128]{1,0:T(8,128)S(1)} %get-tuple-element.55.own_ref, bf16[128,128]{1,0:T(8,128)(2,1)S(1)} %collective-permute-done.12.r1_ref, bf16[128,128]{1,0:T(8,128)(2,1)S(1)} %collective-permute-done.13.r2_ref, bf16[128,128]{1,0:T(8,128)(2,1)S(1)} %collective-permute-done.14.r3_ref, ...), custom_call_target="tpu_custom_call" | custom-call | tf_op jit(solution)/shard_map/finish/pallas_call | solution.py:375
  (12 shorter events, 0.2 us)
Async XLA Ops:
  0.6 11.8 %copy-start = (bf16[192,32,128]{2,1,0:T(8,128)(2,1)S(1)}, bf16[192,32,128]{2,1,0:T(8,128)(2,1)}, u32[]{:S(2)}) copy-start(bf16[192,32,128]{2,1,0:T(8,128)(2,1)} %g_ref.3) | copy-start | bytes 4718596
  11.9 7.4 %collective-permute-start = (bf16[4,2,592,128]{3,2,1,0:T(8,128)(2,1)}, bf16[4,2,592,128]{3,2,1,0:T(8,128)(2,1)S(1)}, u32[]{:S(2)}, u32[]{:S(2)}) collective-permute-start(bf16[4,2,592,128]{3,2,1,0:T(8,128)(2,1)} %get-tuple-element.32), channel_id=1, source_target_pairs={{0,1},{1,0},{2,3},{3,2},{4,5},{5,4},{6,7},{7,6},{8,9},{9,8},{10,11... | collective-permute-start | bytes 3637256 | tf_op jit(solution)/shard_map/ppermute | solution.py:409
  12.4 1.4 %copy-start.1 = (f32[1600,256]{1,0:T(8,128)S(1)}, f32[1600,256]{1,0:T(8,128)}, u32[]{:S(2)}) copy-start(f32[1600,256]{1,0:T(8,128)} %get-tuple-element.28.shared_ref) | copy-start | bytes 4915204
  13.8 0.7 %copy-start.2 = (s32[16,256]{1,0:T(8,128)S(1)}, s32[16,256]{1,0:T(8,128)}, u32[]{:S(2)}) copy-start(s32[16,256]{1,0:T(8,128)} %get-tuple-element.36.table_ref) | copy-start | bytes 49156
  14.5 4.7 %copy-start.3 = (bf16[4,2,592,128]{3,2,1,0:T(8,128)(2,1)S(1)}, bf16[4,2,592,128]{3,2,1,0:T(8,128)(2,1)}, u32[]{:S(2)}) copy-start(bf16[4,2,592,128]{3,2,1,0:T(8,128)(2,1)} %get-tuple-element.33) | copy-start | bytes 3637252
  19.4 5.0 %collective-permute-start.1 = (bf16[4,1,592,128]{3,2,1,0:T(8,128)(2,1)S(1)}, bf16[4,1,592,128]{3,2,1,0:T(8,128)(2,1)S(1)}, u32[]{:S(2)}, u32[]{:S(2)}) collective-permute-start(bf16[4,1,592,128]{3,2,1,0:T(8,128)(2,1)S(1)} %get-tuple-element.35), channel_id=1, source_target_pairs={{0,1},{1,0},{2,3},{3,2},{4,5},{5,4},{6,7},{7,6},{8,9},{9,8},{10,11... | collective-permute-start | bytes 1818632 | tf_op jit(solution)/shard_map/ppermute | solution.py:409
  19.5 10.1 %collective-permute-start.3 = (bf16[2,2,592,128]{3,2,1,0:T(8,128)(2,1)S(1)}, bf16[2,2,592,128]{3,2,1,0:T(8,128)(2,1)S(1)}, u32[]{:S(2)}, u32[]{:S(2)}) collective-permute-start(bf16[2,2,592,128]{3,2,1,0:T(8,128)(2,1)S(1)} %add_convert_fusion), channel_id=1, source_target_pairs={{0,2},{1,5},{2,0},{3,7},{4,6},{5,1},{6,4},{7,3},{8,10},{9,13},{10,... | collective-permute-start | bytes 1818632 | tf_op jit(solution)/shard_map/ppermute | solution.py:409
  24.4 13.2 %collective-permute-start.2 = (bf16[4,1,592,128]{3,2,1,0:T(8,128)(2,1)S(1)}, bf16[4,1,592,128]{3,2,1,0:T(8,128)(2,1)S(1)}, u32[]{:S(2)}, u32[]{:S(2)}) collective-permute-start(bf16[4,1,592,128]{3,2,1,0:T(8,128)(2,1)S(1)} %get-tuple-element.41), channel_id=1, source_target_pairs={{0,1},{1,0},{2,3},{3,2},{4,5},{5,4},{6,7},{7,6},{8,9},{9,8},{10,11... | collective-permute-start | bytes 1818632 | tf_op jit(solution)/shard_map/ppermute | solution.py:409
  29.9 7.6 %collective-permute-start.4 = (bf16[2,592,128]{2,1,0:T(8,128)(2,1)S(1)}, bf16[2,592,128]{2,1,0:T(8,128)(2,1)S(1)}, u32[]{:S(2)}, u32[]{:S(2)}) collective-permute-start(bf16[2,592,128]{2,1,0:T(8,128)(2,1)S(1)} %fusion.1), channel_id=1, source_target_pairs={{0,4},{1,3},{2,6},{3,1},{4,0},{5,7},{6,2},{7,5},{8,12},{9,11},{10,... | collective-permute-start | bytes 909320 | tf_op jit(solution)/shard_map/ppermute | solution.py:409
  37.7 6.9 %collective-permute-start.7 = (bf16[2,1,592,128]{3,2,1,0:T(8,128)(2,1)S(1)}, bf16[2,1,592,128]{3,2,1,0:T(8,128)(2,1)S(1)}, u32[]{:S(2)}, u32[]{:S(2)}) collective-permute-start(bf16[2,1,592,128]{3,2,1,0:T(8,128)(2,1)S(1)} %add_convert_fusion.1), channel_id=1, source_target_pairs={{0,2},{1,5},{2,0},{3,7},{4,6},{5,1},{6,4},{7,3},{8,10},{9,13},{10,... | collective-permute-start | bytes 909320 | tf_op jit(solution)/shard_map/ppermute | solution.py:409
  39.0 7.8 %collective-permute-start.6 = (bf16[592,128]{1,0:T(8,128)(2,1)S(1)}, bf16[592,128]{1,0:T(8,128)(2,1)S(1)}, u32[]{:S(2)}, u32[]{:S(2)}) collective-permute-start(bf16[592,128]{1,0:T(8,128)(2,1)S(1)} %fusion.10), channel_id=1, source_target_pairs={{0,8},{8,0},{16,24},{24,16},{1,9},{9,1},{17,25},{25,17},{2,10},{10... | collective-permute-start | bytes 454664 | tf_op jit(solution)/shard_map/ppermute | solution.py:412
  40.2 9.8 %collective-permute-start.5 = (bf16[2,1,592,128]{3,2,1,0:T(8,128)(2,1)S(1)}, bf16[2,1,592,128]{3,2,1,0:T(8,128)(2,1)S(1)}, u32[]{:S(2)}, u32[]{:S(2)}) collective-permute-start(bf16[2,1,592,128]{3,2,1,0:T(8,128)(2,1)S(1)} %add_convert_fusion.2), channel_id=1, source_target_pairs={{0,2},{1,5},{2,0},{3,7},{4,6},{5,1},{6,4},{7,3},{8,10},{9,13},{10,... | collective-permute-start | bytes 909320 | tf_op jit(solution)/shard_map/ppermute | solution.py:409
  44.7 7.9 %collective-permute-start.10 = (bf16[1,592,128]{2,1,0:T(8,128)(2,1)S(1)}, bf16[1,592,128]{2,1,0:T(8,128)(2,1)S(1)}, u32[]{:S(2)}, u32[]{:S(2)}) collective-permute-start(bf16[1,592,128]{2,1,0:T(8,128)(2,1)S(1)} %fusion.11), channel_id=1, source_target_pairs={{0,4},{1,3},{2,6},{3,1},{4,0},{5,7},{6,2},{7,5},{8,12},{9,11},{10,... | collective-permute-start | bytes 454664 | tf_op jit(solution)/shard_map/ppermute | solution.py:409
  46.8 7.8 %collective-permute-start.9 = (bf16[592,128]{1,0:T(8,128)(2,1)S(1)}, bf16[592,128]{1,0:T(8,128)(2,1)S(1)}, u32[]{:S(2)}, u32[]{:S(2)}) collective-permute-start(bf16[592,128]{1,0:T(8,128)(2,1)S(1)} %fusion.9), channel_id=1, source_target_pairs={{0,16},{8,24},{16,0},{24,8},{1,17},{9,25},{17,1},{25,9},{2,18},{10... | collective-permute-start | bytes 454664 | tf_op jit(solution)/shard_map/ppermute | solution.py:412
  50.2 5.5 %collective-permute-start.8 = (bf16[1,592,128]{2,1,0:T(8,128)(2,1)S(1)}, bf16[1,592,128]{2,1,0:T(8,128)(2,1)S(1)}, u32[]{:S(2)}, u32[]{:S(2)}) collective-permute-start(bf16[1,592,128]{2,1,0:T(8,128)(2,1)S(1)} %fusion.12), channel_id=1, source_target_pairs={{0,4},{1,3},{2,6},{3,1},{4,0},{5,7},{6,2},{7,5},{8,12},{9,11},{10,... | collective-permute-start | bytes 454664 | tf_op jit(solution)/shard_map/ppermute | solution.py:409
  52.6 5.3 %collective-permute-start.11 = (bf16[592,128]{1,0:T(8,128)(2,1)S(1)}, bf16[592,128]{1,0:T(8,128)(2,1)S(1)}, u32[]{:S(2)}, u32[]{:S(2)}) collective-permute-start(bf16[592,128]{1,0:T(8,128)(2,1)S(1)} %fusion.13), channel_id=1, source_target_pairs={{0,8},{8,0},{16,24},{24,16},{1,9},{9,1},{17,25},{25,17},{2,10},{10... | collective-permute-start | bytes 454664 | tf_op jit(solution)/shard_map/ppermute | solution.py:412
  58.0 5.3 %collective-permute-start.14 = (bf16[128,128]{1,0:T(8,128)(2,1)S(1)}, bf16[128,128]{1,0:T(8,128)(2,1)S(1)}, u32[]{:S(2)}, u32[]{:S(2)}) collective-permute-start(bf16[128,128]{1,0:T(8,128)(2,1)S(1)} %get-tuple-element.56), channel_id=1, source_target_pairs={{0,3},{1,4},{2,5},{3,6},{4,7},{5,0},{6,1},{7,2},{8,11},{9,12},{10,... | collective-permute-start | bytes 98312 | tf_op jit(solution)/shard_map/ppermute | solution.py:505
  58.0 5.2 %collective-permute-start.13 = (bf16[128,128]{1,0:T(8,128)(2,1)S(1)}, bf16[128,128]{1,0:T(8,128)(2,1)S(1)}, u32[]{:S(2)}, u32[]{:S(2)}) collective-permute-start(bf16[128,128]{1,0:T(8,128)(2,1)S(1)} %get-tuple-element.57), channel_id=1, source_target_pairs={{0,2},{1,3},{2,4},{3,5},{4,6},{5,7},{6,0},{7,1},{8,10},{9,11},{10,... | collective-permute-start | bytes 98312 | tf_op jit(solution)/shard_map/ppermute | solution.py:505
  58.2 5.0 %collective-permute-start.12 = (bf16[128,128]{1,0:T(8,128)(2,1)S(1)}, bf16[128,128]{1,0:T(8,128)(2,1)S(1)}, u32[]{:S(2)}, u32[]{:S(2)}) collective-permute-start(bf16[128,128]{1,0:T(8,128)(2,1)S(1)} %get-tuple-element.58), channel_id=1, source_target_pairs={{0,1},{1,2},{2,3},{3,4},{4,5},{5,6},{6,7},{7,0},{8,9},{9,10},{10,1... | collective-permute-start | bytes 98312 | tf_op jit(solution)/shard_map/ppermute | solution.py:505
  59.4 3.8 %collective-permute-start.15 = (bf16[64,128]{1,0:T(8,128)(2,1)S(1)}, bf16[64,128]{1,0:T(8,128)(2,1)S(1)}, u32[]{:S(2)}, u32[]{:S(2)}) collective-permute-start(bf16[64,128]{1,0:T(8,128)(2,1)S(1)} %slice.115), channel_id=1, source_target_pairs={{0,4},{1,5},{2,6},{3,7},{4,0},{5,1},{6,2},{7,3},{8,12},{9,13},{10,... | collective-permute-start | bytes 49160 | tf_op jit(solution)/shard_map/ppermute | solution.py:505

commit v4 on v3

--- a/solution.py
+++ b/solution.py
@@ -423,80 +423,45 @@
         return pair[0][part].astype(F32) + pair[1][part].astype(F32)
 
     low, top = slice(0, blocks // 4), slice(blocks // 4, blocks // 2)
-    def upper(pair):
-        return swap(both(pair, top).astype(BF16), 2, 4)
-
-    def lower(pair, more):
-        value = both(pair, low) + more.astype(F32)
-        return value[0], swap(value[1].astype(BF16), 4, 2)
-
-    groups = [(k + 1, k) for k in range(regions - 2, 0, -2)] + [(1,), (0,)]
     def after(value, other):
-        return lax.optimization_barrier((value, other))[0]
-
-    last = len(groups) - 1
-    totals = [None] * regions
-    cores, firsts, seconds = ([None] * (last + 1) for _ in range(3))
-
-    def settle(n):
-        value = seconds[n][0] + seconds[n][1].astype(F32)
-        for place, k in enumerate(groups[n]):
-            totals[k] = value[place]
-
-    for n, ks in enumerate(groups):
-        keep, send, *made = assemble(ks, sub, inputs, global_deriv, blocks, regions)
-        if n == 0:
-            inputs = tuple(made)
-            cores[0] = near(keep, send)
-            continue
-        if n == 1:
-            cores[0] = after(cores[0], send)
-            operand = both(cores[0], top).astype(BF16)
-            firsts[0] = swap(operand, 2, 4)
-            send = after(send, operand)
-        if n < last - 1:
-            cores[n] = near(keep, send)
-            firsts[n] = swap(both(cores[n], top).astype(BF16), 2, 4)
-            seconds[n] = lower(cores[n], firsts[n])
-            settle(n)
-            inputs = inputs[0], after(inputs[1], send)
-        elif n < last:
-            inputs = inputs[0], after(inputs[1], send)
-            cores[n] = near(keep, send)
-        else:
-            firsts[0] = after(firsts[0], send)
-            seconds[0] = lower(cores[0], firsts[0])
-            settle(0)
-            cores[n - 1] = after(cores[n - 1], send)
-            send = after(send, cores[n - 1][1])
-            cores[n] = after(near(keep, send), seconds[0][1])
-            cores[n - 1] = after(cores[n - 1], cores[n][1])
-    firsts[last - 1] = upper(cores[last - 1])
-    operand = both(cores[last], top).astype(BF16)
-    firsts[last - 1] = after(firsts[last - 1], operand)
-    value = both(cores[last - 1], low) + firsts[last - 1].astype(F32)
-    half, more = value[0], value[1].astype(BF16)
-    firsts[last] = swap(operand, 2, 4)
-    seconds[last - 1] = half, after(swap(more, 4, 2), firsts[last])
-    settle(last - 1)
-    crossed = []
-    for k in range(regions - 1, 1, -1):
-        step = k & -k
-        operand = totals[k].astype(BF16)
-        if k == 2:
-            firsts[last] = after(firsts[last], operand)
-        value = across(operand, step)
-        if k == 3:
-            value = after(value, more)
-        if k == step:
-            crossed.append(value)
-        else:
-            totals[k - step] = totals[k - step] + value.astype(F32)
-    seconds[last] = lower(cores[last], firsts[last])
-    settle(last)
-    own = totals[0]
-    for value in crossed + [across(totals[1], 1)]:
-        own = own + value.astype(F32)
+        return value if other is None else lax.optimization_barrier((value, other))[0]
+
+    cores, firsts, seconds = ([None] * regions for _ in range(3))
+    incoming = [[] for _ in range(regions)]
+    own = None
+    for slot in range(regions + 3):
+        done, operands = None, []
+        if slot < regions:
+            k = regions - 1 - slot
+            keep, send, *made = assemble((k,), sub, inputs, global_deriv, blocks, regions)
+            inputs = tuple(made) if made else inputs
+            done = send
+        elif slot == regions:
+            done = both(cores[0], top)[:, 0].astype(BF16)
+        k = regions - 1 - (slot - 3)
+        if 0 <= k < regions:
+            total = seconds[k][0] + after(seconds[k][1], done).astype(F32)
+            for value in incoming[k]:
+                total = total + value.astype(F32)
+            if k:
+                operands.append(total.astype(BF16))
+                incoming[k - (k & -k)].append(across(operands[-1], k & -k))
+            else:
+                own = total
+        k -= 1
+        if 0 <= k < regions:
+            total = both(cores[k], low)[:, 0] + after(firsts[k], done).astype(F32)
+            operands.append(total[1].astype(BF16))
+            seconds[k] = total[0], swap(operands[-1], 4, 2)
+        k -= 1
+        if 0 <= k < regions:
+            if slot < regions:
+                cores[k] = after(cores[k], done)
+            operands.append(both(cores[k], top)[:, 0].astype(BF16))
+            firsts[k] = swap(operands[-1], 2, 4)
+        if slot < regions:
+            inputs = inputs[0], after(inputs[1], (send, operands))
+            cores[k - 1] = near(keep, send)
 
     def onward(value, d):
         pairs = [

time: 65 us -> 59.7 us (0.918)
  waiting for transfers between devices: 24 us -> 18.4 us
  starting transfers between devices: 16.4 us -> 17.8 us
    ppermute x9 -> x12, waiting for transfers between devices: 16.9 us -> 10.5 us  [swap(): return lax.ppermute(value, 'tile', pairs)]
    ppermute x3, starting transfers between devices: 1.9 us -> 5.87 us  [across(): lax.ppermute(value.astype(BF16), 'region', [(r, r ^ k) for r in range(reg...]
    ppermute x9 -> x12, starting transfers between devices: 12.4 us -> 9.42 us  [swap(): return lax.ppermute(value, 'tile', pairs)]
    ppermute x3, waiting for transfers between devices: 4.07 us -> 4.83 us  [across(): lax.ppermute(value.astype(BF16), 'region', [(r, r ^ k) for r in range(reg...]
    pallas_call x3 -> x4, Pallas kernels: 18.8 us -> 18.2 us  [assemble(): pl.pallas_call(functools.partial(lead_kernel if lead else follow_kernel,...]
    unnamed x8 -> x12, local copies, waits for them, and re-layouts: 2.16 us -> 2.16 us
  transfers between devices with their start and end apart: 16 -> 19, of which waited for: 8 -> 8; matrix products, arithmetic and copies ran while one was open for 1% -> 2% of each run, Pallas kernels for 12% -> 16%
where the time goes in v4:
time: 59.7 us; the launch traced here: 59.4 us
  Pallas kernels  19.2 us (32%)
  waiting for transfers between devices  18.4 us (31%)
  starting transfers between devices  17.8 us (30%)
  local copies, waits for them, and re-layouts  2.25 us (4%)
  other arithmetic  0.97 us (2%)
  between operations  0.8 us (1%)
    pallas_call x4, Pallas kernels, assemble(): pl.pallas_call(functools.partial(lead_kernel if lead else follow_kernel,...  18.2 us
    ppermute x12, waiting for transfers between devices, swap(): return lax.ppermute(value, 'tile', pairs)  10.5 us
    ppermute x12, starting transfers between devices, swap(): return lax.ppermute(value, 'tile', pairs)  9.42 us
    ppermute x3, starting transfers between devices, across(): lax.ppermute(value.astype(BF16), 'region', [(r, r ^ k) for r in range(reg...  5.87 us
    ppermute x3, waiting for transfers between devices, across(): lax.ppermute(value.astype(BF16), 'region', [(r, r ^ k) for r in range(reg...  4.83 us
    ppermute x4, waiting for transfers between devices, onward(): return lax.ppermute(value.astype(BF16), 'tile', pairs)  3.09 us
    ppermute x4, starting transfers between devices, onward(): return lax.ppermute(value.astype(BF16), 'tile', pairs)  2.54 us
    unnamed x12, local copies, waits for them, and re-layouts  2.16 us
  transfers between devices with their start and end apart: 19, of which 8 were waited for; matrix products, arithmetic and copies ran while one was open for 2% of the time, Pallas kernels for 16%

profile of v4, /device:TPU:0, one launch (start us, length us, event | category | flops | bytes accessed | tf_op | source)
XLA Modules:
  0.0 59.4 jit_solution(4518010340545093394)
XLA Ops:
  0.6 8.7 %assemble.4 = (bf16[4,1,592,128]{3,2,1,0:T(8,128)(2,1)}, bf16[4,1,592,128]{3,2,1,0:T(8,128)(2,1)}, f32[1600,256]{1,0:T(8,128)}, s32[16,256]{1,0:T(8,128)}) custom-call(s32[8]{0:T(128)} %refs_0_.1, s32[1,192]{1,0:T(1,128)} %bitcast.87, s32[1,192]{1,0:T(1,128)} %bitcast.88, bf16[160,192]{1,0:T(8,128)(2,1)} %bitcast.83, bf16[32,192]{1,0:T(8,128)(2,1)} %bitcast.85, ...), custom_call_target="tpu_custom_call" | custom-call | flops 1000000000 | bytes 4000000 | tf_op jit(solution)/shard_map/assemble/pallas_call | solution.py:321
  9.4 0.5 collective-permute-start
  9.9 1.4 %copy-done.1 = f32[1600,256]{1,0:T(8,128)S(1)} copy-done((f32[1600,256]{1,0:T(8,128)S(1)}, f32[1600,256]{1,0:T(8,128)}, u32[]{:S(2)}) %copy-start.1) | copy-done | bytes 1638424
  11.3 0.7 %copy-done.3 = s32[16,256]{1,0:T(8,128)S(1)} copy-done((s32[16,256]{1,0:T(8,128)S(1)}, s32[16,256]{1,0:T(8,128)}, u32[]{:S(2)}) %copy-start.3) | copy-done | bytes 16408
  12.0 3.3 %assemble.5 = (bf16[4,1,592,128]{3,2,1,0:T(8,128)(2,1)S(1)}, bf16[4,1,592,128]{3,2,1,0:T(8,128)(2,1)S(1)}) custom-call(f32[1600,256]{1,0:T(8,128)S(1)} %copy-done.1, s32[16,256]{1,0:T(8,128)S(1)} %copy-done.3, bf16[192,32,128]{2,1,0:T(8,128)(2,1)S(1)} %copy-done), custom_call_target="tpu_custom_call" | custom-call | flops 1000000000 | bytes 4000000 | tf_op jit(solution)/shard_map/assemble/pallas_call | solution.py:321
  15.4 0.2 collective-permute-start.2
  15.5 0.0 collective-permute-done
  15.5 0.1 fusion
  15.6 4.4 %collective-permute-start.1 = (bf16[2,592,128]{2,1,0:T(8,128)(2,1)S(1)}, bf16[2,592,128]{2,1,0:T(8,128)(2,1)S(1)}, u32[]{:S(2)}, u32[]{:S(2)}) collective-permute-start(bf16[2,592,128]{2,1,0:T(8,128)(2,1)S(1)} %fusion), channel_id=1, source_target_pairs={{0,2},{1,5},{2,0},{3,7},{4,6},{5,1},{6,4},{7,3},{8,10},{9,13},{10,... | collective-permute-start | bytes 909320 | tf_op jit(solution)/shard_map/ppermute | solution.py:409
  20.0 2.9 %assemble.6 = (bf16[4,1,592,128]{3,2,1,0:T(8,128)(2,1)S(1)}, bf16[4,1,592,128]{3,2,1,0:T(8,128)(2,1)S(1)}) custom-call(f32[1600,256]{1,0:T(8,128)S(1)} %copy-done.2, s32[16,256]{1,0:T(8,128)S(1)} %copy-done.4, bf16[192,32,128]{2,1,0:T(8,128)(2,1)S(1)} %copy-done), custom_call_target="tpu_custom_call" | custom-call | flops 1000000000 | bytes 4000000 | tf_op jit(solution)/shard_map/assemble/pallas_call | solution.py:321
  22.8 0.0 collective-permute-done.2
  22.8 0.1 fusion.1
  22.9 0.1 collective-permute-start.6
  23.0 0.1 collective-permute-start.11
  23.1 1.7 %collective-permute-done.1 = bf16[2,592,128]{2,1,0:T(8,128)(2,1)S(1)} collective-permute-done((bf16[2,592,128]{2,1,0:T(8,128)(2,1)S(1)}, bf16[2,592,128]{2,1,0:T(8,128)(2,1)S(1)}, u32[]{:S(2)}, u32[]{:S(2)}) %collective-permute-start.1) | collective-permute-done | bytes 303136 | tf_op jit(solution)/shard_map/ppermute | solution.py:409
  24.8 0.1 bitcast_add_fusion.3
  24.9 0.7 %collective-permute-start.8 = (bf16[592,128]{1,0:T(8,128)(2,1)S(1)}, bf16[592,128]{1,0:T(8,128)(2,1)S(1)}, u32[]{:S(2)}, u32[]{:S(2)}) collective-permute-start(bf16[592,128]{1,0:T(8,128)(2,1)S(1)} %fusion.14), channel_id=1, source_target_pairs={{0,4},{1,3},{2,6},{3,1},{4,0},{5,7},{6,2},{7,5},{8,12},{9,11},{10,... | collective-permute-start | bytes 454664 | tf_op jit(solution)/shard_map/ppermute | solution.py:409
  25.6 3.3 %assemble.7 = (bf16[4,1,592,128]{3,2,1,0:T(8,128)(2,1)S(1)}, bf16[4,1,592,128]{3,2,1,0:T(8,128)(2,1)S(1)}) custom-call(f32[1600,256]{1,0:T(8,128)S(1)} %copy-done.2, s32[16,256]{1,0:T(8,128)S(1)} %copy-done.4, bf16[192,32,128]{2,1,0:T(8,128)(2,1)S(1)} %copy-done), custom_call_target="tpu_custom_call" | custom-call | flops 1000000000 | bytes 4000000 | tf_op jit(solution)/shard_map/assemble/pallas_call | solution.py:321
  28.9 2.5 %collective-permute-done.6 = bf16[2,592,128]{2,1,0:T(8,128)(2,1)S(1)} collective-permute-done((bf16[2,592,128]{2,1,0:T(8,128)(2,1)S(1)}, bf16[2,592,128]{2,1,0:T(8,128)(2,1)S(1)}, u32[]{:S(2)}, u32[]{:S(2)}) %collective-permute-start.6) | collective-permute-done | bytes 303136 | tf_op jit(solution)/shard_map/ppermute | solution.py:409
  31.4 0.1 bitcast_add_fusion.1
  31.6 0.2 collective-permute-start.7
  31.8 0.1 fusion.3
  31.9 0.9 %collective-permute-start.12 = (bf16[2,592,128]{2,1,0:T(8,128)(2,1)S(1)}, bf16[2,592,128]{2,1,0:T(8,128)(2,1)S(1)}, u32[]{:S(2)}, u32[]{:S(2)}) collective-permute-start(bf16[2,592,128]{2,1,0:T(8,128)(2,1)S(1)} %fusion.3), channel_id=1, source_target_pairs={{0,2},{1,5},{2,0},{3,7},{4,6},{5,1},{6,4},{7,3},{8,10},{9,13},{10,... | collective-permute-start | bytes 909320 | tf_op jit(solution)/shard_map/ppermute | solution.py:409
  32.8 2.5 %collective-permute-start.9 = (bf16[592,128]{1,0:T(8,128)(2,1)S(1)}, bf16[592,128]{1,0:T(8,128)(2,1)S(1)}, u32[]{:S(2)}, u32[]{:S(2)}) collective-permute-start(bf16[592,128]{1,0:T(8,128)(2,1)S(1)} %fusion.7), channel_id=1, source_target_pairs={{0,8},{8,0},{16,24},{24,16},{1,9},{9,1},{17,25},{25,17},{2,10},{10... | collective-permute-start | bytes 454664 | tf_op jit(solution)/shard_map/ppermute | solution.py:412
  35.3 0.1 fusion.2
  35.4 0.2 collective-permute-start.4
  35.7 2.8 %collective-permute-done.7 = bf16[592,128]{1,0:T(8,128)(2,1)S(1)} collective-permute-done((bf16[592,128]{1,0:T(8,128)(2,1)S(1)}, bf16[592,128]{1,0:T(8,128)(2,1)S(1)}, u32[]{:S(2)}, u32[]{:S(2)}) %collective-permute-start.7) | collective-permute-done | bytes 151584 | tf_op jit(solution)/shard_map/ppermute | solution.py:409
  38.4 1.2 %collective-permute-done.12 = bf16[2,592,128]{2,1,0:T(8,128)(2,1)S(1)} collective-permute-done((bf16[2,592,128]{2,1,0:T(8,128)(2,1)S(1)}, bf16[2,592,128]{2,1,0:T(8,128)(2,1)S(1)}, u32[]{:S(2)}, u32[]{:S(2)}) %collective-permute-start.12) | collective-permute-done | bytes 303136 | tf_op jit(solution)/shard_map/ppermute | solution.py:409
  39.6 0.1 bitcast_add_fusion
  39.7 1.1 %collective-permute-start.13 = (bf16[592,128]{1,0:T(8,128)(2,1)S(1)}, bf16[592,128]{1,0:T(8,128)(2,1)S(1)}, u32[]{:S(2)}, u32[]{:S(2)}) collective-permute-start(bf16[592,128]{1,0:T(8,128)(2,1)S(1)} %fusion.17), channel_id=1, source_target_pairs={{0,4},{1,3},{2,6},{3,1},{4,0},{5,7},{6,2},{7,5},{8,12},{9,11},{10,... | collective-permute-start | bytes 454664 | tf_op jit(solution)/shard_map/ppermute | solution.py:409
  40.8 0.1 fusion.10
  40.9 1.7 %collective-permute-start.10 = (bf16[592,128]{1,0:T(8,128)(2,1)S(1)}, bf16[592,128]{1,0:T(8,128)(2,1)S(1)}, u32[]{:S(2)}, u32[]{:S(2)}) collective-permute-start(bf16[592,128]{1,0:T(8,128)(2,1)S(1)} %fusion.10), channel_id=1, source_target_pairs={{0,16},{8,24},{16,0},{24,8},{1,17},{9,25},{17,1},{25,9},{2,18},{10... | collective-permute-start | bytes 454664 | tf_op jit(solution)/shard_map/ppermute | solution.py:412
  42.6 2.4 %collective-permute-done.13 = bf16[592,128]{1,0:T(8,128)(2,1)S(1)} collective-permute-done((bf16[592,128]{1,0:T(8,128)(2,1)S(1)}, bf16[592,128]{1,0:T(8,128)(2,1)S(1)}, u32[]{:S(2)}, u32[]{:S(2)}) %collective-permute-start.13) | collective-permute-done | bytes 151584 | tf_op jit(solution)/shard_map/ppermute | solution.py:409
  45.0 1.6 %collective-permute-start.14 = (bf16[592,128]{1,0:T(8,128)(2,1)S(1)}, bf16[592,128]{1,0:T(8,128)(2,1)S(1)}, u32[]{:S(2)}, u32[]{:S(2)}) collective-permute-start(bf16[592,128]{1,0:T(8,128)(2,1)S(1)} %fusion.5), channel_id=1, source_target_pairs={{0,8},{8,0},{16,24},{24,16},{1,9},{9,1},{17,25},{25,17},{2,10},{10... | collective-permute-start | bytes 454664 | tf_op jit(solution)/shard_map/ppermute | solution.py:412
  46.7 0.1 bitcast_add_fusion.2
  46.8 1.1 %collective-permute-start.5 = (bf16[592,128]{1,0:T(8,128)(2,1)S(1)}, bf16[592,128]{1,0:T(8,128)(2,1)S(1)}, u32[]{:S(2)}, u32[]{:S(2)}) collective-permute-start(bf16[592,128]{1,0:T(8,128)(2,1)S(1)} %fusion.15), channel_id=1, source_target_pairs={{0,4},{1,3},{2,6},{3,1},{4,0},{5,7},{6,2},{7,5},{8,12},{9,11},{10,... | collective-permute-start | bytes 454664 | tf_op jit(solution)/shard_map/ppermute | solution.py:409
  47.9 2.5 %collective-permute-done.10 = bf16[592,128]{1,0:T(8,128)(2,1)S(1)} collective-permute-done((bf16[592,128]{1,0:T(8,128)(2,1)S(1)}, bf16[592,128]{1,0:T(8,128)(2,1)S(1)}, u32[]{:S(2)}, u32[]{:S(2)}) %collective-permute-start.10) | collective-permute-done | bytes 151584 | tf_op jit(solution)/shard_map/ppermute | solution.py:412
  50.4 2.3 %collective-permute-done.14 = bf16[592,128]{1,0:T(8,128)(2,1)S(1)} collective-permute-done((bf16[592,128]{1,0:T(8,128)(2,1)S(1)}, bf16[592,128]{1,0:T(8,128)(2,1)S(1)}, u32[]{:S(2)}, u32[]{:S(2)}) %collective-permute-start.14) | collective-permute-done | bytes 151584 | tf_op jit(solution)/shard_map/ppermute | solution.py:412
  52.7 0.0 collective-permute-done.5
  52.7 0.1 fusion.18
  52.8 0.1 collective-permute-start.17
  52.9 0.7 %collective-permute-start.16 = (bf16[128,128]{1,0:T(8,128)(2,1)S(1)}, bf16[128,128]{1,0:T(8,128)(2,1)S(1)}, u32[]{:S(2)}, u32[]{:S(2)}) collective-permute-start(bf16[128,128]{1,0:T(8,128)(2,1)S(1)} %get-tuple-element.57), channel_id=1, source_target_pairs={{0,2},{1,3},{2,4},{3,5},{4,6},{5,7},{6,0},{7,1},{8,10},{9,11},{10,... | collective-permute-start | bytes 98312 | tf_op jit(solution)/shard_map/ppermute | solution.py:470
  53.6 1.0 %collective-permute-start.15 = (bf16[128,128]{1,0:T(8,128)(2,1)S(1)}, bf16[128,128]{1,0:T(8,128)(2,1)S(1)}, u32[]{:S(2)}, u32[]{:S(2)}) collective-permute-start(bf16[128,128]{1,0:T(8,128)(2,1)S(1)} %get-tuple-element.58), channel_id=1, source_target_pairs={{0,1},{1,2},{2,3},{3,4},{4,5},{5,6},{6,7},{7,0},{8,9},{9,10},{10,1... | collective-permute-start | bytes 98312 | tf_op jit(solution)/shard_map/ppermute | solution.py:470
  54.5 0.8 %collective-permute-start.18 = (bf16[64,128]{1,0:T(8,128)(2,1)S(1)}, bf16[64,128]{1,0:T(8,128)(2,1)S(1)}, u32[]{:S(2)}, u32[]{:S(2)}) collective-permute-start(bf16[64,128]{1,0:T(8,128)(2,1)S(1)} %slice.143), channel_id=1, source_target_pairs={{0,4},{1,5},{2,6},{3,7},{4,0},{5,1},{6,2},{7,3},{8,12},{9,13},{10,... | collective-permute-start | bytes 49160 | tf_op jit(solution)/shard_map/ppermute | solution.py:470
  55.4 3.1 %collective-permute-done.18.e_ref = bf16[64,128]{1,0:T(8,128)(2,1)S(1)} collective-permute-done((bf16[64,128]{1,0:T(8,128)(2,1)S(1)}, bf16[64,128]{1,0:T(8,128)(2,1)S(1)}, u32[]{:S(2)}, u32[]{:S(2)}) %collective-permute-start.18) | collective-permute-done | bytes 16416 | tf_op jit(solution)/shard_map/ppermute | solution.py:470
  58.5 0.0 collective-permute-done.17.r3_ref
  58.5 0.0 collective-permute-done.16.r2_ref
  58.5 0.9 %finish.1 = (f32[128,1024]{1,0:T(8,128)}, f32[1,128]{1,0:T(1,128)}) custom-call(f32[592,128]{1,0:T(8,128)S(1)} %get-tuple-element.55.own_ref, bf16[128,128]{1,0:T(8,128)(2,1)S(1)} %collective-permute-done.15.r1_ref, bf16[128,128]{1,0:T(8,128)(2,1)S(1)} %collective-permute-done.16.r2_ref, bf16[128,128]{1,0:T(8,128)(2,1)S(1)} %collective-permute-done.17.r3_ref, ...), custom_call_target="tpu_custom_call" | custom-call | tf_op jit(solution)/shard_map/finish/pallas_call | solution.py:375
  (25 shorter events, 0.2 us)
Async XLA Ops:
  0.6 9.2 %copy-start = (bf16[192,32,128]{2,1,0:T(8,128)(2,1)S(1)}, bf16[192,32,128]{2,1,0:T(8,128)(2,1)}, u32[]{:S(2)}) copy-start(bf16[192,32,128]{2,1,0:T(8,128)(2,1)} %g_ref.5) | copy-start | bytes 4718596
  9.4 6.2 %collective-permute-start = (bf16[4,1,592,128]{3,2,0,1:T(8,128)(2,1)}, bf16[4,1,592,128]{3,2,0,1:T(8,128)(2,1)S(1)}, u32[]{:S(2)}, u32[]{:S(2)}) collective-permute-start(bf16[4,1,592,128]{3,2,0,1:T(8,128)(2,1)} %bitcast.81), channel_id=1, source_target_pairs={{0,1},{1,0},{2,3},{3,2},{4,5},{5,4},{6,7},{7,6},{8,9},{9,8},{10,11... | collective-permute-start | bytes 1818632 | tf_op jit(solution)/shard_map/ppermute | solution.py:409
  9.9 1.4 %copy-start.1 = (f32[1600,256]{1,0:T(8,128)S(1)}, f32[1600,256]{1,0:T(8,128)}, u32[]{:S(2)}) copy-start(f32[1600,256]{1,0:T(8,128)} %get-tuple-element.28.shared_ref) | copy-start | bytes 4915204
  11.3 0.7 %copy-start.3 = (s32[16,256]{1,0:T(8,128)S(1)}, s32[16,256]{1,0:T(8,128)}, u32[]{:S(2)}) copy-start(s32[16,256]{1,0:T(8,128)} %get-tuple-element.42.table_ref) | copy-start | bytes 49156
  12.0 3.5 %copy-start.5 = (bf16[4,1,592,128]{3,2,1,0:T(8,128)(2,1)S(1)}, bf16[4,1,592,128]{3,2,1,0:T(8,128)(2,1)}, u32[]{:S(2)}) copy-start(bf16[4,1,592,128]{3,2,1,0:T(8,128)(2,1)} %get-tuple-element.34) | copy-start | bytes 1818628
  12.0 8.0 %copy-start.2 = (f32[1600,256]{1,0:T(8,128)S(1)}, f32[1600,256]{1,0:T(8,128)}, u32[]{:S(2)}) copy-start(f32[1600,256]{1,0:T(8,128)} %get-tuple-element.28.shared_ref) | copy-start | bytes 4915204
  12.0 8.0 %copy-start.4 = (s32[16,256]{1,0:T(8,128)S(1)}, s32[16,256]{1,0:T(8,128)}, u32[]{:S(2)}) copy-start(s32[16,256]{1,0:T(8,128)} %get-tuple-element.42.table_ref) | copy-start | bytes 49156
  15.4 7.5 %collective-permute-start.2 = (bf16[4,1,592,128]{3,2,0,1:T(8,128)(2,1)S(1)}, bf16[4,1,592,128]{3,2,0,1:T(8,128)(2,1)S(1)}, u32[]{:S(2)}, u32[]{:S(2)}) collective-permute-start(bf16[4,1,592,128]{3,2,0,1:T(8,128)(2,1)S(1)} %bitcast.78), channel_id=1, source_target_pairs={{0,1},{1,0},{2,3},{3,2},{4,5},{5,4},{6,7},{7,6},{8,9},{9,8},{10,11... | collective-permute-start | bytes 1818632 | tf_op jit(solution)/shard_map/ppermute | solution.py:409
  15.6 9.2 %collective-permute-start.1 = (bf16[2,592,128]{2,1,0:T(8,128)(2,1)S(1)}, bf16[2,592,128]{2,1,0:T(8,128)(2,1)S(1)}, u32[]{:S(2)}, u32[]{:S(2)}) collective-permute-start(bf16[2,592,128]{2,1,0:T(8,128)(2,1)S(1)} %fusion), channel_id=1, source_target_pairs={{0,2},{1,5},{2,0},{3,7},{4,6},{5,1},{6,4},{7,3},{8,10},{9,13},{10,... | collective-permute-start | bytes 909320 | tf_op jit(solution)/shard_map/ppermute | solution.py:409
  22.9 8.5 %collective-permute-start.6 = (bf16[2,592,128]{2,1,0:T(8,128)(2,1)S(1)}, bf16[2,592,128]{2,1,0:T(8,128)(2,1)S(1)}, u32[]{:S(2)}, u32[]{:S(2)}) collective-permute-start(bf16[2,592,128]{2,1,0:T(8,128)(2,1)S(1)} %fusion.1), channel_id=1, source_target_pairs={{0,2},{1,5},{2,0},{3,7},{4,6},{5,1},{6,4},{7,3},{8,10},{9,13},{10,... | collective-permute-start | bytes 909320 | tf_op jit(solution)/shard_map/ppermute | solution.py:409
  23.0 8.8 %collective-permute-start.11 = (bf16[4,1,592,128]{3,2,0,1:T(8,128)(2,1)S(1)}, bf16[4,1,592,128]{3,2,0,1:T(8,128)(2,1)S(1)}, u32[]{:S(2)}, u32[]{:S(2)}) collective-permute-start(bf16[4,1,592,128]{3,2,0,1:T(8,128)(2,1)S(1)} %bitcast.76), channel_id=1, source_target_pairs={{0,1},{1,0},{2,3},{3,2},{4,5},{5,4},{6,7},{7,6},{8,9},{9,8},{10,11... | collective-permute-start | bytes 1818632 | tf_op jit(solution)/shard_map/ppermute | solution.py:409
  24.9 6.9 %collective-permute-start.8 = (bf16[592,128]{1,0:T(8,128)(2,1)S(1)}, bf16[592,128]{1,0:T(8,128)(2,1)S(1)}, u32[]{:S(2)}, u32[]{:S(2)}) collective-permute-start(bf16[592,128]{1,0:T(8,128)(2,1)S(1)} %fusion.14), channel_id=1, source_target_pairs={{0,4},{1,3},{2,6},{3,1},{4,0},{5,7},{6,2},{7,5},{8,12},{9,11},{10,... | collective-permute-start | bytes 454664 | tf_op jit(solution)/shard_map/ppermute | solution.py:409
  31.4 3.9 %collective-permute-start.3 = (bf16[4,1,592,128]{3,2,0,1:T(8,128)(2,1)S(1)}, bf16[4,1,592,128]{3,2,0,1:T(8,128)(2,1)S(1)}, u32[]{:S(2)}, u32[]{:S(2)}) collective-permute-start(bf16[4,1,592,128]{3,2,0,1:T(8,128)(2,1)S(1)} %bitcast.77), channel_id=1, source_target_pairs={{0,1},{1,0},{2,3},{3,2},{4,5},{5,4},{6,7},{7,6},{8,9},{9,8},{10,11... | collective-permute-start | bytes 1818632 | tf_op jit(solution)/shard_map/ppermute | solution.py:409
  31.6 6.9 %collective-permute-start.7 = (bf16[592,128]{1,0:T(8,128)(2,1)S(1)}, bf16[592,128]{1,0:T(8,128)(2,1)S(1)}, u32[]{:S(2)}, u32[]{:S(2)}) collective-permute-start(bf16[592,128]{1,0:T(8,128)(2,1)S(1)} %fusion.16), channel_id=1, source_target_pairs={{0,4},{1,3},{2,6},{3,1},{4,0},{5,7},{6,2},{7,5},{8,12},{9,11},{10,... | collective-permute-start | bytes 454664 | tf_op jit(solution)/shard_map/ppermute | solution.py:409
  31.9 7.7 %collective-permute-start.12 = (bf16[2,592,128]{2,1,0:T(8,128)(2,1)S(1)}, bf16[2,592,128]{2,1,0:T(8,128)(2,1)S(1)}, u32[]{:S(2)}, u32[]{:S(2)}) collective-permute-start(bf16[2,592,128]{2,1,0:T(8,128)(2,1)S(1)} %fusion.3), channel_id=1, source_target_pairs={{0,2},{1,5},{2,0},{3,7},{4,6},{5,1},{6,4},{7,3},{8,10},{9,13},{10,... | collective-permute-start | bytes 909320 | tf_op jit(solution)/shard_map/ppermute | solution.py:409
  32.8 8.0 %collective-permute-start.9 = (bf16[592,128]{1,0:T(8,128)(2,1)S(1)}, bf16[592,128]{1,0:T(8,128)(2,1)S(1)}, u32[]{:S(2)}, u32[]{:S(2)}) collective-permute-start(bf16[592,128]{1,0:T(8,128)(2,1)S(1)} %fusion.7), channel_id=1, source_target_pairs={{0,8},{8,0},{16,24},{24,16},{1,9},{9,1},{17,25},{25,17},{2,10},{10... | collective-permute-start | bytes 454664 | tf_op jit(solution)/shard_map/ppermute | solution.py:412
  35.4 11.2 %collective-permute-start.4 = (bf16[2,592,128]{2,1,0:T(8,128)(2,1)S(1)}, bf16[2,592,128]{2,1,0:T(8,128)(2,1)S(1)}, u32[]{:S(2)}, u32[]{:S(2)}) collective-permute-start(bf16[2,592,128]{2,1,0:T(8,128)(2,1)S(1)} %fusion.2), channel_id=1, source_target_pairs={{0,2},{1,5},{2,0},{3,7},{4,6},{5,1},{6,4},{7,3},{8,10},{9,13},{10,... | collective-permute-start | bytes 909320 | tf_op jit(solution)/shard_map/ppermute | solution.py:409
  39.7 5.3 %collective-permute-start.13 = (bf16[592,128]{1,0:T(8,128)(2,1)S(1)}, bf16[592,128]{1,0:T(8,128)(2,1)S(1)}, u32[]{:S(2)}, u32[]{:S(2)}) collective-permute-start(bf16[592,128]{1,0:T(8,128)(2,1)S(1)} %fusion.17), channel_id=1, source_target_pairs={{0,4},{1,3},{2,6},{3,1},{4,0},{5,7},{6,2},{7,5},{8,12},{9,11},{10,... | collective-permute-start | bytes 454664 | tf_op jit(solution)/shard_map/ppermute | solution.py:409
  40.9 9.5 %collective-permute-start.10 = (bf16[592,128]{1,0:T(8,128)(2,1)S(1)}, bf16[592,128]{1,0:T(8,128)(2,1)S(1)}, u32[]{:S(2)}, u32[]{:S(2)}) collective-permute-start(bf16[592,128]{1,0:T(8,128)(2,1)S(1)} %fusion.10), channel_id=1, source_target_pairs={{0,16},{8,24},{16,0},{24,8},{1,17},{9,25},{17,1},{25,9},{2,18},{10... | collective-permute-start | bytes 454664 | tf_op jit(solution)/shard_map/ppermute | solution.py:412
  45.0 7.7 %collective-permute-start.14 = (bf16[592,128]{1,0:T(8,128)(2,1)S(1)}, bf16[592,128]{1,0:T(8,128)(2,1)S(1)}, u32[]{:S(2)}, u32[]{:S(2)}) collective-permute-start(bf16[592,128]{1,0:T(8,128)(2,1)S(1)} %fusion.5), channel_id=1, source_target_pairs={{0,8},{8,0},{16,24},{24,16},{1,9},{9,1},{17,25},{25,17},{2,10},{10... | collective-permute-start | bytes 454664 | tf_op jit(solution)/shard_map/ppermute | solution.py:412
  46.8 5.9 %collective-permute-start.5 = (bf16[592,128]{1,0:T(8,128)(2,1)S(1)}, bf16[592,128]{1,0:T(8,128)(2,1)S(1)}, u32[]{:S(2)}, u32[]{:S(2)}) collective-permute-start(bf16[592,128]{1,0:T(8,128)(2,1)S(1)} %fusion.15), channel_id=1, source_target_pairs={{0,4},{1,3},{2,6},{3,1},{4,0},{5,7},{6,2},{7,5},{8,12},{9,11},{10,... | collective-permute-start | bytes 454664 | tf_op jit(solution)/shard_map/ppermute | solution.py:409
  52.8 5.6 %collective-permute-start.17 = (bf16[128,128]{1,0:T(8,128)(2,1)S(1)}, bf16[128,128]{1,0:T(8,128)(2,1)S(1)}, u32[]{:S(2)}, u32[]{:S(2)}) collective-permute-start(bf16[128,128]{1,0:T(8,128)(2,1)S(1)} %get-tuple-element.56), channel_id=1, source_target_pairs={{0,3},{1,4},{2,5},{3,6},{4,7},{5,0},{6,1},{7,2},{8,11},{9,12},{10,... | collective-permute-start | bytes 98312 | tf_op jit(solution)/shard_map/ppermute | solution.py:470
  52.9 5.6 %collective-permute-start.16 = (bf16[128,128]{1,0:T(8,128)(2,1)S(1)}, bf16[128,128]{1,0:T(8,128)(2,1)S(1)}, u32[]{:S(2)}, u32[]{:S(2)}) collective-permute-start(bf16[128,128]{1,0:T(8,128)(2,1)S(1)} %get-tuple-element.57), channel_id=1, source_target_pairs={{0,2},{1,3},{2,4},{3,5},{4,6},{5,7},{6,0},{7,1},{8,10},{9,11},{10,... | collective-permute-start | bytes 98312 | tf_op jit(solution)/shard_map/ppermute | solution.py:470
  53.6 4.9 %collective-permute-start.15 = (bf16[128,128]{1,0:T(8,128)(2,1)S(1)}, bf16[128,128]{1,0:T(8,128)(2,1)S(1)}, u32[]{:S(2)}, u32[]{:S(2)}) collective-permute-start(bf16[128,128]{1,0:T(8,128)(2,1)S(1)} %get-tuple-element.58), channel_id=1, source_target_pairs={{0,1},{1,2},{2,3},{3,4},{4,5},{5,6},{6,7},{7,0},{8,9},{9,10},{10,1... | collective-permute-start | bytes 98312 | tf_op jit(solution)/shard_map/ppermute | solution.py:470
  54.5 3.9 %collective-permute-start.18 = (bf16[64,128]{1,0:T(8,128)(2,1)S(1)}, bf16[64,128]{1,0:T(8,128)(2,1)S(1)}, u32[]{:S(2)}, u32[]{:S(2)}) collective-permute-start(bf16[64,128]{1,0:T(8,128)(2,1)S(1)} %slice.143), channel_id=1, source_target_pairs={{0,4},{1,5},{2,6},{3,7},{4,0},{5,1},{6,2},{7,3},{8,12},{9,13},{10,... | collective-permute-start | bytes 49160 | tf_op jit(solution)/shard_map/ppermute | solution.py:470

commit v5 on v4

--- a/solution.py
+++ b/solution.py
@@ -427,10 +427,9 @@
         return value if other is None else lax.optimization_barrier((value, other))[0]
 
     cores, firsts, seconds = ([None] * regions for _ in range(3))
-    incoming = [[] for _ in range(regions)]
-    own = None
+    crossed, own = [], None
     for slot in range(regions + 3):
-        done, operands = None, []
+        done, operands, ready = None, [], None
         if slot < regions:
             k = regions - 1 - slot
             keep, send, *made = assemble((k,), sub, inputs, global_deriv, blocks, regions)
@@ -440,14 +439,9 @@
             done = both(cores[0], top)[:, 0].astype(BF16)
         k = regions - 1 - (slot - 3)
         if 0 <= k < regions:
-            total = seconds[k][0] + after(seconds[k][1], done).astype(F32)
-            for value in incoming[k]:
-                total = total + value.astype(F32)
-            if k:
-                operands.append(total.astype(BF16))
-                incoming[k - (k & -k)].append(across(operands[-1], k & -k))
-            else:
-                own = total
+            ready = seconds[k][0] + after(seconds[k][1], done).astype(F32)
+            if k == 0:
+                own = ready
         k -= 1
         if 0 <= k < regions:
             total = both(cores[k], low)[:, 0] + after(firsts[k], done).astype(F32)
@@ -459,9 +453,19 @@
                 cores[k] = after(cores[k], done)
             operands.append(both(cores[k], top)[:, 0].astype(BF16))
             firsts[k] = swap(operands[-1], 2, 4)
+        k = regions - 1 - (slot - 3)
+        if 0 < k < regions:
+            value = ready.astype(BF16)
+            if k == 1:
+                value = after(value, operands)
+            operands.append(value)
+            crossed.append(across(value, k))
         if slot < regions:
             inputs = inputs[0], after(inputs[1], (send, operands))
-            cores[k - 1] = near(keep, send)
+            k = regions - 1 - slot
+            cores[k] = near(keep, send)
+    for value in crossed:
+        own = own + value.astype(F32)
 
     def onward(value, d):
         pairs = [

time: 59.7 us -> 61.3 us (1.027)
  starting transfers between devices: 17.8 us -> 24.4 us
  waiting for transfers between devices: 18.4 us -> 13.7 us
    ppermute x3, starting transfers between devices: 5.87 us -> 10.8 us  [across(): lax.ppermute(value.astype(BF16), 'region', [(r, r ^ k) for r in range(reg...]
    ppermute x12, waiting for transfers between devices: 10.5 us -> 6.41 us  [swap(): return lax.ppermute(value, 'tile', pairs)]
    ppermute x4, starting transfers between devices: 2.54 us -> 4.08 us  [onward(): return lax.ppermute(value.astype(BF16), 'tile', pairs)]
  transfers between devices with their start and end apart: 19 -> 19, of which waited for: 8 -> 10; matrix products, arithmetic and copies ran while one was open for 2% -> 2% of each run, Pallas kernels for 16% -> 15%
where the time goes in v5:
time: 61.3 us; the launch traced here: 60.7 us
  starting transfers between devices  24.4 us (40%)
  Pallas kernels  18.7 us (31%)
  waiting for transfers between devices  13.7 us (22%)
  local copies, waits for them, and re-layouts  2.25 us (4%)
  other arithmetic  0.96 us (2%)
  between operations  0.77 us (1%)
    pallas_call x4, Pallas kernels, assemble(): pl.pallas_call(functools.partial(lead_kernel if lead else follow_kernel,...  17.7 us
    ppermute x3, starting transfers between devices, across(): lax.ppermute(value.astype(BF16), 'region', [(r, r ^ k) for r in range(reg...  10.8 us
    ppermute x12, starting transfers between devices, swap(): return lax.ppermute(value, 'tile', pairs)  9.58 us
    ppermute x12, waiting for transfers between devices, swap(): return lax.ppermute(value, 'tile', pairs)  6.41 us
    ppermute x3, waiting for transfers between devices, across(): lax.ppermute(value.astype(BF16), 'region', [(r, r ^ k) for r in range(reg...  4.41 us
    ppermute x4, starting transfers between devices, onward(): return lax.ppermute(value.astype(BF16), 'tile', pairs)  4.08 us
    ppermute x4, waiting for transfers between devices, onward(): return lax.ppermute(value.astype(BF16), 'tile', pairs)  2.86 us
    unnamed x12, local copies, waits for them, and re-layouts  2.16 us
  transfers between devices with their start and end apart: 19, of which 10 were waited for; matrix products, arithmetic and copies ran while one was open for 2% of the time, Pallas kernels for 15%

profile of v5, /device:TPU:0, one launch (start us, length us, event | category | flops | bytes accessed | tf_op | source)
XLA Modules:
  0.0 60.7 jit_solution(8257408056755091827)
XLA Ops:
  0.6 8.7 %assemble.4 = (bf16[4,1,592,128]{3,2,1,0:T(8,128)(2,1)}, bf16[4,1,592,128]{3,2,1,0:T(8,128)(2,1)}, f32[1600,256]{1,0:T(8,128)}, s32[16,256]{1,0:T(8,128)}) custom-call(s32[8]{0:T(128)} %refs_0_.1, s32[1,192]{1,0:T(1,128)} %bitcast.87, s32[1,192]{1,0:T(1,128)} %bitcast.88, bf16[160,192]{1,0:T(8,128)(2,1)} %bitcast.83, bf16[32,192]{1,0:T(8,128)(2,1)} %bitcast.85, ...), custom_call_target="tpu_custom_call" | custom-call | flops 1000000000 | bytes 4000000 | tf_op jit(solution)/shard_map/assemble/pallas_call | solution.py:321
  9.3 0.5 collective-permute-start
  9.9 1.4 %copy-done.1 = f32[1600,256]{1,0:T(8,128)S(1)} copy-done((f32[1600,256]{1,0:T(8,128)S(1)}, f32[1600,256]{1,0:T(8,128)}, u32[]{:S(2)}) %copy-start.1) | copy-done | bytes 1638424
  11.3 0.7 %copy-done.3 = s32[16,256]{1,0:T(8,128)S(1)} copy-done((s32[16,256]{1,0:T(8,128)S(1)}, s32[16,256]{1,0:T(8,128)}, u32[]{:S(2)}) %copy-start.3) | copy-done | bytes 16408
  12.0 2.9 %assemble.5 = (bf16[4,1,592,128]{3,2,1,0:T(8,128)(2,1)S(1)}, bf16[4,1,592,128]{3,2,1,0:T(8,128)(2,1)S(1)}) custom-call(f32[1600,256]{1,0:T(8,128)S(1)} %copy-done.1, s32[16,256]{1,0:T(8,128)S(1)} %copy-done.3, bf16[192,32,128]{2,1,0:T(8,128)(2,1)S(1)} %copy-done), custom_call_target="tpu_custom_call" | custom-call | flops 1000000000 | bytes 4000000 | tf_op jit(solution)/shard_map/assemble/pallas_call | solution.py:321
  14.9 1.9 %collective-permute-start.2 = (bf16[4,1,592,128]{3,2,0,1:T(8,128)(2,1)S(1)}, bf16[4,1,592,128]{3,2,0,1:T(8,128)(2,1)S(1)}, u32[]{:S(2)}, u32[]{:S(2)}) collective-permute-start(bf16[4,1,592,128]{3,2,0,1:T(8,128)(2,1)S(1)} %bitcast.78), channel_id=1, source_target_pairs={{0,1},{1,0},{2,3},{3,2},{4,5},{5,4},{6,7},{7,6},{8,9},{9,8},{10,11... | collective-permute-start | bytes 1818632 | tf_op jit(solution)/shard_map/ppermute | solution.py:409
  16.8 0.0 collective-permute-done
  16.8 0.1 fusion
  16.9 1.2 %collective-permute-start.1 = (bf16[2,592,128]{2,1,0:T(8,128)(2,1)S(1)}, bf16[2,592,128]{2,1,0:T(8,128)(2,1)S(1)}, u32[]{:S(2)}, u32[]{:S(2)}) collective-permute-start(bf16[2,592,128]{2,1,0:T(8,128)(2,1)S(1)} %fusion), channel_id=1, source_target_pairs={{0,2},{1,5},{2,0},{3,7},{4,6},{5,1},{6,4},{7,3},{8,10},{9,13},{10,... | collective-permute-start | bytes 909320 | tf_op jit(solution)/shard_map/ppermute | solution.py:409
  18.1 3.3 %assemble.6 = (bf16[4,1,592,128]{3,2,1,0:T(8,128)(2,1)S(1)}, bf16[4,1,592,128]{3,2,1,0:T(8,128)(2,1)S(1)}) custom-call(f32[1600,256]{1,0:T(8,128)S(1)} %copy-done.2, s32[16,256]{1,0:T(8,128)S(1)} %copy-done.4, bf16[192,32,128]{2,1,0:T(8,128)(2,1)S(1)} %copy-done), custom_call_target="tpu_custom_call" | custom-call | flops 1000000000 | bytes 4000000 | tf_op jit(solution)/shard_map/assemble/pallas_call | solution.py:321
  21.5 0.0 collective-permute-done.2
  21.5 0.1 fusion.1
  21.6 0.5 collective-permute-start.8
  22.1 1.8 %collective-permute-done.1 = bf16[2,592,128]{2,1,0:T(8,128)(2,1)S(1)} collective-permute-done((bf16[2,592,128]{2,1,0:T(8,128)(2,1)S(1)}, bf16[2,592,128]{2,1,0:T(8,128)(2,1)S(1)}, u32[]{:S(2)}, u32[]{:S(2)}) %collective-permute-start.1) | collective-permute-done | bytes 303136 | tf_op jit(solution)/shard_map/ppermute | solution.py:409
  23.8 0.1 bitcast_add_fusion.3
  23.9 1.7 %collective-permute-start.6 = (bf16[592,128]{1,0:T(8,128)(2,1)S(1)}, bf16[592,128]{1,0:T(8,128)(2,1)S(1)}, u32[]{:S(2)}, u32[]{:S(2)}) collective-permute-start(bf16[592,128]{1,0:T(8,128)(2,1)S(1)} %fusion.14), channel_id=1, source_target_pairs={{0,4},{1,3},{2,6},{3,1},{4,0},{5,7},{6,2},{7,5},{8,12},{9,11},{10,... | collective-permute-start | bytes 454664 | tf_op jit(solution)/shard_map/ppermute | solution.py:409
  25.6 2.9 %assemble.7 = (bf16[4,1,592,128]{3,2,1,0:T(8,128)(2,1)S(1)}, bf16[4,1,592,128]{3,2,1,0:T(8,128)(2,1)S(1)}) custom-call(f32[1600,256]{1,0:T(8,128)S(1)} %copy-done.2, s32[16,256]{1,0:T(8,128)S(1)} %copy-done.4, bf16[192,32,128]{2,1,0:T(8,128)(2,1)S(1)} %copy-done), custom_call_target="tpu_custom_call" | custom-call | flops 1000000000 | bytes 4000000 | tf_op jit(solution)/shard_map/assemble/pallas_call | solution.py:321
  28.5 1.6 %collective-permute-done.8 = bf16[2,592,128]{2,1,0:T(8,128)(2,1)S(1)} collective-permute-done((bf16[2,592,128]{2,1,0:T(8,128)(2,1)S(1)}, bf16[2,592,128]{2,1,0:T(8,128)(2,1)S(1)}, u32[]{:S(2)}, u32[]{:S(2)}) %collective-permute-start.8) | collective-permute-done | bytes 303136 | tf_op jit(solution)/shard_map/ppermute | solution.py:409
  30.1 0.1 bitcast_add_fusion.1
  30.2 1.2 %collective-permute-start.9 = (bf16[592,128]{1,0:T(8,128)(2,1)S(1)}, bf16[592,128]{1,0:T(8,128)(2,1)S(1)}, u32[]{:S(2)}, u32[]{:S(2)}) collective-permute-start(bf16[592,128]{1,0:T(8,128)(2,1)S(1)} %fusion.16), channel_id=1, source_target_pairs={{0,4},{1,3},{2,6},{3,1},{4,0},{5,7},{6,2},{7,5},{8,12},{9,11},{10,... | collective-permute-start | bytes 454664 | tf_op jit(solution)/shard_map/ppermute | solution.py:409
  31.3 0.0 collective-permute-done.6
  31.3 0.0 collective-permute-done.11
  31.3 0.1 fusion.3
  31.4 0.9 %collective-permute-start.12 = (bf16[2,592,128]{2,1,0:T(8,128)(2,1)S(1)}, bf16[2,592,128]{2,1,0:T(8,128)(2,1)S(1)}, u32[]{:S(2)}, u32[]{:S(2)}) collective-permute-start(bf16[2,592,128]{2,1,0:T(8,128)(2,1)S(1)} %fusion.3), channel_id=1, source_target_pairs={{0,2},{1,5},{2,0},{3,7},{4,6},{5,1},{6,4},{7,3},{8,10},{9,13},{10,... | collective-permute-start | bytes 909320 | tf_op jit(solution)/shard_map/ppermute | solution.py:409
  32.4 3.6 %collective-permute-start.7 = (bf16[592,128]{1,0:T(8,128)(2,1)S(1)}, bf16[592,128]{1,0:T(8,128)(2,1)S(1)}, u32[]{:S(2)}, u32[]{:S(2)}) collective-permute-start(bf16[592,128]{1,0:T(8,128)(2,1)S(1)} %fusion.9), channel_id=1, source_target_pairs={{0,24},{8,16},{16,8},{24,0},{1,25},{9,17},{17,9},{25,1},{2,26},{10... | collective-permute-start | bytes 454664 | tf_op jit(solution)/shard_map/ppermute | solution.py:412
  36.0 0.1 fusion.2
  36.1 0.1 collective-permute-start.4
  36.2 0.1 collective-permute-done.9
  36.3 2.0 %collective-permute-done.12 = bf16[2,592,128]{2,1,0:T(8,128)(2,1)S(1)} collective-permute-done((bf16[2,592,128]{2,1,0:T(8,128)(2,1)S(1)}, bf16[2,592,128]{2,1,0:T(8,128)(2,1)S(1)}, u32[]{:S(2)}, u32[]{:S(2)}) %collective-permute-start.12) | collective-permute-done | bytes 303136 | tf_op jit(solution)/shard_map/ppermute | solution.py:409
  38.3 0.1 bitcast_add_fusion
  38.4 1.1 %collective-permute-start.13 = (bf16[592,128]{1,0:T(8,128)(2,1)S(1)}, bf16[592,128]{1,0:T(8,128)(2,1)S(1)}, u32[]{:S(2)}, u32[]{:S(2)}) collective-permute-start(bf16[592,128]{1,0:T(8,128)(2,1)S(1)} %fusion.17), channel_id=1, source_target_pairs={{0,4},{1,3},{2,6},{3,1},{4,0},{5,7},{6,2},{7,5},{8,12},{9,11},{10,... | collective-permute-start | bytes 454664 | tf_op jit(solution)/shard_map/ppermute | solution.py:409
  39.6 3.8 %collective-permute-start.10 = (bf16[592,128]{1,0:T(8,128)(2,1)S(1)}, bf16[592,128]{1,0:T(8,128)(2,1)S(1)}, u32[]{:S(2)}, u32[]{:S(2)}) collective-permute-start(bf16[592,128]{1,0:T(8,128)(2,1)S(1)} %fusion.7), channel_id=1, source_target_pairs={{0,16},{8,24},{16,0},{24,8},{1,17},{9,25},{17,1},{25,9},{2,18},{10... | collective-permute-start | bytes 454664 | tf_op jit(solution)/shard_map/ppermute | solution.py:412
  43.3 0.4 collective-permute-done.13
  43.7 0.6 collective-permute-done.4
  44.3 0.1 bitcast_add_fusion.2
  44.4 0.5 collective-permute-start.5
  45.0 3.4 %collective-permute-start.14 = (bf16[592,128]{1,0:T(8,128)(2,1)S(1)}, bf16[592,128]{1,0:T(8,128)(2,1)S(1)}, u32[]{:S(2)}, u32[]{:S(2)}) collective-permute-start(bf16[592,128]{1,0:T(8,128)(2,1)S(1)} %fusion.5), channel_id=1, source_target_pairs={{0,8},{8,0},{16,24},{24,16},{1,9},{9,1},{17,25},{25,17},{2,10},{10... | collective-permute-start | bytes 454664 | tf_op jit(solution)/shard_map/ppermute | solution.py:412
  48.3 2.0 %collective-permute-done.10 = bf16[592,128]{1,0:T(8,128)(2,1)S(1)} collective-permute-done((bf16[592,128]{1,0:T(8,128)(2,1)S(1)}, bf16[592,128]{1,0:T(8,128)(2,1)S(1)}, u32[]{:S(2)}, u32[]{:S(2)}) %collective-permute-start.10) | collective-permute-done | bytes 151584 | tf_op jit(solution)/shard_map/ppermute | solution.py:412
  50.3 2.4 %collective-permute-done.14 = bf16[592,128]{1,0:T(8,128)(2,1)S(1)} collective-permute-done((bf16[592,128]{1,0:T(8,128)(2,1)S(1)}, bf16[592,128]{1,0:T(8,128)(2,1)S(1)}, u32[]{:S(2)}, u32[]{:S(2)}) %collective-permute-start.14) | collective-permute-done | bytes 151584 | tf_op jit(solution)/shard_map/ppermute | solution.py:412
  52.7 0.1 fusion.18
  52.9 1.8 %collective-permute-start.17 = (bf16[128,128]{1,0:T(8,128)(2,1)S(1)}, bf16[128,128]{1,0:T(8,128)(2,1)S(1)}, u32[]{:S(2)}, u32[]{:S(2)}) collective-permute-start(bf16[128,128]{1,0:T(8,128)(2,1)S(1)} %get-tuple-element.58), channel_id=1, source_target_pairs={{0,3},{1,4},{2,5},{3,6},{4,7},{5,0},{6,1},{7,2},{8,11},{9,12},{10,... | collective-permute-start | bytes 98312 | tf_op jit(solution)/shard_map/ppermute | solution.py:474
  54.6 0.5 collective-permute-start.16
  55.1 0.0 collective-permute-start.15
  55.1 1.8 %collective-permute-start.18 = (bf16[64,128]{1,0:T(8,128)(2,1)S(1)}, bf16[64,128]{1,0:T(8,128)(2,1)S(1)}, u32[]{:S(2)}, u32[]{:S(2)}) collective-permute-start(bf16[64,128]{1,0:T(8,128)(2,1)S(1)} %slice.143), channel_id=1, source_target_pairs={{0,4},{1,5},{2,6},{3,7},{4,0},{5,1},{6,2},{7,3},{8,12},{9,13},{10,... | collective-permute-start | bytes 49160 | tf_op jit(solution)/shard_map/ppermute | solution.py:474
  56.9 1.9 %collective-permute-done.18.e_ref = bf16[64,128]{1,0:T(8,128)(2,1)S(1)} collective-permute-done((bf16[64,128]{1,0:T(8,128)(2,1)S(1)}, bf16[64,128]{1,0:T(8,128)(2,1)S(1)}, u32[]{:S(2)}, u32[]{:S(2)}) %collective-permute-start.18) | collective-permute-done | bytes 16416 | tf_op jit(solution)/shard_map/ppermute | solution.py:474
  58.9 0.9 %collective-permute-done.16.r2_ref = bf16[128,128]{1,0:T(8,128)(2,1)S(1)} collective-permute-done((bf16[128,128]{1,0:T(8,128)(2,1)S(1)}, bf16[128,128]{1,0:T(8,128)(2,1)S(1)}, u32[]{:S(2)}, u32[]{:S(2)}) %collective-permute-start.16) | collective-permute-done | bytes 32800 | tf_op jit(solution)/shard_map/ppermute | solution.py:474
  59.8 0.0 collective-permute-done.15.r1_ref
  59.8 0.9 %finish.1 = (f32[128,1024]{1,0:T(8,128)}, f32[1,128]{1,0:T(1,128)}) custom-call(f32[592,128]{1,0:T(8,128)S(1)} %get-tuple-element.57.own_ref, bf16[128,128]{1,0:T(8,128)(2,1)S(1)} %collective-permute-done.15.r1_ref, bf16[128,128]{1,0:T(8,128)(2,1)S(1)} %collective-permute-done.16.r2_ref, bf16[128,128]{1,0:T(8,128)(2,1)S(1)} %collective-permute-done.17.r3_ref, ...), custom_call_target="tpu_custom_call" | custom-call | tf_op jit(solution)/shard_map/finish/pallas_call | solution.py:375
  (25 shorter events, 0.2 us)
Async XLA Ops:
  0.6 9.2 %copy-start = (bf16[192,32,128]{2,1,0:T(8,128)(2,1)S(1)}, bf16[192,32,128]{2,1,0:T(8,128)(2,1)}, u32[]{:S(2)}) copy-start(bf16[192,32,128]{2,1,0:T(8,128)(2,1)} %g_ref.5) | copy-start | bytes 4718596
  9.3 7.5 %collective-permute-start = (bf16[4,1,592,128]{3,2,0,1:T(8,128)(2,1)}, bf16[4,1,592,128]{3,2,0,1:T(8,128)(2,1)S(1)}, u32[]{:S(2)}, u32[]{:S(2)}) collective-permute-start(bf16[4,1,592,128]{3,2,0,1:T(8,128)(2,1)} %bitcast.81), channel_id=1, source_target_pairs={{0,1},{1,0},{2,3},{3,2},{4,5},{5,4},{6,7},{7,6},{8,9},{9,8},{10,11... | collective-permute-start | bytes 1818632 | tf_op jit(solution)/shard_map/ppermute | solution.py:409
  9.9 1.4 %copy-start.1 = (f32[1600,256]{1,0:T(8,128)S(1)}, f32[1600,256]{1,0:T(8,128)}, u32[]{:S(2)}) copy-start(f32[1600,256]{1,0:T(8,128)} %get-tuple-element.29.shared_ref) | copy-start | bytes 4915204
  11.3 0.7 %copy-start.3 = (s32[16,256]{1,0:T(8,128)S(1)}, s32[16,256]{1,0:T(8,128)}, u32[]{:S(2)}) copy-start(s32[16,256]{1,0:T(8,128)} %get-tuple-element.43.table_ref) | copy-start | bytes 49156
  12.0 4.8 %copy-start.5 = (bf16[4,1,592,128]{3,2,1,0:T(8,128)(2,1)S(1)}, bf16[4,1,592,128]{3,2,1,0:T(8,128)(2,1)}, u32[]{:S(2)}) copy-start(bf16[4,1,592,128]{3,2,1,0:T(8,128)(2,1)} %get-tuple-element.35) | copy-start | bytes 1818628
  12.0 6.1 %copy-start.2 = (f32[1600,256]{1,0:T(8,128)S(1)}, f32[1600,256]{1,0:T(8,128)}, u32[]{:S(2)}) copy-start(f32[1600,256]{1,0:T(8,128)} %get-tuple-element.29.shared_ref) | copy-start | bytes 4915204
  12.0 6.1 %copy-start.4 = (s32[16,256]{1,0:T(8,128)S(1)}, s32[16,256]{1,0:T(8,128)}, u32[]{:S(2)}) copy-start(s32[16,256]{1,0:T(8,128)} %get-tuple-element.43.table_ref) | copy-start | bytes 49156
  14.9 6.6 %collective-permute-start.2 = (bf16[4,1,592,128]{3,2,0,1:T(8,128)(2,1)S(1)}, bf16[4,1,592,128]{3,2,0,1:T(8,128)(2,1)S(1)}, u32[]{:S(2)}, u32[]{:S(2)}) collective-permute-start(bf16[4,1,592,128]{3,2,0,1:T(8,128)(2,1)S(1)} %bitcast.78), channel_id=1, source_target_pairs={{0,1},{1,0},{2,3},{3,2},{4,5},{5,4},{6,7},{7,6},{8,9},{9,8},{10,11... | collective-permute-start | bytes 1818632 | tf_op jit(solution)/shard_map/ppermute | solution.py:409
  16.9 6.9 %collective-permute-start.1 = (bf16[2,592,128]{2,1,0:T(8,128)(2,1)S(1)}, bf16[2,592,128]{2,1,0:T(8,128)(2,1)S(1)}, u32[]{:S(2)}, u32[]{:S(2)}) collective-permute-start(bf16[2,592,128]{2,1,0:T(8,128)(2,1)S(1)} %fusion), channel_id=1, source_target_pairs={{0,2},{1,5},{2,0},{3,7},{4,6},{5,1},{6,4},{7,3},{8,10},{9,13},{10,... | collective-permute-start | bytes 909320 | tf_op jit(solution)/shard_map/ppermute | solution.py:409
  21.6 8.5 %collective-permute-start.8 = (bf16[2,592,128]{2,1,0:T(8,128)(2,1)S(1)}, bf16[2,592,128]{2,1,0:T(8,128)(2,1)S(1)}, u32[]{:S(2)}, u32[]{:S(2)}) collective-permute-start(bf16[2,592,128]{2,1,0:T(8,128)(2,1)S(1)} %fusion.1), channel_id=1, source_target_pairs={{0,2},{1,5},{2,0},{3,7},{4,6},{5,1},{6,4},{7,3},{8,10},{9,13},{10,... | collective-permute-start | bytes 909320 | tf_op jit(solution)/shard_map/ppermute | solution.py:409
  22.1 9.3 %collective-permute-start.11 = (bf16[4,1,592,128]{3,2,0,1:T(8,128)(2,1)S(1)}, bf16[4,1,592,128]{3,2,0,1:T(8,128)(2,1)S(1)}, u32[]{:S(2)}, u32[]{:S(2)}) collective-permute-start(bf16[4,1,592,128]{3,2,0,1:T(8,128)(2,1)S(1)} %bitcast.76), channel_id=1, source_target_pairs={{0,1},{1,0},{2,3},{3,2},{4,5},{5,4},{6,7},{7,6},{8,9},{9,8},{10,11... | collective-permute-start | bytes 1818632 | tf_op jit(solution)/shard_map/ppermute | solution.py:409
  23.9 7.4 %collective-permute-start.6 = (bf16[592,128]{1,0:T(8,128)(2,1)S(1)}, bf16[592,128]{1,0:T(8,128)(2,1)S(1)}, u32[]{:S(2)}, u32[]{:S(2)}) collective-permute-start(bf16[592,128]{1,0:T(8,128)(2,1)S(1)} %fusion.14), channel_id=1, source_target_pairs={{0,4},{1,3},{2,6},{3,1},{4,0},{5,7},{6,2},{7,5},{8,12},{9,11},{10,... | collective-permute-start | bytes 454664 | tf_op jit(solution)/shard_map/ppermute | solution.py:409
  30.1 6.0 %collective-permute-start.3 = (bf16[4,1,592,128]{3,2,0,1:T(8,128)(2,1)S(1)}, bf16[4,1,592,128]{3,2,0,1:T(8,128)(2,1)S(1)}, u32[]{:S(2)}, u32[]{:S(2)}) collective-permute-start(bf16[4,1,592,128]{3,2,0,1:T(8,128)(2,1)S(1)} %bitcast.77), channel_id=1, source_target_pairs={{0,1},{1,0},{2,3},{3,2},{4,5},{5,4},{6,7},{7,6},{8,9},{9,8},{10,11... | collective-permute-start | bytes 1818632 | tf_op jit(solution)/shard_map/ppermute | solution.py:409
  30.2 6.1 %collective-permute-start.9 = (bf16[592,128]{1,0:T(8,128)(2,1)S(1)}, bf16[592,128]{1,0:T(8,128)(2,1)S(1)}, u32[]{:S(2)}, u32[]{:S(2)}) collective-permute-start(bf16[592,128]{1,0:T(8,128)(2,1)S(1)} %fusion.16), channel_id=1, source_target_pairs={{0,4},{1,3},{2,6},{3,1},{4,0},{5,7},{6,2},{7,5},{8,12},{9,11},{10,... | collective-permute-start | bytes 454664 | tf_op jit(solution)/shard_map/ppermute | solution.py:409
  31.4 6.9 %collective-permute-start.12 = (bf16[2,592,128]{2,1,0:T(8,128)(2,1)S(1)}, bf16[2,592,128]{2,1,0:T(8,128)(2,1)S(1)}, u32[]{:S(2)}, u32[]{:S(2)}) collective-permute-start(bf16[2,592,128]{2,1,0:T(8,128)(2,1)S(1)} %fusion.3), channel_id=1, source_target_pairs={{0,2},{1,5},{2,0},{3,7},{4,6},{5,1},{6,4},{7,3},{8,10},{9,13},{10,... | collective-permute-start | bytes 909320 | tf_op jit(solution)/shard_map/ppermute | solution.py:409
  32.4 15.9 %collective-permute-start.7 = (bf16[592,128]{1,0:T(8,128)(2,1)S(1)}, bf16[592,128]{1,0:T(8,128)(2,1)S(1)}, u32[]{:S(2)}, u32[]{:S(2)}) collective-permute-start(bf16[592,128]{1,0:T(8,128)(2,1)S(1)} %fusion.9), channel_id=1, source_target_pairs={{0,24},{8,16},{16,8},{24,0},{1,25},{9,17},{17,9},{25,1},{2,26},{10... | collective-permute-start | bytes 454664 | tf_op jit(solution)/shard_map/ppermute | solution.py:412
  36.1 8.2 %collective-permute-start.4 = (bf16[2,592,128]{2,1,0:T(8,128)(2,1)S(1)}, bf16[2,592,128]{2,1,0:T(8,128)(2,1)S(1)}, u32[]{:S(2)}, u32[]{:S(2)}) collective-permute-start(bf16[2,592,128]{2,1,0:T(8,128)(2,1)S(1)} %fusion.2), channel_id=1, source_target_pairs={{0,2},{1,5},{2,0},{3,7},{4,6},{5,1},{6,4},{7,3},{8,10},{9,13},{10,... | collective-permute-start | bytes 909320 | tf_op jit(solution)/shard_map/ppermute | solution.py:409
  38.4 5.3 %collective-permute-start.13 = (bf16[592,128]{1,0:T(8,128)(2,1)S(1)}, bf16[592,128]{1,0:T(8,128)(2,1)S(1)}, u32[]{:S(2)}, u32[]{:S(2)}) collective-permute-start(bf16[592,128]{1,0:T(8,128)(2,1)S(1)} %fusion.17), channel_id=1, source_target_pairs={{0,4},{1,3},{2,6},{3,1},{4,0},{5,7},{6,2},{7,5},{8,12},{9,11},{10,... | collective-permute-start | bytes 454664 | tf_op jit(solution)/shard_map/ppermute | solution.py:409
  39.6 10.8 %collective-permute-start.10 = (bf16[592,128]{1,0:T(8,128)(2,1)S(1)}, bf16[592,128]{1,0:T(8,128)(2,1)S(1)}, u32[]{:S(2)}, u32[]{:S(2)}) collective-permute-start(bf16[592,128]{1,0:T(8,128)(2,1)S(1)} %fusion.7), channel_id=1, source_target_pairs={{0,16},{8,24},{16,0},{24,8},{1,17},{9,25},{17,1},{25,9},{2,18},{10... | collective-permute-start | bytes 454664 | tf_op jit(solution)/shard_map/ppermute | solution.py:412
  44.4 5.9 %collective-permute-start.5 = (bf16[592,128]{1,0:T(8,128)(2,1)S(1)}, bf16[592,128]{1,0:T(8,128)(2,1)S(1)}, u32[]{:S(2)}, u32[]{:S(2)}) collective-permute-start(bf16[592,128]{1,0:T(8,128)(2,1)S(1)} %fusion.15), channel_id=1, source_target_pairs={{0,4},{1,3},{2,6},{3,1},{4,0},{5,7},{6,2},{7,5},{8,12},{9,11},{10,... | collective-permute-start | bytes 454664 | tf_op jit(solution)/shard_map/ppermute | solution.py:409
  45.0 7.8 %collective-permute-start.14 = (bf16[592,128]{1,0:T(8,128)(2,1)S(1)}, bf16[592,128]{1,0:T(8,128)(2,1)S(1)}, u32[]{:S(2)}, u32[]{:S(2)}) collective-permute-start(bf16[592,128]{1,0:T(8,128)(2,1)S(1)} %fusion.5), channel_id=1, source_target_pairs={{0,8},{8,0},{16,24},{24,16},{1,9},{9,1},{17,25},{25,17},{2,10},{10... | collective-permute-start | bytes 454664 | tf_op jit(solution)/shard_map/ppermute | solution.py:412
  52.9 6.0 %collective-permute-start.17 = (bf16[128,128]{1,0:T(8,128)(2,1)S(1)}, bf16[128,128]{1,0:T(8,128)(2,1)S(1)}, u32[]{:S(2)}, u32[]{:S(2)}) collective-permute-start(bf16[128,128]{1,0:T(8,128)(2,1)S(1)} %get-tuple-element.58), channel_id=1, source_target_pairs={{0,3},{1,4},{2,5},{3,6},{4,7},{5,0},{6,1},{7,2},{8,11},{9,12},{10,... | collective-permute-start | bytes 98312 | tf_op jit(solution)/shard_map/ppermute | solution.py:474
  54.6 5.2 %collective-permute-start.16 = (bf16[128,128]{1,0:T(8,128)(2,1)S(1)}, bf16[128,128]{1,0:T(8,128)(2,1)S(1)}, u32[]{:S(2)}, u32[]{:S(2)}) collective-permute-start(bf16[128,128]{1,0:T(8,128)(2,1)S(1)} %get-tuple-element.59), channel_id=1, source_target_pairs={{0,2},{1,3},{2,4},{3,5},{4,6},{5,7},{6,0},{7,1},{8,10},{9,11},{10,... | collective-permute-start | bytes 98312 | tf_op jit(solution)/shard_map/ppermute | solution.py:474
  55.1 4.7 %collective-permute-start.15 = (bf16[128,128]{1,0:T(8,128)(2,1)S(1)}, bf16[128,128]{1,0:T(8,128)(2,1)S(1)}, u32[]{:S(2)}, u32[]{:S(2)}) collective-permute-start(bf16[128,128]{1,0:T(8,128)(2,1)S(1)} %get-tuple-element.60), channel_id=1, source_target_pairs={{0,1},{1,2},{2,3},{3,4},{4,5},{5,6},{6,7},{7,0},{8,9},{9,10},{10,1... | collective-permute-start | bytes 98312 | tf_op jit(solution)/shard_map/ppermute | solution.py:474
  55.1 3.7 %collective-permute-start.18 = (bf16[64,128]{1,0:T(8,128)(2,1)S(1)}, bf16[64,128]{1,0:T(8,128)(2,1)S(1)}, u32[]{:S(2)}, u32[]{:S(2)}) collective-permute-start(bf16[64,128]{1,0:T(8,128)(2,1)S(1)} %slice.143), channel_id=1, source_target_pairs={{0,4},{1,5},{2,6},{3,7},{4,0},{5,1},{6,2},{7,3},{8,12},{9,13},{10,... | collective-permute-start | bytes 49160 | tf_op jit(solution)/shard_map/ppermute | solution.py:474

commit v6 on v5

--- a/solution.py
+++ b/solution.py
@@ -437,6 +437,9 @@
             done = send
         elif slot == regions:
             done = both(cores[0], top)[:, 0].astype(BF16)
+            value = after(waiting[0], done)
+            crossed.append(across(value, waiting[1]))
+            done = done, value
         k = regions - 1 - (slot - 3)
         if 0 <= k < regions:
             ready = seconds[k][0] + after(seconds[k][1], done).astype(F32)
@@ -455,11 +458,11 @@
             firsts[k] = swap(operands[-1], 2, 4)
         k = regions - 1 - (slot - 3)
         if 0 < k < regions:
-            value = ready.astype(BF16)
-            if k == 1:
-                value = after(value, operands)
-            operands.append(value)
-            crossed.append(across(value, k))
+            if slot == regions - 1:
+                waiting = ready.astype(BF16), k
+            else:
+                operands.append(ready.astype(BF16))
+                crossed.append(across(operands[-1], k))
         if slot < regions:
             inputs = inputs[0], after(inputs[1], (send, operands))
             k = regions - 1 - slot

time: 61.3 us -> 60.3 us (0.984)
  starting transfers between devices: 24.4 us -> 21.2 us
  waiting for transfers between devices: 13.7 us -> 15.1 us
  Pallas kernels: 18.7 us -> 19.6 us
    ppermute x3, starting transfers between devices: 10.8 us -> 6.34 us  [across(): lax.ppermute(value.astype(BF16), 'region', [(r, r ^ k) for r in range(reg...]
    ppermute x12, starting transfers between devices: 9.58 us -> 11.8 us  [swap(): return lax.ppermute(value, 'tile', pairs)]
    pallas_call x4, Pallas kernels: 17.7 us -> 18.7 us  [assemble(): pl.pallas_call(functools.partial(lead_kernel if lead else follow_kernel,...]
    ppermute x4, starting transfers between devices: 4.08 us -> 3.13 us  [onward(): return lax.ppermute(value.astype(BF16), 'tile', pairs)]
    ppermute x12, waiting for transfers between devices: 6.41 us -> 7.22 us  [swap(): return lax.ppermute(value, 'tile', pairs)]
  transfers between devices with their start and end apart: 19 -> 19, of which waited for: 10 -> 7; matrix products, arithmetic and copies ran while one was open for 2% -> 2% of each run, Pallas kernels for 15% -> 18%
where the time goes in v6:
time: 60.3 us; the launch traced here: 59.9 us
  starting transfers between devices  21.2 us (35%)
  Pallas kernels  19.6 us (33%)
  waiting for transfers between devices  15.1 us (25%)
  local copies, waits for them, and re-layouts  2.24 us (4%)
  other arithmetic  0.96 us (2%)
  between operations  0.82 us (1%)
    pallas_call x4, Pallas kernels, assemble(): pl.pallas_call(functools.partial(lead_kernel if lead else follow_kernel,...  18.7 us
    ppermute x12, starting transfers between devices, swap(): return lax.ppermute(value, 'tile', pairs)  11.8 us
    ppermute x12, waiting for transfers between devices, swap(): return lax.ppermute(value, 'tile', pairs)  7.22 us
    ppermute x3, starting transfers between devices, across(): lax.ppermute(value.astype(BF16), 'region', [(r, r ^ k) for r in range(reg...  6.34 us
    ppermute x3, waiting for transfers between devices, across(): lax.ppermute(value.astype(BF16), 'region', [(r, r ^ k) for r in range(reg...  5 us
    ppermute x4, starting transfers between devices, onward(): return lax.ppermute(value.astype(BF16), 'tile', pairs)  3.13 us
    ppermute x4, waiting for transfers between devices, onward(): return lax.ppermute(value.astype(BF16), 'tile', pairs)  2.85 us
    unnamed x12, local copies, waits for them, and re-layouts  2.16 us
  transfers between devices with their start and end apart: 19, of which 7 were waited for; matrix products, arithmetic and copies ran while one was open for 2% of the time, Pallas kernels for 18%

profile of v6, /device:TPU:0, one launch (start us, length us, event | category | flops | bytes accessed | tf_op | source)
XLA Modules:
  0.0 59.9 jit_solution(746290281859222607)
XLA Ops:
  0.6 7.8 %assemble.4 = (bf16[4,1,592,128]{3,2,1,0:T(8,128)(2,1)}, bf16[4,1,592,128]{3,2,1,0:T(8,128)(2,1)}, f32[1600,256]{1,0:T(8,128)}, s32[16,256]{1,0:T(8,128)}) custom-call(s32[8]{0:T(128)} %refs_0_.1, s32[1,192]{1,0:T(1,128)} %bitcast.87, s32[1,192]{1,0:T(1,128)} %bitcast.88, bf16[160,192]{1,0:T(8,128)(2,1)} %bitcast.83, bf16[32,192]{1,0:T(8,128)(2,1)} %bitcast.85, ...), custom_call_target="tpu_custom_call" | custom-call | flops 1000000000 | bytes 4000000 | tf_op jit(solution)/shard_map/assemble/pallas_call | solution.py:321
  8.5 0.1 collective-permute-start
  8.6 1.4 %copy-done.1 = f32[1600,256]{1,0:T(8,128)S(1)} copy-done((f32[1600,256]{1,0:T(8,128)S(1)}, f32[1600,256]{1,0:T(8,128)}, u32[]{:S(2)}) %copy-start.1) | copy-done | bytes 1638424
  10.0 0.7 %copy-done.3 = s32[16,256]{1,0:T(8,128)S(1)} copy-done((s32[16,256]{1,0:T(8,128)S(1)}, s32[16,256]{1,0:T(8,128)}, u32[]{:S(2)}) %copy-start.3) | copy-done | bytes 16408
  10.7 5.6 %assemble.5 = (bf16[4,1,592,128]{3,2,1,0:T(8,128)(2,1)S(1)}, bf16[4,1,592,128]{3,2,1,0:T(8,128)(2,1)S(1)}) custom-call(f32[1600,256]{1,0:T(8,128)S(1)} %copy-done.1, s32[16,256]{1,0:T(8,128)S(1)} %copy-done.3, bf16[192,32,128]{2,1,0:T(8,128)(2,1)S(1)} %copy-done), custom_call_target="tpu_custom_call" | custom-call | flops 1000000000 | bytes 4000000 | tf_op jit(solution)/shard_map/assemble/pallas_call | solution.py:321
  16.3 0.5 collective-permute-start.2
  16.9 0.1 fusion
  17.0 2.4 %collective-permute-start.1 = (bf16[2,592,128]{2,1,0:T(8,128)(2,1)S(1)}, bf16[2,592,128]{2,1,0:T(8,128)(2,1)S(1)}, u32[]{:S(2)}, u32[]{:S(2)}) collective-permute-start(bf16[2,592,128]{2,1,0:T(8,128)(2,1)S(1)} %fusion), channel_id=1, source_target_pairs={{0,2},{1,5},{2,0},{3,7},{4,6},{5,1},{6,4},{7,3},{8,10},{9,13},{10,... | collective-permute-start | bytes 909320 | tf_op jit(solution)/shard_map/ppermute | solution.py:409
  19.4 2.9 %assemble.6 = (bf16[4,1,592,128]{3,2,1,0:T(8,128)(2,1)S(1)}, bf16[4,1,592,128]{3,2,1,0:T(8,128)(2,1)S(1)}) custom-call(f32[1600,256]{1,0:T(8,128)S(1)} %copy-done.2, s32[16,256]{1,0:T(8,128)S(1)} %copy-done.4, bf16[192,32,128]{2,1,0:T(8,128)(2,1)S(1)} %copy-done), custom_call_target="tpu_custom_call" | custom-call | flops 1000000000 | bytes 4000000 | tf_op jit(solution)/shard_map/assemble/pallas_call | solution.py:321
  22.2 0.0 collective-permute-done.2
  22.2 0.1 fusion.1
  22.3 0.1 collective-permute-start.8
  22.4 0.9 %collective-permute-start.11 = (bf16[4,1,592,128]{3,2,0,1:T(8,128)(2,1)S(1)}, bf16[4,1,592,128]{3,2,0,1:T(8,128)(2,1)S(1)}, u32[]{:S(2)}, u32[]{:S(2)}) collective-permute-start(bf16[4,1,592,128]{3,2,0,1:T(8,128)(2,1)S(1)} %bitcast.76), channel_id=1, source_target_pairs={{0,1},{1,0},{2,3},{3,2},{4,5},{5,4},{6,7},{7,6},{8,9},{9,8},{10,11... | collective-permute-start | bytes 1818632 | tf_op jit(solution)/shard_map/ppermute | solution.py:409
  23.3 0.8 %collective-permute-done.1 = bf16[2,592,128]{2,1,0:T(8,128)(2,1)S(1)} collective-permute-done((bf16[2,592,128]{2,1,0:T(8,128)(2,1)S(1)}, bf16[2,592,128]{2,1,0:T(8,128)(2,1)S(1)}, u32[]{:S(2)}, u32[]{:S(2)}) %collective-permute-start.1) | collective-permute-done | bytes 303136 | tf_op jit(solution)/shard_map/ppermute | solution.py:409
  24.2 0.1 bitcast_add_fusion.3
  24.3 2.7 %collective-permute-start.6 = (bf16[592,128]{1,0:T(8,128)(2,1)S(1)}, bf16[592,128]{1,0:T(8,128)(2,1)S(1)}, u32[]{:S(2)}, u32[]{:S(2)}) collective-permute-start(bf16[592,128]{1,0:T(8,128)(2,1)S(1)} %fusion.14), channel_id=1, source_target_pairs={{0,4},{1,3},{2,6},{3,1},{4,0},{5,7},{6,2},{7,5},{8,12},{9,11},{10,... | collective-permute-start | bytes 454664 | tf_op jit(solution)/shard_map/ppermute | solution.py:409
  27.0 2.4 %assemble.7 = (bf16[4,1,592,128]{3,2,1,0:T(8,128)(2,1)S(1)}, bf16[4,1,592,128]{3,2,1,0:T(8,128)(2,1)S(1)}) custom-call(f32[1600,256]{1,0:T(8,128)S(1)} %copy-done.2, s32[16,256]{1,0:T(8,128)S(1)} %copy-done.4, bf16[192,32,128]{2,1,0:T(8,128)(2,1)S(1)} %copy-done), custom_call_target="tpu_custom_call" | custom-call | flops 1000000000 | bytes 4000000 | tf_op jit(solution)/shard_map/assemble/pallas_call | solution.py:321
  29.4 1.4 %collective-permute-done.8 = bf16[2,592,128]{2,1,0:T(8,128)(2,1)S(1)} collective-permute-done((bf16[2,592,128]{2,1,0:T(8,128)(2,1)S(1)}, bf16[2,592,128]{2,1,0:T(8,128)(2,1)S(1)}, u32[]{:S(2)}, u32[]{:S(2)}) %collective-permute-start.8) | collective-permute-done | bytes 303136 | tf_op jit(solution)/shard_map/ppermute | solution.py:409
  30.8 0.1 bitcast_add_fusion.1
  31.0 0.5 collective-permute-start.9
  31.5 0.0 collective-permute-done.6
  31.5 0.0 collective-permute-done.11
  31.5 0.1 fusion.3
  31.6 2.3 %collective-permute-start.12 = (bf16[2,592,128]{2,1,0:T(8,128)(2,1)S(1)}, bf16[2,592,128]{2,1,0:T(8,128)(2,1)S(1)}, u32[]{:S(2)}, u32[]{:S(2)}) collective-permute-start(bf16[2,592,128]{2,1,0:T(8,128)(2,1)S(1)} %fusion.3), channel_id=1, source_target_pairs={{0,2},{1,5},{2,0},{3,7},{4,6},{5,1},{6,4},{7,3},{8,10},{9,13},{10,... | collective-permute-start | bytes 909320 | tf_op jit(solution)/shard_map/ppermute | solution.py:409
  33.9 0.1 fusion.2
  34.0 0.1 collective-permute-start.4
  34.1 3.6 %collective-permute-start.7 = (bf16[592,128]{1,0:T(8,128)(2,1)S(1)}, bf16[592,128]{1,0:T(8,128)(2,1)S(1)}, u32[]{:S(2)}, u32[]{:S(2)}) collective-permute-start(bf16[592,128]{1,0:T(8,128)(2,1)S(1)} %fusion.9), channel_id=1, source_target_pairs={{0,24},{8,16},{16,8},{24,0},{1,25},{9,17},{17,9},{25,1},{2,26},{10... | collective-permute-start | bytes 454664 | tf_op jit(solution)/shard_map/ppermute | solution.py:412
  37.7 0.0 collective-permute-done.9
  37.7 1.3 %collective-permute-done.12 = bf16[2,592,128]{2,1,0:T(8,128)(2,1)S(1)} collective-permute-done((bf16[2,592,128]{2,1,0:T(8,128)(2,1)S(1)}, bf16[2,592,128]{2,1,0:T(8,128)(2,1)S(1)}, u32[]{:S(2)}, u32[]{:S(2)}) %collective-permute-start.12) | collective-permute-done | bytes 303136 | tf_op jit(solution)/shard_map/ppermute | solution.py:409
  39.0 0.1 bitcast_add_fusion
  39.1 1.1 %collective-permute-start.13 = (bf16[592,128]{1,0:T(8,128)(2,1)S(1)}, bf16[592,128]{1,0:T(8,128)(2,1)S(1)}, u32[]{:S(2)}, u32[]{:S(2)}) collective-permute-start(bf16[592,128]{1,0:T(8,128)(2,1)S(1)} %fusion.17), channel_id=1, source_target_pairs={{0,4},{1,3},{2,6},{3,1},{4,0},{5,7},{6,2},{7,5},{8,12},{9,11},{10,... | collective-permute-start | bytes 454664 | tf_op jit(solution)/shard_map/ppermute | solution.py:409
  40.3 0.5 collective-permute-start.10
  40.7 3.7 %collective-permute-done.13 = bf16[592,128]{1,0:T(8,128)(2,1)S(1)} collective-permute-done((bf16[592,128]{1,0:T(8,128)(2,1)S(1)}, bf16[592,128]{1,0:T(8,128)(2,1)S(1)}, u32[]{:S(2)}, u32[]{:S(2)}) %collective-permute-start.13) | collective-permute-done | bytes 151584 | tf_op jit(solution)/shard_map/ppermute | solution.py:409
  44.4 2.2 %collective-permute-start.14 = (bf16[592,128]{1,0:T(8,128)(2,1)S(1)}, bf16[592,128]{1,0:T(8,128)(2,1)S(1)}, u32[]{:S(2)}, u32[]{:S(2)}) collective-permute-start(bf16[592,128]{1,0:T(8,128)(2,1)S(1)} %fusion.5), channel_id=1, source_target_pairs={{0,8},{8,0},{16,24},{24,16},{1,9},{9,1},{17,25},{25,17},{2,10},{10... | collective-permute-start | bytes 454664 | tf_op jit(solution)/shard_map/ppermute | solution.py:412
  46.7 0.1 bitcast_add_fusion.2
  46.8 1.1 %collective-permute-start.5 = (bf16[592,128]{1,0:T(8,128)(2,1)S(1)}, bf16[592,128]{1,0:T(8,128)(2,1)S(1)}, u32[]{:S(2)}, u32[]{:S(2)}) collective-permute-start(bf16[592,128]{1,0:T(8,128)(2,1)S(1)} %fusion.15), channel_id=1, source_target_pairs={{0,4},{1,3},{2,6},{3,1},{4,0},{5,7},{6,2},{7,5},{8,12},{9,11},{10,... | collective-permute-start | bytes 454664 | tf_op jit(solution)/shard_map/ppermute | solution.py:409
  47.9 2.8 %collective-permute-done.10 = bf16[592,128]{1,0:T(8,128)(2,1)S(1)} collective-permute-done((bf16[592,128]{1,0:T(8,128)(2,1)S(1)}, bf16[592,128]{1,0:T(8,128)(2,1)S(1)}, u32[]{:S(2)}, u32[]{:S(2)}) %collective-permute-start.10) | collective-permute-done | bytes 151584 | tf_op jit(solution)/shard_map/ppermute | solution.py:412
  50.7 0.0 collective-permute-done.7
  50.7 2.2 %collective-permute-done.14 = bf16[592,128]{1,0:T(8,128)(2,1)S(1)} collective-permute-done((bf16[592,128]{1,0:T(8,128)(2,1)S(1)}, bf16[592,128]{1,0:T(8,128)(2,1)S(1)}, u32[]{:S(2)}, u32[]{:S(2)}) %collective-permute-start.14) | collective-permute-done | bytes 151584 | tf_op jit(solution)/shard_map/ppermute | solution.py:412
  52.9 0.1 fusion.18
  53.0 0.1 collective-permute-start.17
  53.1 1.3 %collective-permute-start.16 = (bf16[128,128]{1,0:T(8,128)(2,1)S(1)}, bf16[128,128]{1,0:T(8,128)(2,1)S(1)}, u32[]{:S(2)}, u32[]{:S(2)}) collective-permute-start(bf16[128,128]{1,0:T(8,128)(2,1)S(1)} %get-tuple-element.59), channel_id=1, source_target_pairs={{0,2},{1,3},{2,4},{3,5},{4,6},{5,7},{6,0},{7,1},{8,10},{9,11},{10,... | collective-permute-start | bytes 98312 | tf_op jit(solution)/shard_map/ppermute | solution.py:477
  54.3 0.9 %collective-permute-start.15 = (bf16[128,128]{1,0:T(8,128)(2,1)S(1)}, bf16[128,128]{1,0:T(8,128)(2,1)S(1)}, u32[]{:S(2)}, u32[]{:S(2)}) collective-permute-start(bf16[128,128]{1,0:T(8,128)(2,1)S(1)} %get-tuple-element.60), channel_id=1, source_target_pairs={{0,1},{1,2},{2,3},{3,4},{4,5},{5,6},{6,7},{7,0},{8,9},{9,10},{10,1... | collective-permute-start | bytes 98312 | tf_op jit(solution)/shard_map/ppermute | solution.py:477
  55.2 0.9 %collective-permute-start.18 = (bf16[64,128]{1,0:T(8,128)(2,1)S(1)}, bf16[64,128]{1,0:T(8,128)(2,1)S(1)}, u32[]{:S(2)}, u32[]{:S(2)}) collective-permute-start(bf16[64,128]{1,0:T(8,128)(2,1)S(1)} %slice.143), channel_id=1, source_target_pairs={{0,4},{1,5},{2,6},{3,7},{4,0},{5,1},{6,2},{7,3},{8,12},{9,13},{10,... | collective-permute-start | bytes 49160 | tf_op jit(solution)/shard_map/ppermute | solution.py:477
  56.1 2.8 %collective-permute-done.18.e_ref = bf16[64,128]{1,0:T(8,128)(2,1)S(1)} collective-permute-done((bf16[64,128]{1,0:T(8,128)(2,1)S(1)}, bf16[64,128]{1,0:T(8,128)(2,1)S(1)}, u32[]{:S(2)}, u32[]{:S(2)}) %collective-permute-start.18) | collective-permute-done | bytes 16416 | tf_op jit(solution)/shard_map/ppermute | solution.py:477
  59.0 0.0 collective-permute-done.16.r2_ref
  59.0 0.0 collective-permute-done.15.r1_ref
  59.0 0.9 %finish.1 = (f32[128,1024]{1,0:T(8,128)}, f32[1,128]{1,0:T(1,128)}) custom-call(f32[592,128]{1,0:T(8,128)S(1)} %get-tuple-element.57.own_ref, bf16[128,128]{1,0:T(8,128)(2,1)S(1)} %collective-permute-done.15.r1_ref, bf16[128,128]{1,0:T(8,128)(2,1)S(1)} %collective-permute-done.16.r2_ref, bf16[128,128]{1,0:T(8,128)(2,1)S(1)} %collective-permute-done.17.r3_ref, ...), custom_call_target="tpu_custom_call" | custom-call | tf_op jit(solution)/shard_map/finish/pallas_call | solution.py:375
  (25 shorter events, 0.2 us)
Async XLA Ops:
  0.6 7.9 %copy-start = (bf16[192,32,128]{2,1,0:T(8,128)(2,1)S(1)}, bf16[192,32,128]{2,1,0:T(8,128)(2,1)}, u32[]{:S(2)}) copy-start(bf16[192,32,128]{2,1,0:T(8,128)(2,1)} %g_ref.5) | copy-start | bytes 4718596
  8.5 8.4 %collective-permute-start = (bf16[4,1,592,128]{3,2,0,1:T(8,128)(2,1)}, bf16[4,1,592,128]{3,2,0,1:T(8,128)(2,1)S(1)}, u32[]{:S(2)}, u32[]{:S(2)}) collective-permute-start(bf16[4,1,592,128]{3,2,0,1:T(8,128)(2,1)} %bitcast.81), channel_id=1, source_target_pairs={{0,1},{1,0},{2,3},{3,2},{4,5},{5,4},{6,7},{7,6},{8,9},{9,8},{10,11... | collective-permute-start | bytes 1818632 | tf_op jit(solution)/shard_map/ppermute | solution.py:409
  8.6 1.4 %copy-start.1 = (f32[1600,256]{1,0:T(8,128)S(1)}, f32[1600,256]{1,0:T(8,128)}, u32[]{:S(2)}) copy-start(f32[1600,256]{1,0:T(8,128)} %get-tuple-element.29.shared_ref) | copy-start | bytes 4915204
  10.0 0.7 %copy-start.3 = (s32[16,256]{1,0:T(8,128)S(1)}, s32[16,256]{1,0:T(8,128)}, u32[]{:S(2)}) copy-start(s32[16,256]{1,0:T(8,128)} %get-tuple-element.43.table_ref) | copy-start | bytes 49156
  10.7 6.2 %copy-start.5 = (bf16[4,1,592,128]{3,2,1,0:T(8,128)(2,1)S(1)}, bf16[4,1,592,128]{3,2,1,0:T(8,128)(2,1)}, u32[]{:S(2)}) copy-start(bf16[4,1,592,128]{3,2,1,0:T(8,128)(2,1)} %get-tuple-element.35) | copy-start | bytes 1818628
  10.7 8.7 %copy-start.2 = (f32[1600,256]{1,0:T(8,128)S(1)}, f32[1600,256]{1,0:T(8,128)}, u32[]{:S(2)}) copy-start(f32[1600,256]{1,0:T(8,128)} %get-tuple-element.29.shared_ref) | copy-start | bytes 4915204
  10.7 8.7 %copy-start.4 = (s32[16,256]{1,0:T(8,128)S(1)}, s32[16,256]{1,0:T(8,128)}, u32[]{:S(2)}) copy-start(s32[16,256]{1,0:T(8,128)} %get-tuple-element.43.table_ref) | copy-start | bytes 49156
  16.3 5.9 %collective-permute-start.2 = (bf16[4,1,592,128]{3,2,0,1:T(8,128)(2,1)S(1)}, bf16[4,1,592,128]{3,2,0,1:T(8,128)(2,1)S(1)}, u32[]{:S(2)}, u32[]{:S(2)}) collective-permute-start(bf16[4,1,592,128]{3,2,0,1:T(8,128)(2,1)S(1)} %bitcast.78), channel_id=1, source_target_pairs={{0,1},{1,0},{2,3},{3,2},{4,5},{5,4},{6,7},{7,6},{8,9},{9,8},{10,11... | collective-permute-start | bytes 1818632 | tf_op jit(solution)/shard_map/ppermute | solution.py:409
  17.0 7.2 %collective-permute-start.1 = (bf16[2,592,128]{2,1,0:T(8,128)(2,1)S(1)}, bf16[2,592,128]{2,1,0:T(8,128)(2,1)S(1)}, u32[]{:S(2)}, u32[]{:S(2)}) collective-permute-start(bf16[2,592,128]{2,1,0:T(8,128)(2,1)S(1)} %fusion), channel_id=1, source_target_pairs={{0,2},{1,5},{2,0},{3,7},{4,6},{5,1},{6,4},{7,3},{8,10},{9,13},{10,... | collective-permute-start | bytes 909320 | tf_op jit(solution)/shard_map/ppermute | solution.py:409
  22.3 8.5 %collective-permute-start.8 = (bf16[2,592,128]{2,1,0:T(8,128)(2,1)S(1)}, bf16[2,592,128]{2,1,0:T(8,128)(2,1)S(1)}, u32[]{:S(2)}, u32[]{:S(2)}) collective-permute-start(bf16[2,592,128]{2,1,0:T(8,128)(2,1)S(1)} %fusion.1), channel_id=1, source_target_pairs={{0,2},{1,5},{2,0},{3,7},{4,6},{5,1},{6,4},{7,3},{8,10},{9,13},{10,... | collective-permute-start | bytes 909320 | tf_op jit(solution)/shard_map/ppermute | solution.py:409
  22.4 9.0 %collective-permute-start.11 = (bf16[4,1,592,128]{3,2,0,1:T(8,128)(2,1)S(1)}, bf16[4,1,592,128]{3,2,0,1:T(8,128)(2,1)S(1)}, u32[]{:S(2)}, u32[]{:S(2)}) collective-permute-start(bf16[4,1,592,128]{3,2,0,1:T(8,128)(2,1)S(1)} %bitcast.76), channel_id=1, source_target_pairs={{0,1},{1,0},{2,3},{3,2},{4,5},{5,4},{6,7},{7,6},{8,9},{9,8},{10,11... | collective-permute-start | bytes 1818632 | tf_op jit(solution)/shard_map/ppermute | solution.py:409
  24.3 7.2 %collective-permute-start.6 = (bf16[592,128]{1,0:T(8,128)(2,1)S(1)}, bf16[592,128]{1,0:T(8,128)(2,1)S(1)}, u32[]{:S(2)}, u32[]{:S(2)}) collective-permute-start(bf16[592,128]{1,0:T(8,128)(2,1)S(1)} %fusion.14), channel_id=1, source_target_pairs={{0,4},{1,3},{2,6},{3,1},{4,0},{5,7},{6,2},{7,5},{8,12},{9,11},{10,... | collective-permute-start | bytes 454664 | tf_op jit(solution)/shard_map/ppermute | solution.py:409
  30.8 3.1 %collective-permute-start.3 = (bf16[4,1,592,128]{3,2,0,1:T(8,128)(2,1)S(1)}, bf16[4,1,592,128]{3,2,0,1:T(8,128)(2,1)S(1)}, u32[]{:S(2)}, u32[]{:S(2)}) collective-permute-start(bf16[4,1,592,128]{3,2,0,1:T(8,128)(2,1)S(1)} %bitcast.77), channel_id=1, source_target_pairs={{0,1},{1,0},{2,3},{3,2},{4,5},{5,4},{6,7},{7,6},{8,9},{9,8},{10,11... | collective-permute-start | bytes 1818632 | tf_op jit(solution)/shard_map/ppermute | solution.py:409
  31.0 6.8 %collective-permute-start.9 = (bf16[592,128]{1,0:T(8,128)(2,1)S(1)}, bf16[592,128]{1,0:T(8,128)(2,1)S(1)}, u32[]{:S(2)}, u32[]{:S(2)}) collective-permute-start(bf16[592,128]{1,0:T(8,128)(2,1)S(1)} %fusion.16), channel_id=1, source_target_pairs={{0,4},{1,3},{2,6},{3,1},{4,0},{5,7},{6,2},{7,5},{8,12},{9,11},{10,... | collective-permute-start | bytes 454664 | tf_op jit(solution)/shard_map/ppermute | solution.py:409
  31.6 7.4 %collective-permute-start.12 = (bf16[2,592,128]{2,1,0:T(8,128)(2,1)S(1)}, bf16[2,592,128]{2,1,0:T(8,128)(2,1)S(1)}, u32[]{:S(2)}, u32[]{:S(2)}) collective-permute-start(bf16[2,592,128]{2,1,0:T(8,128)(2,1)S(1)} %fusion.3), channel_id=1, source_target_pairs={{0,2},{1,5},{2,0},{3,7},{4,6},{5,1},{6,4},{7,3},{8,10},{9,13},{10,... | collective-permute-start | bytes 909320 | tf_op jit(solution)/shard_map/ppermute | solution.py:409
  34.0 12.7 %collective-permute-start.4 = (bf16[2,592,128]{2,1,0:T(8,128)(2,1)S(1)}, bf16[2,592,128]{2,1,0:T(8,128)(2,1)S(1)}, u32[]{:S(2)}, u32[]{:S(2)}) collective-permute-start(bf16[2,592,128]{2,1,0:T(8,128)(2,1)S(1)} %fusion.2), channel_id=1, source_target_pairs={{0,2},{1,5},{2,0},{3,7},{4,6},{5,1},{6,4},{7,3},{8,10},{9,13},{10,... | collective-permute-start | bytes 909320 | tf_op jit(solution)/shard_map/ppermute | solution.py:409
  34.1 16.6 %collective-permute-start.7 = (bf16[592,128]{1,0:T(8,128)(2,1)S(1)}, bf16[592,128]{1,0:T(8,128)(2,1)S(1)}, u32[]{:S(2)}, u32[]{:S(2)}) collective-permute-start(bf16[592,128]{1,0:T(8,128)(2,1)S(1)} %fusion.9), channel_id=1, source_target_pairs={{0,24},{8,16},{16,8},{24,0},{1,25},{9,17},{17,9},{25,1},{2,26},{10... | collective-permute-start | bytes 454664 | tf_op jit(solution)/shard_map/ppermute | solution.py:412
  39.1 5.3 %collective-permute-start.13 = (bf16[592,128]{1,0:T(8,128)(2,1)S(1)}, bf16[592,128]{1,0:T(8,128)(2,1)S(1)}, u32[]{:S(2)}, u32[]{:S(2)}) collective-permute-start(bf16[592,128]{1,0:T(8,128)(2,1)S(1)} %fusion.17), channel_id=1, source_target_pairs={{0,4},{1,3},{2,6},{3,1},{4,0},{5,7},{6,2},{7,5},{8,12},{9,11},{10,... | collective-permute-start | bytes 454664 | tf_op jit(solution)/shard_map/ppermute | solution.py:409
  40.3 10.4 %collective-permute-start.10 = (bf16[592,128]{1,0:T(8,128)(2,1)S(1)}, bf16[592,128]{1,0:T(8,128)(2,1)S(1)}, u32[]{:S(2)}, u32[]{:S(2)}) collective-permute-start(bf16[592,128]{1,0:T(8,128)(2,1)S(1)} %fusion.7), channel_id=1, source_target_pairs={{0,16},{8,24},{16,0},{24,8},{1,17},{9,25},{17,1},{25,9},{2,18},{10... | collective-permute-start | bytes 454664 | tf_op jit(solution)/shard_map/ppermute | solution.py:412
  44.4 8.4 %collective-permute-start.14 = (bf16[592,128]{1,0:T(8,128)(2,1)S(1)}, bf16[592,128]{1,0:T(8,128)(2,1)S(1)}, u32[]{:S(2)}, u32[]{:S(2)}) collective-permute-start(bf16[592,128]{1,0:T(8,128)(2,1)S(1)} %fusion.5), channel_id=1, source_target_pairs={{0,8},{8,0},{16,24},{24,16},{1,9},{9,1},{17,25},{25,17},{2,10},{10... | collective-permute-start | bytes 454664 | tf_op jit(solution)/shard_map/ppermute | solution.py:412
  46.8 6.1 %collective-permute-start.5 = (bf16[592,128]{1,0:T(8,128)(2,1)S(1)}, bf16[592,128]{1,0:T(8,128)(2,1)S(1)}, u32[]{:S(2)}, u32[]{:S(2)}) collective-permute-start(bf16[592,128]{1,0:T(8,128)(2,1)S(1)} %fusion.15), channel_id=1, source_target_pairs={{0,4},{1,3},{2,6},{3,1},{4,0},{5,7},{6,2},{7,5},{8,12},{9,11},{10,... | collective-permute-start | bytes 454664 | tf_op jit(solution)/shard_map/ppermute | solution.py:409
  53.0 6.0 %collective-permute-start.17 = (bf16[128,128]{1,0:T(8,128)(2,1)S(1)}, bf16[128,128]{1,0:T(8,128)(2,1)S(1)}, u32[]{:S(2)}, u32[]{:S(2)}) collective-permute-start(bf16[128,128]{1,0:T(8,128)(2,1)S(1)} %get-tuple-element.58), channel_id=1, source_target_pairs={{0,3},{1,4},{2,5},{3,6},{4,7},{5,0},{6,1},{7,2},{8,11},{9,12},{10,... | collective-permute-start | bytes 98312 | tf_op jit(solution)/shard_map/ppermute | solution.py:477
  53.1 5.9 %collective-permute-start.16 = (bf16[128,128]{1,0:T(8,128)(2,1)S(1)}, bf16[128,128]{1,0:T(8,128)(2,1)S(1)}, u32[]{:S(2)}, u32[]{:S(2)}) collective-permute-start(bf16[128,128]{1,0:T(8,128)(2,1)S(1)} %get-tuple-element.59), channel_id=1, source_target_pairs={{0,2},{1,3},{2,4},{3,5},{4,6},{5,7},{6,0},{7,1},{8,10},{9,11},{10,... | collective-permute-start | bytes 98312 | tf_op jit(solution)/shard_map/ppermute | solution.py:477
  54.3 4.7 %collective-permute-start.15 = (bf16[128,128]{1,0:T(8,128)(2,1)S(1)}, bf16[128,128]{1,0:T(8,128)(2,1)S(1)}, u32[]{:S(2)}, u32[]{:S(2)}) collective-permute-start(bf16[128,128]{1,0:T(8,128)(2,1)S(1)} %get-tuple-element.60), channel_id=1, source_target_pairs={{0,1},{1,2},{2,3},{3,4},{4,5},{5,6},{6,7},{7,0},{8,9},{9,10},{10,1... | collective-permute-start | bytes 98312 | tf_op jit(solution)/shard_map/ppermute | solution.py:477
  55.2 3.8 %collective-permute-start.18 = (bf16[64,128]{1,0:T(8,128)(2,1)S(1)}, bf16[64,128]{1,0:T(8,128)(2,1)S(1)}, u32[]{:S(2)}, u32[]{:S(2)}) collective-permute-start(bf16[64,128]{1,0:T(8,128)(2,1)S(1)} %slice.143), channel_id=1, source_target_pairs={{0,4},{1,5},{2,6},{3,7},{4,0},{5,1},{6,2},{7,3},{8,12},{9,13},{10,... | collective-permute-start | bytes 49160 | tf_op jit(solution)/shard_map/ppermute | solution.py:477

commit v7 on v4

--- a/solution.py
+++ b/solution.py
@@ -287,9 +287,13 @@
             p = block ^ (jnp.where(block % 2 == 1 - odd, ODD[n], EVEN[n]) + odd)
             columns = pl.ds(pl.multiple_of(p * width, width), width)
             parts = [direct_s[0:width, columns] + acc_s[p, :, 0:width]]
-            parts += [acc_s[p, :, d * width : (d + 1) * width] for d in range(1, many)]
+            for d in range(1, many):
+                parts.append(acc_s[p, :half, d * width : (d + 1) * width])
             upper = pl.multiple_of((p // many) * half, half)
             parts.append(acc_s[p % many, pl.ds(upper, half), many * width :])
+            for d in range(1, many):
+                other = (p + blocks - d) % blocks
+                parts.append(acc_s[other, half:, d * width : (d + 1) * width])
             row = direct_s[width : width + 1, columns]
             high = row.astype(BF16).astype(F32)
             sub = iota((16, width), 0)
@@ -340,49 +344,69 @@
     )(*inputs, g)
 
 
-def finish_kernel(sub, own_ref, r1_ref, r2_ref, r3_ref, e_ref, out_ref, vec_ref):
+def gather_kernel(sub, own_ref, *refs):
+    crossed, (total_ref, send_ref) = refs[:-2], refs[-2:]
     width = own_ref.shape[1]
+    half = width // 2
+    blocks = send_ref.shape[0]
+    p = lax.axis_index("tile") // sub
+    total = own_ref[...]
+    for ref in crossed:
+        total = total + ref[...].astype(F32)
+    total_ref[...] = total
+    send_ref[p] = jnp.zeros(send_ref.shape[1:], BF16)
+    for n, d in enumerate(distances(blocks)):
+        at = width + n * half
+        send_ref[(p + blocks + d) % blocks] = total[at : at + half].astype(BF16)
+
+
+def distances(blocks):
+    return [*range(1, blocks // 2 + 1), *range(-1, -(blocks // 2), -1)]
+
+
+def finish_kernel(sub, own_ref, got_ref, out_ref, vec_ref):
+    width = own_ref.shape[1]
+    half = width // 2
     p = lax.axis_index("tile") // sub
     blocks = out_ref.shape[1] // width
     many = blocks // 2
 
-    def put(column, value):
-        column = pl.multiple_of(((column + blocks) % blocks) * width, width)
-        out_ref[:, pl.ds(column, width)] = value
-
-    for d in range(many):
-        put(p + d, own_ref[d * width : (d + 1) * width, :])
-    for d, ref in ((1, r1_ref), (2, r2_ref), (3, r3_ref)):
-        put(p - d, ref[...].astype(F32).T)
-    tail = many * width + width // 2
-    mine = own_ref[many * width : tail, :]
-    other = e_ref[...].astype(F32)
-
-    @pl.when(p < many)
-    def _():
-        put(p + many, jnp.concatenate([mine, other], axis=0))
-
-    @pl.when(p >= many)
-    def _():
-        put(p + many, jnp.concatenate([other, mine], axis=0).T)
-
+    def put(place, value):
+        out_ref[:, pl.ds(pl.multiple_of(place * width, width), width)] = value
+
+    put(p, own_ref[0:width, :])
+    for n, d in enumerate(distances(blocks)):
+        at = width + n * half
+        place = (p + blocks + d) % blocks
+        mine, other = own_ref[at : at + half, :], got_ref[place].astype(F32)
+        if 0 < d < many:
+            put(place, jnp.concatenate([mine, other], axis=0))
+        elif d < 0:
+            put(place, jnp.concatenate([other, mine], axis=0).T)
+        else:
+
+            @pl.when(p < many)
+            def _():
+                put(place, jnp.concatenate([mine, other], axis=0))
+
+            @pl.when(p >= many)
+            def _():
+                put(place, jnp.concatenate([other, mine], axis=0).T)
+
+    tail = width + (blocks - 1) * half
     vec_ref[...] = own_ref[tail : tail + 1, :] + own_ref[tail + 1 : tail + 2, :]
 
 
-def finish(sub, own, r1, r2, r3, ext, blocks):
-    width = own.shape[1]
+def small_call(kernel, out_shape, name, *values):
     vmem = pl.BlockSpec(memory_space=pltpu.VMEM)
     return pl.pallas_call(
-        functools.partial(finish_kernel, sub),
-        in_specs=[vmem] * 5,
-        out_specs=[vmem, vmem],
-        out_shape=[
-            jax.ShapeDtypeStruct((width, blocks * width), F32),
-            jax.ShapeDtypeStruct((1, width), F32),
-        ],
+        kernel,
+        in_specs=[vmem] * len(values),
+        out_specs=[vmem] * len(out_shape),
+        out_shape=out_shape,
         compiler_params=pltpu.CompilerParams(vmem_limit_bytes=8 * 1024 * 1024),
-        name="finish",
-    )(own, r1, r2, r3, ext)
+        name=name,
+    )(*values)
 
 
 def local(
@@ -441,9 +465,9 @@
         k = regions - 1 - (slot - 3)
         if 0 <= k < regions:
             total = seconds[k][0] + after(seconds[k][1], done).astype(F32)
-            for value in incoming[k]:
-                total = total + value.astype(F32)
             if k:
+                for value in incoming[k]:
+                    total = total + value.astype(F32)
                 operands.append(total.astype(BF16))
                 incoming[k - (k & -k)].append(across(operands[-1], k & -k))
             else:
@@ -463,18 +487,30 @@
             inputs = inputs[0], after(inputs[1], (send, operands))
             cores[k - 1] = near(keep, send)
 
-    def onward(value, d):
-        pairs = [
-            (p * sub + s, ((p + d) % blocks) * sub + s) for p in range(blocks) for s in range(sub)
-        ]
-        return lax.ppermute(value.astype(BF16), "tile", pairs)
-
-    matrix, vector = finish(
-        sub,
+    crossed = incoming[0]
+    own, send = small_call(
+        functools.partial(gather_kernel, sub),
+        [
+            jax.ShapeDtypeStruct(own.shape, F32),
+            jax.ShapeDtypeStruct((blocks, width // 2, width), BF16),
+        ],
+        "gather",
         own,
-        *(onward(own[d * width : (d + 1) * width], d) for d in range(1, blocks // 2)),
-        onward(own[blocks // 2 * width : blocks // 2 * width + width // 2], blocks // 2),
-        blocks,
+        *crossed,
+    )
+    across_tiles = [[b * sub + n for b in range(blocks)] for n in range(sub)]
+    got = lax.all_to_all(
+        send, "tile", 0, 0, axis_index_groups=across_tiles if sub > 1 else None, tiled=True
+    )
+    matrix, vector = small_call(
+        functools.partial(finish_kernel, sub),
+        [
+            jax.ShapeDtypeStruct((width, blocks * width), F32),
+            jax.ShapeDtypeStruct((1, width), F32),
+        ],
+        "finish",
+        own,
+        got,
     )
     if sub > 1:
         part = tile % sub

time: 59.7 us -> 61 us (1.022)
  blocking collectives: 0 us -> 8.37 us
  waiting for transfers between devices: 18.4 us -> 12 us
    all_to_all x0 -> x1, blocking collectives: none -> 8.37 us  [local(): lax.all_to_all(send, 'tile', 0, 0, axis_index_groups=across_tiles if sub...]
    ppermute x12, waiting for transfers between devices: 10.5 us -> 6.34 us  [swap(): return lax.ppermute(value, 'tile', pairs)]
    ppermute x4 -> x0, waiting for transfers between devices: 3.09 us -> none  [onward(): return lax.ppermute(value.astype(BF16), 'tile', pairs)]
    ppermute x12, starting transfers between devices: 9.42 us -> 12 us  [swap(): return lax.ppermute(value, 'tile', pairs)]
    ppermute x4 -> x0, starting transfers between devices: 2.54 us -> none  [onward(): return lax.ppermute(value.astype(BF16), 'tile', pairs)]
    ppermute x3, waiting for transfers between devices: 4.83 us -> 5.71 us  [across(): lax.ppermute(value.astype(BF16), 'region', [(r, r ^ k) for r in range(reg...]
  transfers between devices with their start and end apart: 19 -> 15, of which waited for: 8 -> 6; matrix products, arithmetic and copies ran while one was open for 2% -> 2% of each run, Pallas kernels for 16% -> 19%
where the time goes in v7:
time: 61 us
  Pallas kernels  18.8 us (31%)
  starting transfers between devices  17.8 us (29%)
  waiting for transfers between devices  12 us (20%)
  blocking collectives  8.37 us (14%)
  local copies, waits for them, and re-layouts  2.23 us (4%)
  other arithmetic  0.91 us (1%)
  between operations  0.8 us (1%)
    pallas_call x4, Pallas kernels, assemble(): pl.pallas_call(functools.partial(lead_kernel if lead else follow_kernel,...  17.8 us
    ppermute x12, starting transfers between devices, swap(): return lax.ppermute(value, 'tile', pairs)  12 us
    all_to_all x1, blocking collectives, local(): lax.all_to_all(send, 'tile', 0, 0, axis_index_groups=across_tiles if sub...  8.37 us
    ppermute x12, waiting for transfers between devices, swap(): return lax.ppermute(value, 'tile', pairs)  6.34 us
    ppermute x3, starting transfers between devices, across(): lax.ppermute(value.astype(BF16), 'region', [(r, r ^ k) for r in range(reg...  5.79 us
    ppermute x3, waiting for transfers between devices, across(): lax.ppermute(value.astype(BF16), 'region', [(r, r ^ k) for r in range(reg...  5.71 us
    unnamed x12, local copies, waits for them, and re-layouts  2.16 us
  transfers between devices with their start and end apart: 15, of which 6 were waited for; matrix products, arithmetic and copies ran while one was open for 2% of the time, Pallas kernels for 19%

profile of v7, /device:TPU:0, one launch (start us, length us, event | category | flops | bytes accessed | tf_op | source)
XLA Modules:
  0.0 61.0 jit_solution(4513474770004937819)
XLA Ops:
  0.6 6.4 %assemble.4 = (bf16[4,1,592,128]{3,2,1,0:T(8,128)(2,1)}, bf16[4,1,592,128]{3,2,1,0:T(8,128)(2,1)}, f32[1600,256]{1,0:T(8,128)}, s32[16,256]{1,0:T(8,128)}) custom-call(s32[8]{0:T(128)} %refs_0_.1, s32[1,192]{1,0:T(1,128)} %bitcast.82, s32[1,192]{1,0:T(1,128)} %bitcast.83, bf16[160,192]{1,0:T(8,128)(2,1)} %bitcast.78, bf16[32,192]{1,0:T(8,128)(2,1)} %bitcast.80, ...), custom_call_target="tpu_custom_call" | custom-call | flops 1000000000 | bytes 4000000 | tf_op jit(solution)/shard_map/assemble/pallas_call | solution.py:325
  7.0 0.5 collective-permute-start
  7.6 1.4 %copy-done.1 = f32[1600,256]{1,0:T(8,128)S(1)} copy-done((f32[1600,256]{1,0:T(8,128)S(1)}, f32[1600,256]{1,0:T(8,128)}, u32[]{:S(2)}) %copy-start.1) | copy-done | bytes 1638424
  9.0 0.7 %copy-done.3 = s32[16,256]{1,0:T(8,128)S(1)} copy-done((s32[16,256]{1,0:T(8,128)S(1)}, s32[16,256]{1,0:T(8,128)}, u32[]{:S(2)}) %copy-start.3) | copy-done | bytes 16408
  9.7 2.4 %assemble.5 = (bf16[4,1,592,128]{3,2,1,0:T(8,128)(2,1)S(1)}, bf16[4,1,592,128]{3,2,1,0:T(8,128)(2,1)S(1)}) custom-call(f32[1600,256]{1,0:T(8,128)S(1)} %copy-done.1, s32[16,256]{1,0:T(8,128)S(1)} %copy-done.3, bf16[192,32,128]{2,1,0:T(8,128)(2,1)S(1)} %copy-done), custom_call_target="tpu_custom_call" | custom-call | flops 1000000000 | bytes 4000000 | tf_op jit(solution)/shard_map/assemble/pallas_call | solution.py:325
  12.1 0.6 collective-permute-start.2
  12.7 0.0 collective-permute-done
  12.7 0.1 fusion
  12.8 2.5 %collective-permute-start.1 = (bf16[2,592,128]{2,1,0:T(8,128)(2,1)S(1)}, bf16[2,592,128]{2,1,0:T(8,128)(2,1)S(1)}, u32[]{:S(2)}, u32[]{:S(2)}) collective-permute-start(bf16[2,592,128]{2,1,0:T(8,128)(2,1)S(1)} %fusion), channel_id=1, source_target_pairs={{0,2},{1,5},{2,0},{3,7},{4,6},{5,1},{6,4},{7,3},{8,10},{9,13},{10,... | collective-permute-start | bytes 909320 | tf_op jit(solution)/shard_map/ppermute | solution.py:433
  15.3 5.6 %assemble.6 = (bf16[4,1,592,128]{3,2,1,0:T(8,128)(2,1)S(1)}, bf16[4,1,592,128]{3,2,1,0:T(8,128)(2,1)S(1)}) custom-call(f32[1600,256]{1,0:T(8,128)S(1)} %copy-done.2, s32[16,256]{1,0:T(8,128)S(1)} %copy-done.4, bf16[192,32,128]{2,1,0:T(8,128)(2,1)S(1)} %copy-done), custom_call_target="tpu_custom_call" | custom-call | flops 1000000000 | bytes 4000000 | tf_op jit(solution)/shard_map/assemble/pallas_call | solution.py:325
  21.0 0.0 collective-permute-done.2
  21.0 0.1 fusion.1
  21.1 0.1 collective-permute-start.6
  21.2 0.0 collective-permute-start.11
  21.2 0.0 collective-permute-done.1
  21.2 0.1 bitcast_add_fusion.3
  21.4 2.1 %collective-permute-start.8 = (bf16[592,128]{1,0:T(8,128)(2,1)S(1)}, bf16[592,128]{1,0:T(8,128)(2,1)S(1)}, u32[]{:S(2)}, u32[]{:S(2)}) collective-permute-start(bf16[592,128]{1,0:T(8,128)(2,1)S(1)} %fusion.12), channel_id=1, source_target_pairs={{0,4},{1,3},{2,6},{3,1},{4,0},{5,7},{6,2},{7,5},{8,12},{9,11},{10,... | collective-permute-start | bytes 454664 | tf_op jit(solution)/shard_map/ppermute | solution.py:433
  23.4 3.3 %assemble.7 = (bf16[4,1,592,128]{3,2,1,0:T(8,128)(2,1)S(1)}, bf16[4,1,592,128]{3,2,1,0:T(8,128)(2,1)S(1)}) custom-call(f32[1600,256]{1,0:T(8,128)S(1)} %copy-done.2, s32[16,256]{1,0:T(8,128)S(1)} %copy-done.4, bf16[192,32,128]{2,1,0:T(8,128)(2,1)S(1)} %copy-done), custom_call_target="tpu_custom_call" | custom-call | flops 1000000000 | bytes 4000000 | tf_op jit(solution)/shard_map/assemble/pallas_call | solution.py:325
  26.8 2.8 %collective-permute-done.6 = bf16[2,592,128]{2,1,0:T(8,128)(2,1)S(1)} collective-permute-done((bf16[2,592,128]{2,1,0:T(8,128)(2,1)S(1)}, bf16[2,592,128]{2,1,0:T(8,128)(2,1)S(1)}, u32[]{:S(2)}, u32[]{:S(2)}) %collective-permute-start.6) | collective-permute-done | bytes 303136 | tf_op jit(solution)/shard_map/ppermute | solution.py:433
  29.6 0.1 bitcast_add_fusion.1
  29.7 0.1 collective-permute-start.3
  29.8 1.6 %collective-permute-start.7 = (bf16[592,128]{1,0:T(8,128)(2,1)S(1)}, bf16[592,128]{1,0:T(8,128)(2,1)S(1)}, u32[]{:S(2)}, u32[]{:S(2)}) collective-permute-start(bf16[592,128]{1,0:T(8,128)(2,1)S(1)} %fusion.14), channel_id=1, source_target_pairs={{0,4},{1,3},{2,6},{3,1},{4,0},{5,7},{6,2},{7,5},{8,12},{9,11},{10,... | collective-permute-start | bytes 454664 | tf_op jit(solution)/shard_map/ppermute | solution.py:433
  31.4 0.0 collective-permute-done.8
  31.4 1.0 %collective-permute-start.9 = (bf16[592,128]{1,0:T(8,128)(2,1)S(1)}, bf16[592,128]{1,0:T(8,128)(2,1)S(1)}, u32[]{:S(2)}, u32[]{:S(2)}) collective-permute-start(bf16[592,128]{1,0:T(8,128)(2,1)S(1)} %fusion.7), channel_id=1, source_target_pairs={{0,8},{8,0},{16,24},{24,16},{1,9},{9,1},{17,25},{25,17},{2,10},{10... | collective-permute-start | bytes 454664 | tf_op jit(solution)/shard_map/ppermute | solution.py:436
  32.5 0.0 collective-permute-done.11
  32.5 0.1 fusion.3
  32.5 0.8 %collective-permute-start.12 = (bf16[2,592,128]{2,1,0:T(8,128)(2,1)S(1)}, bf16[2,592,128]{2,1,0:T(8,128)(2,1)S(1)}, u32[]{:S(2)}, u32[]{:S(2)}) collective-permute-start(bf16[2,592,128]{2,1,0:T(8,128)(2,1)S(1)} %fusion.3), channel_id=1, source_target_pairs={{0,2},{1,5},{2,0},{3,7},{4,6},{5,1},{6,4},{7,3},{8,10},{9,13},{10,... | collective-permute-start | bytes 909320 | tf_op jit(solution)/shard_map/ppermute | solution.py:433
  33.3 0.0 collective-permute-done.3
  33.3 0.1 fusion.2
  33.4 1.4 %collective-permute-start.4 = (bf16[2,592,128]{2,1,0:T(8,128)(2,1)S(1)}, bf16[2,592,128]{2,1,0:T(8,128)(2,1)S(1)}, u32[]{:S(2)}, u32[]{:S(2)}) collective-permute-start(bf16[2,592,128]{2,1,0:T(8,128)(2,1)S(1)} %fusion.2), channel_id=1, source_target_pairs={{0,2},{1,5},{2,0},{3,7},{4,6},{5,1},{6,4},{7,3},{8,10},{9,13},{10,... | collective-permute-start | bytes 909320 | tf_op jit(solution)/shard_map/ppermute | solution.py:433
  34.8 0.2 collective-permute-done.7
  35.0 2.4 %collective-permute-done.9 = bf16[592,128]{1,0:T(8,128)(2,1)S(1)} collective-permute-done((bf16[592,128]{1,0:T(8,128)(2,1)S(1)}, bf16[592,128]{1,0:T(8,128)(2,1)S(1)}, u32[]{:S(2)}, u32[]{:S(2)}) %collective-permute-start.9) | collective-permute-done | bytes 151584 | tf_op jit(solution)/shard_map/ppermute | solution.py:436
  37.4 0.1 fusion.10
  37.5 3.4 %collective-permute-start.10 = (bf16[592,128]{1,0:T(8,128)(2,1)S(1)}, bf16[592,128]{1,0:T(8,128)(2,1)S(1)}, u32[]{:S(2)}, u32[]{:S(2)}) collective-permute-start(bf16[592,128]{1,0:T(8,128)(2,1)S(1)} %fusion.10), channel_id=1, source_target_pairs={{0,16},{8,24},{16,0},{24,8},{1,17},{9,25},{17,1},{25,9},{2,18},{10... | collective-permute-start | bytes 454664 | tf_op jit(solution)/shard_map/ppermute | solution.py:436
  40.9 0.0 collective-permute-done.12
  40.9 0.1 bitcast_add_fusion
  41.0 1.8 %collective-permute-start.13 = (bf16[592,128]{1,0:T(8,128)(2,1)S(1)}, bf16[592,128]{1,0:T(8,128)(2,1)S(1)}, u32[]{:S(2)}, u32[]{:S(2)}) collective-permute-start(bf16[592,128]{1,0:T(8,128)(2,1)S(1)} %fusion.15), channel_id=1, source_target_pairs={{0,4},{1,3},{2,6},{3,1},{4,0},{5,7},{6,2},{7,5},{8,12},{9,11},{10,... | collective-permute-start | bytes 454664 | tf_op jit(solution)/shard_map/ppermute | solution.py:433
  42.9 0.0 collective-permute-done.4
  42.9 0.1 bitcast_add_fusion.2
  43.0 0.6 collective-permute-start.5
  43.6 2.7 %collective-permute-done.13 = bf16[592,128]{1,0:T(8,128)(2,1)S(1)} collective-permute-done((bf16[592,128]{1,0:T(8,128)(2,1)S(1)}, bf16[592,128]{1,0:T(8,128)(2,1)S(1)}, u32[]{:S(2)}, u32[]{:S(2)}) %collective-permute-start.13) | collective-permute-done | bytes 151584 | tf_op jit(solution)/shard_map/ppermute | solution.py:433
  46.3 1.4 %collective-permute-start.14 = (bf16[592,128]{1,0:T(8,128)(2,1)S(1)}, bf16[592,128]{1,0:T(8,128)(2,1)S(1)}, u32[]{:S(2)}, u32[]{:S(2)}) collective-permute-start(bf16[592,128]{1,0:T(8,128)(2,1)S(1)} %fusion.5), channel_id=1, source_target_pairs={{0,8},{8,0},{16,24},{24,16},{1,9},{9,1},{17,25},{25,17},{2,10},{10... | collective-permute-start | bytes 454664 | tf_op jit(solution)/shard_map/ppermute | solution.py:436
  47.7 0.5 collective-permute-done.5
  48.3 0.0 collective-permute-done.10.refs_0_
  48.3 3.3 %collective-permute-done.14.refs_1_ = bf16[592,128]{1,0:T(8,128)(2,1)S(1)} collective-permute-done((bf16[592,128]{1,0:T(8,128)(2,1)S(1)}, bf16[592,128]{1,0:T(8,128)(2,1)S(1)}, u32[]{:S(2)}, u32[]{:S(2)}) %collective-permute-start.14) | collective-permute-done | bytes 151584 | tf_op jit(solution)/shard_map/ppermute | solution.py:436
  51.6 0.1 gather.1
  51.6 8.4 %all_to_all.5.got_ref = bf16[8,64,128]{2,1,0:T(8,128)(2,1)S(1)} all-to-all(bf16[8,64,128]{2,1,0:T(8,128)(2,1)S(1)} %get-tuple-element.55), channel_id=1, replica_groups=mesh['region'=4,'tile'=8] {'tile'}, dimensions={0} | all-to-all | bytes 262144 | tf_op jit(solution)/shard_map/all_to_all | solution.py:502
  60.0 1.0 %finish.1 = (f32[128,1024]{1,0:T(8,128)}, f32[1,128]{1,0:T(1,128)}) custom-call(f32[592,128]{1,0:T(8,128)S(1)} %get-tuple-element.54.own_ref, bf16[8,64,128]{2,1,0:T(8,128)(2,1)S(1)} %all_to_all.5.got_ref), custom_call_target="tpu_custom_call" | custom-call | tf_op jit(solution)/shard_map/finish/pallas_call | solution.py:402
  (17 shorter events, 0.2 us)
Async XLA Ops:
  0.6 6.9 %copy-start = (bf16[192,32,128]{2,1,0:T(8,128)(2,1)S(1)}, bf16[192,32,128]{2,1,0:T(8,128)(2,1)}, u32[]{:S(2)}) copy-start(bf16[192,32,128]{2,1,0:T(8,128)(2,1)} %g_ref.5) | copy-start | bytes 4718596
  7.0 5.7 %collective-permute-start = (bf16[4,1,592,128]{3,2,0,1:T(8,128)(2,1)}, bf16[4,1,592,128]{3,2,0,1:T(8,128)(2,1)S(1)}, u32[]{:S(2)}, u32[]{:S(2)}) collective-permute-start(bf16[4,1,592,128]{3,2,0,1:T(8,128)(2,1)} %bitcast.76), channel_id=1, source_target_pairs={{0,1},{1,0},{2,3},{3,2},{4,5},{5,4},{6,7},{7,6},{8,9},{9,8},{10,11... | collective-permute-start | bytes 1818632 | tf_op jit(solution)/shard_map/ppermute | solution.py:433
  7.6 1.4 %copy-start.1 = (f32[1600,256]{1,0:T(8,128)S(1)}, f32[1600,256]{1,0:T(8,128)}, u32[]{:S(2)}) copy-start(f32[1600,256]{1,0:T(8,128)} %get-tuple-element.30.shared_ref) | copy-start | bytes 4915204
  9.0 0.7 %copy-start.3 = (s32[16,256]{1,0:T(8,128)S(1)}, s32[16,256]{1,0:T(8,128)}, u32[]{:S(2)}) copy-start(s32[16,256]{1,0:T(8,128)} %get-tuple-element.44.table_ref) | copy-start | bytes 49156
  9.7 3.0 %copy-start.5 = (bf16[4,1,592,128]{3,2,1,0:T(8,128)(2,1)S(1)}, bf16[4,1,592,128]{3,2,1,0:T(8,128)(2,1)}, u32[]{:S(2)}) copy-start(bf16[4,1,592,128]{3,2,1,0:T(8,128)(2,1)} %get-tuple-element.36) | copy-start | bytes 1818628
  9.7 5.6 %copy-start.2 = (f32[1600,256]{1,0:T(8,128)S(1)}, f32[1600,256]{1,0:T(8,128)}, u32[]{:S(2)}) copy-start(f32[1600,256]{1,0:T(8,128)} %get-tuple-element.30.shared_ref) | copy-start | bytes 4915204
  9.7 5.6 %copy-start.4 = (s32[16,256]{1,0:T(8,128)S(1)}, s32[16,256]{1,0:T(8,128)}, u32[]{:S(2)}) copy-start(s32[16,256]{1,0:T(8,128)} %get-tuple-element.44.table_ref) | copy-start | bytes 49156
  12.1 8.8 %collective-permute-start.2 = (bf16[4,1,592,128]{3,2,0,1:T(8,128)(2,1)S(1)}, bf16[4,1,592,128]{3,2,0,1:T(8,128)(2,1)S(1)}, u32[]{:S(2)}, u32[]{:S(2)}) collective-permute-start(bf16[4,1,592,128]{3,2,0,1:T(8,128)(2,1)S(1)} %bitcast.73), channel_id=1, source_target_pairs={{0,1},{1,0},{2,3},{3,2},{4,5},{5,4},{6,7},{7,6},{8,9},{9,8},{10,11... | collective-permute-start | bytes 1818632 | tf_op jit(solution)/shard_map/ppermute | solution.py:433
  12.8 8.4 %collective-permute-start.1 = (bf16[2,592,128]{2,1,0:T(8,128)(2,1)S(1)}, bf16[2,592,128]{2,1,0:T(8,128)(2,1)S(1)}, u32[]{:S(2)}, u32[]{:S(2)}) collective-permute-start(bf16[2,592,128]{2,1,0:T(8,128)(2,1)S(1)} %fusion), channel_id=1, source_target_pairs={{0,2},{1,5},{2,0},{3,7},{4,6},{5,1},{6,4},{7,3},{8,10},{9,13},{10,... | collective-permute-start | bytes 909320 | tf_op jit(solution)/shard_map/ppermute | solution.py:433
  21.1 8.5 %collective-permute-start.6 = (bf16[2,592,128]{2,1,0:T(8,128)(2,1)S(1)}, bf16[2,592,128]{2,1,0:T(8,128)(2,1)S(1)}, u32[]{:S(2)}, u32[]{:S(2)}) collective-permute-start(bf16[2,592,128]{2,1,0:T(8,128)(2,1)S(1)} %fusion.1), channel_id=1, source_target_pairs={{0,2},{1,5},{2,0},{3,7},{4,6},{5,1},{6,4},{7,3},{8,10},{9,13},{10,... | collective-permute-start | bytes 909320 | tf_op jit(solution)/shard_map/ppermute | solution.py:433
  21.2 11.2 %collective-permute-start.11 = (bf16[4,1,592,128]{3,2,0,1:T(8,128)(2,1)S(1)}, bf16[4,1,592,128]{3,2,0,1:T(8,128)(2,1)S(1)}, u32[]{:S(2)}, u32[]{:S(2)}) collective-permute-start(bf16[4,1,592,128]{3,2,0,1:T(8,128)(2,1)S(1)} %bitcast.71), channel_id=1, source_target_pairs={{0,1},{1,0},{2,3},{3,2},{4,5},{5,4},{6,7},{7,6},{8,9},{9,8},{10,11... | collective-permute-start | bytes 1818632 | tf_op jit(solution)/shard_map/ppermute | solution.py:433
  21.4 10.0 %collective-permute-start.8 = (bf16[592,128]{1,0:T(8,128)(2,1)S(1)}, bf16[592,128]{1,0:T(8,128)(2,1)S(1)}, u32[]{:S(2)}, u32[]{:S(2)}) collective-permute-start(bf16[592,128]{1,0:T(8,128)(2,1)S(1)} %fusion.12), channel_id=1, source_target_pairs={{0,4},{1,3},{2,6},{3,1},{4,0},{5,7},{6,2},{7,5},{8,12},{9,11},{10,... | collective-permute-start | bytes 454664 | tf_op jit(solution)/shard_map/ppermute | solution.py:433
  29.7 3.6 %collective-permute-start.3 = (bf16[4,1,592,128]{3,2,0,1:T(8,128)(2,1)S(1)}, bf16[4,1,592,128]{3,2,0,1:T(8,128)(2,1)S(1)}, u32[]{:S(2)}, u32[]{:S(2)}) collective-permute-start(bf16[4,1,592,128]{3,2,0,1:T(8,128)(2,1)S(1)} %bitcast.72), channel_id=1, source_target_pairs={{0,1},{1,0},{2,3},{3,2},{4,5},{5,4},{6,7},{7,6},{8,9},{9,8},{10,11... | collective-permute-start | bytes 1818632 | tf_op jit(solution)/shard_map/ppermute | solution.py:433
  29.8 5.3 %collective-permute-start.7 = (bf16[592,128]{1,0:T(8,128)(2,1)S(1)}, bf16[592,128]{1,0:T(8,128)(2,1)S(1)}, u32[]{:S(2)}, u32[]{:S(2)}) collective-permute-start(bf16[592,128]{1,0:T(8,128)(2,1)S(1)} %fusion.14), channel_id=1, source_target_pairs={{0,4},{1,3},{2,6},{3,1},{4,0},{5,7},{6,2},{7,5},{8,12},{9,11},{10,... | collective-permute-start | bytes 454664 | tf_op jit(solution)/shard_map/ppermute | solution.py:433
  31.4 6.0 %collective-permute-start.9 = (bf16[592,128]{1,0:T(8,128)(2,1)S(1)}, bf16[592,128]{1,0:T(8,128)(2,1)S(1)}, u32[]{:S(2)}, u32[]{:S(2)}) collective-permute-start(bf16[592,128]{1,0:T(8,128)(2,1)S(1)} %fusion.7), channel_id=1, source_target_pairs={{0,8},{8,0},{16,24},{24,16},{1,9},{9,1},{17,25},{25,17},{2,10},{10... | collective-permute-start | bytes 454664 | tf_op jit(solution)/shard_map/ppermute | solution.py:436
  32.5 8.4 %collective-permute-start.12 = (bf16[2,592,128]{2,1,0:T(8,128)(2,1)S(1)}, bf16[2,592,128]{2,1,0:T(8,128)(2,1)S(1)}, u32[]{:S(2)}, u32[]{:S(2)}) collective-permute-start(bf16[2,592,128]{2,1,0:T(8,128)(2,1)S(1)} %fusion.3), channel_id=1, source_target_pairs={{0,2},{1,5},{2,0},{3,7},{4,6},{5,1},{6,4},{7,3},{8,10},{9,13},{10,... | collective-permute-start | bytes 909320 | tf_op jit(solution)/shard_map/ppermute | solution.py:433
  33.4 9.5 %collective-permute-start.4 = (bf16[2,592,128]{2,1,0:T(8,128)(2,1)S(1)}, bf16[2,592,128]{2,1,0:T(8,128)(2,1)S(1)}, u32[]{:S(2)}, u32[]{:S(2)}) collective-permute-start(bf16[2,592,128]{2,1,0:T(8,128)(2,1)S(1)} %fusion.2), channel_id=1, source_target_pairs={{0,2},{1,5},{2,0},{3,7},{4,6},{5,1},{6,4},{7,3},{8,10},{9,13},{10,... | collective-permute-start | bytes 909320 | tf_op jit(solution)/shard_map/ppermute | solution.py:433
  37.5 10.8 %collective-permute-start.10 = (bf16[592,128]{1,0:T(8,128)(2,1)S(1)}, bf16[592,128]{1,0:T(8,128)(2,1)S(1)}, u32[]{:S(2)}, u32[]{:S(2)}) collective-permute-start(bf16[592,128]{1,0:T(8,128)(2,1)S(1)} %fusion.10), channel_id=1, source_target_pairs={{0,16},{8,24},{16,0},{24,8},{1,17},{9,25},{17,1},{25,9},{2,18},{10... | collective-permute-start | bytes 454664 | tf_op jit(solution)/shard_map/ppermute | solution.py:436
  41.0 5.3 %collective-permute-start.13 = (bf16[592,128]{1,0:T(8,128)(2,1)S(1)}, bf16[592,128]{1,0:T(8,128)(2,1)S(1)}, u32[]{:S(2)}, u32[]{:S(2)}) collective-permute-start(bf16[592,128]{1,0:T(8,128)(2,1)S(1)} %fusion.15), channel_id=1, source_target_pairs={{0,4},{1,3},{2,6},{3,1},{4,0},{5,7},{6,2},{7,5},{8,12},{9,11},{10,... | collective-permute-start | bytes 454664 | tf_op jit(solution)/shard_map/ppermute | solution.py:433
  43.0 5.3 %collective-permute-start.5 = (bf16[592,128]{1,0:T(8,128)(2,1)S(1)}, bf16[592,128]{1,0:T(8,128)(2,1)S(1)}, u32[]{:S(2)}, u32[]{:S(2)}) collective-permute-start(bf16[592,128]{1,0:T(8,128)(2,1)S(1)} %fusion.13), channel_id=1, source_target_pairs={{0,4},{1,3},{2,6},{3,1},{4,0},{5,7},{6,2},{7,5},{8,12},{9,11},{10,... | collective-permute-start | bytes 454664 | tf_op jit(solution)/shard_map/ppermute | solution.py:433
  46.3 5.3 %collective-permute-start.14 = (bf16[592,128]{1,0:T(8,128)(2,1)S(1)}, bf16[592,128]{1,0:T(8,128)(2,1)S(1)}, u32[]{:S(2)}, u32[]{:S(2)}) collective-permute-start(bf16[592,128]{1,0:T(8,128)(2,1)S(1)} %fusion.5), channel_id=1, source_target_pairs={{0,8},{8,0},{16,24},{24,16},{1,9},{9,1},{17,25},{25,17},{2,10},{10... | collective-permute-start | bytes 454664 | tf_op jit(solution)/shard_map/ppermute | solution.py:436

commit v8 on v4

--- a/solution.py
+++ b/solution.py
@@ -369,6 +369,33 @@
     vec_ref[...] = own_ref[tail : tail + 1, :] + own_ref[tail + 1 : tail + 2, :]
 
 
+def gather_kernel(number, own_ref, *refs):
+    crossed, total_ref, sends = refs[:number], refs[number], refs[number + 1 :]
+    width = own_ref.shape[1]
+    total = own_ref[...]
+    for ref in crossed:
+        total = total + ref[...].astype(F32)
+    total_ref[...] = total
+    for n, ref in enumerate(sends):
+        at = (n + 1) * width
+        ref[...] = total[at : at + ref.shape[0]].astype(BF16)
+
+
+def gather(own, crossed, blocks):
+    width = own.shape[1]
+    vmem = pl.BlockSpec(memory_space=pltpu.VMEM)
+    rows = [width] * (blocks // 2 - 1) + [width // 2]
+    return pl.pallas_call(
+        functools.partial(gather_kernel, len(crossed)),
+        in_specs=[vmem] * (1 + len(crossed)),
+        out_specs=[vmem] * (1 + len(rows)),
+        out_shape=[jax.ShapeDtypeStruct(own.shape, F32)]
+        + [jax.ShapeDtypeStruct((n, width), BF16) for n in rows],
+        compiler_params=pltpu.CompilerParams(vmem_limit_bytes=8 * 1024 * 1024),
+        name="gather",
+    )(own, *crossed)
+
+
 def finish(sub, own, r1, r2, r3, ext, blocks):
     width = own.shape[1]
     vmem = pl.BlockSpec(memory_space=pltpu.VMEM)
@@ -439,24 +466,30 @@
         elif slot == regions:
             done = both(cores[0], top)[:, 0].astype(BF16)
         k = regions - 1 - (slot - 3)
+
+        def lowered(k, done):
+            total = both(cores[k], low)[:, 0] + after(firsts[k], done).astype(F32)
+            seconds[k] = total[0], swap(total[1].astype(BF16), 4, 2)
+            return total[1].astype(BF16)
+
+        if slot > regions and k > 0:
+            done = lowered(k - 1, done)
         if 0 <= k < regions:
             total = seconds[k][0] + after(seconds[k][1], done).astype(F32)
-            for value in incoming[k]:
-                total = total + value.astype(F32)
             if k:
+                for value in incoming[k]:
+                    total = total + value.astype(F32)
                 operands.append(total.astype(BF16))
                 incoming[k - (k & -k)].append(across(operands[-1], k & -k))
             else:
                 own = total
         k -= 1
-        if 0 <= k < regions:
-            total = both(cores[k], low)[:, 0] + after(firsts[k], done).astype(F32)
-            operands.append(total[1].astype(BF16))
-            seconds[k] = total[0], swap(operands[-1], 4, 2)
+        if 0 <= k < regions and slot <= regions:
+            operands.append(lowered(k, (done, operands) if slot == regions else done))
         k -= 1
         if 0 <= k < regions:
             if slot < regions:
-                cores[k] = after(cores[k], done)
+                cores[k] = after(cores[k], (done, operands) if slot == regions - 1 else done)
             operands.append(both(cores[k], top)[:, 0].astype(BF16))
             firsts[k] = swap(operands[-1], 2, 4)
         if slot < regions:
@@ -467,15 +500,10 @@
         pairs = [
             (p * sub + s, ((p + d) % blocks) * sub + s) for p in range(blocks) for s in range(sub)
         ]
-        return lax.ppermute(value.astype(BF16), "tile", pairs)
-
-    matrix, vector = finish(
-        sub,
-        own,
-        *(onward(own[d * width : (d + 1) * width], d) for d in range(1, blocks // 2)),
-        onward(own[blocks // 2 * width : blocks // 2 * width + width // 2], blocks // 2),
-        blocks,
-    )
+        return lax.ppermute(value, "tile", pairs)
+
+    own, *sends = gather(own, incoming[0], blocks)
+    matrix, vector = finish(sub, own, *(onward(v, d + 1) for d, v in enumerate(sends)), blocks)
     if sub > 1:
         part = tile % sub
         rows = width // sub

time: 59.7 us -> 60.2 us (level)
  waiting for transfers between devices: 18.4 us -> 12.2 us
  starting transfers between devices: 17.8 us -> 23.8 us
    ppermute x12, starting transfers between devices: 9.42 us -> 15.3 us  [swap(): return lax.ppermute(value, 'tile', pairs)]
    ppermute x12, waiting for transfers between devices: 10.5 us -> 5.57 us  [swap(): return lax.ppermute(value, 'tile', pairs)]
    ppermute x4, starting transfers between devices: 2.54 us -> 3.3 us  [onward(): return lax.ppermute(value, 'tile', pairs)]
    ppermute x4, waiting for transfers between devices: 3.09 us -> 2.39 us  [onward(): return lax.ppermute(value, 'tile', pairs)]
    ppermute x3, starting transfers between devices: 5.87 us -> 5.21 us  [across(): lax.ppermute(value.astype(BF16), 'region', [(r, r ^ k) for r in range(reg...]
    ppermute x3, waiting for transfers between devices: 4.83 us -> 4.22 us  [across(): lax.ppermute(value.astype(BF16), 'region', [(r, r ^ k) for r in range(reg...]
  transfers between devices with their start and end apart: 19 -> 19, of which waited for: 8 -> 6; matrix products, arithmetic and copies ran while one was open for 2% -> 2% of each run, Pallas kernels for 16% -> 21%
where the time goes in v8:
time: 60.2 us; the launch traced here: 59.5 us
  starting transfers between devices  23.8 us (40%)
  Pallas kernels  19.6 us (33%)
  waiting for transfers between devices  12.2 us (20%)
  local copies, waits for them, and re-layouts  2.23 us (4%)
  other arithmetic  0.91 us (2%)
  between operations  0.82 us (1%)
    pallas_call x4, Pallas kernels, assemble(): pl.pallas_call(functools.partial(lead_kernel if lead else follow_kernel,...  18.6 us
    ppermute x12, starting transfers between devices, swap(): return lax.ppermute(value, 'tile', pairs)  15.3 us
    ppermute x12, waiting for transfers between devices, swap(): return lax.ppermute(value, 'tile', pairs)  5.57 us
    ppermute x3, starting transfers between devices, across(): lax.ppermute(value.astype(BF16), 'region', [(r, r ^ k) for r in range(reg...  5.21 us
    ppermute x3, waiting for transfers between devices, across(): lax.ppermute(value.astype(BF16), 'region', [(r, r ^ k) for r in range(reg...  4.22 us
    ppermute x4, starting transfers between devices, onward(): return lax.ppermute(value, 'tile', pairs)  3.3 us
    ppermute x4, waiting for transfers between devices, onward(): return lax.ppermute(value, 'tile', pairs)  2.39 us
    unnamed x12, local copies, waits for them, and re-layouts  2.16 us
  transfers between devices with their start and end apart: 19, of which 6 were waited for; matrix products, arithmetic and copies ran while one was open for 2% of the time, Pallas kernels for 21%

profile of v8, /device:TPU:0, one launch (start us, length us, event | category | flops | bytes accessed | tf_op | source)
XLA Modules:
  0.0 59.5 jit_solution(14540165356505786338)
XLA Ops:
  0.6 5.9 %assemble.4 = (bf16[4,1,592,128]{3,2,1,0:T(8,128)(2,1)}, bf16[4,1,592,128]{3,2,1,0:T(8,128)(2,1)}, f32[1600,256]{1,0:T(8,128)}, s32[16,256]{1,0:T(8,128)}) custom-call(s32[8]{0:T(128)} %refs_0_.1, s32[1,192]{1,0:T(1,128)} %bitcast.82, s32[1,192]{1,0:T(1,128)} %bitcast.83, bf16[160,192]{1,0:T(8,128)(2,1)} %bitcast.78, bf16[32,192]{1,0:T(8,128)(2,1)} %bitcast.80, ...), custom_call_target="tpu_custom_call" | custom-call | flops 1000000000 | bytes 4000000 | tf_op jit(solution)/shard_map/assemble/pallas_call | solution.py:321
  6.6 0.5 collective-permute-start
  7.1 1.4 %copy-done.1 = f32[1600,256]{1,0:T(8,128)S(1)} copy-done((f32[1600,256]{1,0:T(8,128)S(1)}, f32[1600,256]{1,0:T(8,128)}, u32[]{:S(2)}) %copy-start.1) | copy-done | bytes 1638424
  8.5 0.7 %copy-done.3 = s32[16,256]{1,0:T(8,128)S(1)} copy-done((s32[16,256]{1,0:T(8,128)S(1)}, s32[16,256]{1,0:T(8,128)}, u32[]{:S(2)}) %copy-start.3) | copy-done | bytes 16408
  9.2 5.6 %assemble.5 = (bf16[4,1,592,128]{3,2,1,0:T(8,128)(2,1)S(1)}, bf16[4,1,592,128]{3,2,1,0:T(8,128)(2,1)S(1)}) custom-call(f32[1600,256]{1,0:T(8,128)S(1)} %copy-done.1, s32[16,256]{1,0:T(8,128)S(1)} %copy-done.3, bf16[192,32,128]{2,1,0:T(8,128)(2,1)S(1)} %copy-done), custom_call_target="tpu_custom_call" | custom-call | flops 1000000000 | bytes 4000000 | tf_op jit(solution)/shard_map/assemble/pallas_call | solution.py:321
  14.9 0.1 collective-permute-start.2
  15.0 0.1 fusion
  15.1 3.0 %collective-permute-start.1 = (bf16[2,592,128]{2,1,0:T(8,128)(2,1)S(1)}, bf16[2,592,128]{2,1,0:T(8,128)(2,1)S(1)}, u32[]{:S(2)}, u32[]{:S(2)}) collective-permute-start(bf16[2,592,128]{2,1,0:T(8,128)(2,1)S(1)} %fusion), channel_id=1, source_target_pairs={{0,2},{1,5},{2,0},{3,7},{4,6},{5,1},{6,4},{7,3},{8,10},{9,13},{10,... | collective-permute-start | bytes 909320 | tf_op jit(solution)/shard_map/ppermute | solution.py:436
  18.1 2.4 %assemble.6 = (bf16[4,1,592,128]{3,2,1,0:T(8,128)(2,1)S(1)}, bf16[4,1,592,128]{3,2,1,0:T(8,128)(2,1)S(1)}) custom-call(f32[1600,256]{1,0:T(8,128)S(1)} %copy-done.2, s32[16,256]{1,0:T(8,128)S(1)} %copy-done.4, bf16[192,32,128]{2,1,0:T(8,128)(2,1)S(1)} %copy-done), custom_call_target="tpu_custom_call" | custom-call | flops 1000000000 | bytes 4000000 | tf_op jit(solution)/shard_map/assemble/pallas_call | solution.py:321
  20.5 0.0 collective-permute-done.2
  20.5 0.1 fusion.1
  20.6 0.5 collective-permute-start.6
  21.1 0.3 collective-permute-start.11
  21.4 1.4 %collective-permute-done.1 = bf16[2,592,128]{2,1,0:T(8,128)(2,1)S(1)} collective-permute-done((bf16[2,592,128]{2,1,0:T(8,128)(2,1)S(1)}, bf16[2,592,128]{2,1,0:T(8,128)(2,1)S(1)}, u32[]{:S(2)}, u32[]{:S(2)}) %collective-permute-start.1) | collective-permute-done | bytes 303136 | tf_op jit(solution)/shard_map/ppermute | solution.py:436
  22.9 0.1 bitcast_add_fusion.3
  23.0 2.1 %collective-permute-start.8 = (bf16[592,128]{1,0:T(8,128)(2,1)S(1)}, bf16[592,128]{1,0:T(8,128)(2,1)S(1)}, u32[]{:S(2)}, u32[]{:S(2)}) collective-permute-start(bf16[592,128]{1,0:T(8,128)(2,1)S(1)} %fusion.12), channel_id=1, source_target_pairs={{0,4},{1,3},{2,6},{3,1},{4,0},{5,7},{6,2},{7,5},{8,12},{9,11},{10,... | collective-permute-start | bytes 454664 | tf_op jit(solution)/shard_map/ppermute | solution.py:436
  25.1 4.7 %assemble.7 = (bf16[4,1,592,128]{3,2,1,0:T(8,128)(2,1)S(1)}, bf16[4,1,592,128]{3,2,1,0:T(8,128)(2,1)S(1)}) custom-call(f32[1600,256]{1,0:T(8,128)S(1)} %copy-done.2, s32[16,256]{1,0:T(8,128)S(1)} %copy-done.4, bf16[192,32,128]{2,1,0:T(8,128)(2,1)S(1)} %copy-done), custom_call_target="tpu_custom_call" | custom-call | flops 1000000000 | bytes 4000000 | tf_op jit(solution)/shard_map/assemble/pallas_call | solution.py:321
  29.8 0.1 bitcast_add_fusion.1
  30.0 0.1 collective-permute-start.3
  30.1 1.8 %collective-permute-start.7 = (bf16[592,128]{1,0:T(8,128)(2,1)S(1)}, bf16[592,128]{1,0:T(8,128)(2,1)S(1)}, u32[]{:S(2)}, u32[]{:S(2)}) collective-permute-start(bf16[592,128]{1,0:T(8,128)(2,1)S(1)} %fusion.14), channel_id=1, source_target_pairs={{0,4},{1,3},{2,6},{3,1},{4,0},{5,7},{6,2},{7,5},{8,12},{9,11},{10,... | collective-permute-start | bytes 454664 | tf_op jit(solution)/shard_map/ppermute | solution.py:436
  31.8 0.0 collective-permute-done.8
  31.9 1.7 %collective-permute-start.9 = (bf16[592,128]{1,0:T(8,128)(2,1)S(1)}, bf16[592,128]{1,0:T(8,128)(2,1)S(1)}, u32[]{:S(2)}, u32[]{:S(2)}) collective-permute-start(bf16[592,128]{1,0:T(8,128)(2,1)S(1)} %fusion.7), channel_id=1, source_target_pairs={{0,8},{8,0},{16,24},{24,16},{1,9},{9,1},{17,25},{25,17},{2,10},{10... | collective-permute-start | bytes 454664 | tf_op jit(solution)/shard_map/ppermute | solution.py:439
  33.5 0.1 fusion.3
  33.6 1.5 %collective-permute-start.12 = (bf16[2,592,128]{2,1,0:T(8,128)(2,1)S(1)}, bf16[2,592,128]{2,1,0:T(8,128)(2,1)S(1)}, u32[]{:S(2)}, u32[]{:S(2)}) collective-permute-start(bf16[2,592,128]{2,1,0:T(8,128)(2,1)S(1)} %fusion.3), channel_id=1, source_target_pairs={{0,2},{1,5},{2,0},{3,7},{4,6},{5,1},{6,4},{7,3},{8,10},{9,13},{10,... | collective-permute-start | bytes 909320 | tf_op jit(solution)/shard_map/ppermute | solution.py:436
  35.1 0.0 collective-permute-done.3
  35.1 0.1 fusion.2
  35.2 0.6 %collective-permute-start.4 = (bf16[2,592,128]{2,1,0:T(8,128)(2,1)S(1)}, bf16[2,592,128]{2,1,0:T(8,128)(2,1)S(1)}, u32[]{:S(2)}, u32[]{:S(2)}) collective-permute-start(bf16[2,592,128]{2,1,0:T(8,128)(2,1)S(1)} %fusion.2), channel_id=1, source_target_pairs={{0,2},{1,5},{2,0},{3,7},{4,6},{5,1},{6,4},{7,3},{8,10},{9,13},{10,... | collective-permute-start | bytes 909320 | tf_op jit(solution)/shard_map/ppermute | solution.py:436
  35.9 0.0 collective-permute-done.7
  35.9 2.1 %collective-permute-done.9 = bf16[592,128]{1,0:T(8,128)(2,1)S(1)} collective-permute-done((bf16[592,128]{1,0:T(8,128)(2,1)S(1)}, bf16[592,128]{1,0:T(8,128)(2,1)S(1)}, u32[]{:S(2)}, u32[]{:S(2)}) %collective-permute-start.9) | collective-permute-done | bytes 151584 | tf_op jit(solution)/shard_map/ppermute | solution.py:439
  38.0 0.1 fusion.10
  38.0 2.9 %collective-permute-start.10 = (bf16[592,128]{1,0:T(8,128)(2,1)S(1)}, bf16[592,128]{1,0:T(8,128)(2,1)S(1)}, u32[]{:S(2)}, u32[]{:S(2)}) collective-permute-start(bf16[592,128]{1,0:T(8,128)(2,1)S(1)} %fusion.10), channel_id=1, source_target_pairs={{0,16},{8,24},{16,0},{24,8},{1,17},{9,25},{17,1},{25,9},{2,18},{10... | collective-permute-start | bytes 454664 | tf_op jit(solution)/shard_map/ppermute | solution.py:439
  41.0 0.1 bitcast_add_fusion
  41.1 1.4 %collective-permute-start.13 = (bf16[592,128]{1,0:T(8,128)(2,1)S(1)}, bf16[592,128]{1,0:T(8,128)(2,1)S(1)}, u32[]{:S(2)}, u32[]{:S(2)}) collective-permute-start(bf16[592,128]{1,0:T(8,128)(2,1)S(1)} %fusion.15), channel_id=1, source_target_pairs={{0,4},{1,3},{2,6},{3,1},{4,0},{5,7},{6,2},{7,5},{8,12},{9,11},{10,... | collective-permute-start | bytes 454664 | tf_op jit(solution)/shard_map/ppermute | solution.py:436
  42.6 1.6 %collective-permute-done.4 = bf16[2,592,128]{2,1,0:T(8,128)(2,1)S(1)} collective-permute-done((bf16[2,592,128]{2,1,0:T(8,128)(2,1)S(1)}, bf16[2,592,128]{2,1,0:T(8,128)(2,1)S(1)}, u32[]{:S(2)}, u32[]{:S(2)}) %collective-permute-start.4) | collective-permute-done | bytes 303136 | tf_op jit(solution)/shard_map/ppermute | solution.py:436
  44.2 0.1 bitcast_add_fusion.2
  44.3 3.2 %collective-permute-start.5 = (bf16[592,128]{1,0:T(8,128)(2,1)S(1)}, bf16[592,128]{1,0:T(8,128)(2,1)S(1)}, u32[]{:S(2)}, u32[]{:S(2)}) collective-permute-start(bf16[592,128]{1,0:T(8,128)(2,1)S(1)} %fusion.13), channel_id=1, source_target_pairs={{0,4},{1,3},{2,6},{3,1},{4,0},{5,7},{6,2},{7,5},{8,12},{9,11},{10,... | collective-permute-start | bytes 454664 | tf_op jit(solution)/shard_map/ppermute | solution.py:436
  47.5 0.0 collective-permute-done.13
  47.6 0.6 %collective-permute-start.14 = (bf16[592,128]{1,0:T(8,128)(2,1)S(1)}, bf16[592,128]{1,0:T(8,128)(2,1)S(1)}, u32[]{:S(2)}, u32[]{:S(2)}) collective-permute-start(bf16[592,128]{1,0:T(8,128)(2,1)S(1)} %fusion.5), channel_id=1, source_target_pairs={{0,8},{8,0},{16,24},{24,16},{1,9},{9,1},{17,25},{25,17},{2,10},{10... | collective-permute-start | bytes 454664 | tf_op jit(solution)/shard_map/ppermute | solution.py:439
  48.2 2.5 %collective-permute-done.5 = bf16[592,128]{1,0:T(8,128)(2,1)S(1)} collective-permute-done((bf16[592,128]{1,0:T(8,128)(2,1)S(1)}, bf16[592,128]{1,0:T(8,128)(2,1)S(1)}, u32[]{:S(2)}, u32[]{:S(2)}) %collective-permute-start.5) | collective-permute-done | bytes 151584 | tf_op jit(solution)/shard_map/ppermute | solution.py:436
  50.7 2.1 %collective-permute-done.14.refs_1_ = bf16[592,128]{1,0:T(8,128)(2,1)S(1)} collective-permute-done((bf16[592,128]{1,0:T(8,128)(2,1)S(1)}, bf16[592,128]{1,0:T(8,128)(2,1)S(1)}, u32[]{:S(2)}, u32[]{:S(2)}) %collective-permute-start.14) | collective-permute-done | bytes 151584 | tf_op jit(solution)/shard_map/ppermute | solution.py:439
  52.8 0.1 gather.1
  52.9 0.1 collective-permute-start.15
  53.0 0.3 collective-permute-start.16
  53.3 1.4 %collective-permute-start.17 = (bf16[128,128]{1,0:T(8,128)(2,1)S(1)}, bf16[128,128]{1,0:T(8,128)(2,1)S(1)}, u32[]{:S(2)}, u32[]{:S(2)}) collective-permute-start(bf16[128,128]{1,0:T(8,128)(2,1)S(1)} %get-tuple-element.62), channel_id=1, source_target_pairs={{0,3},{1,4},{2,5},{3,6},{4,7},{5,0},{6,1},{7,2},{8,11},{9,12},{10,... | collective-permute-start | bytes 98312 | tf_op jit(solution)/shard_map/ppermute | solution.py:503
  54.7 1.5 %collective-permute-start.18 = (bf16[64,128]{1,0:T(8,128)(2,1)S(1)}, bf16[64,128]{1,0:T(8,128)(2,1)S(1)}, u32[]{:S(2)}, u32[]{:S(2)}) collective-permute-start(bf16[64,128]{1,0:T(8,128)(2,1)S(1)} %get-tuple-element.63), channel_id=1, source_target_pairs={{0,4},{1,5},{2,6},{3,7},{4,0},{5,1},{6,2},{7,3},{8,12},{9,13},{10,... | collective-permute-start | bytes 49160 | tf_op jit(solution)/shard_map/ppermute | solution.py:503
  56.2 2.4 %collective-permute-done.18.e_ref = bf16[64,128]{1,0:T(8,128)(2,1)S(1)} collective-permute-done((bf16[64,128]{1,0:T(8,128)(2,1)S(1)}, bf16[64,128]{1,0:T(8,128)(2,1)S(1)}, u32[]{:S(2)}, u32[]{:S(2)}) %collective-permute-start.18) | collective-permute-done | bytes 16416 | tf_op jit(solution)/shard_map/ppermute | solution.py:503
  58.6 0.0 collective-permute-done.15.r1_ref
  58.6 0.9 %finish.1 = (f32[128,1024]{1,0:T(8,128)}, f32[1,128]{1,0:T(1,128)}) custom-call(f32[592,128]{1,0:T(8,128)S(1)} %get-tuple-element.59.own_ref, bf16[128,128]{1,0:T(8,128)(2,1)S(1)} %collective-permute-done.15.r1_ref, bf16[128,128]{1,0:T(8,128)(2,1)S(1)} %collective-permute-done.16.r2_ref, bf16[128,128]{1,0:T(8,128)(2,1)S(1)} %collective-permute-done.17.r3_ref, ...), custom_call_target="tpu_custom_call" | custom-call | tf_op jit(solution)/shard_map/finish/pallas_call | solution.py:402
  (24 shorter events, 0.2 us)
Async XLA Ops:
  0.6 6.5 %copy-start = (bf16[192,32,128]{2,1,0:T(8,128)(2,1)S(1)}, bf16[192,32,128]{2,1,0:T(8,128)(2,1)}, u32[]{:S(2)}) copy-start(bf16[192,32,128]{2,1,0:T(8,128)(2,1)} %g_ref.5) | copy-start | bytes 4718596
  6.6 8.4 %collective-permute-start = (bf16[4,1,592,128]{3,2,0,1:T(8,128)(2,1)}, bf16[4,1,592,128]{3,2,0,1:T(8,128)(2,1)S(1)}, u32[]{:S(2)}, u32[]{:S(2)}) collective-permute-start(bf16[4,1,592,128]{3,2,0,1:T(8,128)(2,1)} %bitcast.76), channel_id=1, source_target_pairs={{0,1},{1,0},{2,3},{3,2},{4,5},{5,4},{6,7},{7,6},{8,9},{9,8},{10,11... | collective-permute-start | bytes 1818632 | tf_op jit(solution)/shard_map/ppermute | solution.py:436
  7.1 1.4 %copy-start.1 = (f32[1600,256]{1,0:T(8,128)S(1)}, f32[1600,256]{1,0:T(8,128)}, u32[]{:S(2)}) copy-start(f32[1600,256]{1,0:T(8,128)} %get-tuple-element.34.shared_ref) | copy-start | bytes 4915204
  8.5 0.7 %copy-start.3 = (s32[16,256]{1,0:T(8,128)S(1)}, s32[16,256]{1,0:T(8,128)}, u32[]{:S(2)}) copy-start(s32[16,256]{1,0:T(8,128)} %get-tuple-element.48.table_ref) | copy-start | bytes 49156
  9.2 5.8 %copy-start.5 = (bf16[4,1,592,128]{3,2,1,0:T(8,128)(2,1)S(1)}, bf16[4,1,592,128]{3,2,1,0:T(8,128)(2,1)}, u32[]{:S(2)}) copy-start(bf16[4,1,592,128]{3,2,1,0:T(8,128)(2,1)} %get-tuple-element.40) | copy-start | bytes 1818628
  9.2 8.8 %copy-start.2 = (f32[1600,256]{1,0:T(8,128)S(1)}, f32[1600,256]{1,0:T(8,128)}, u32[]{:S(2)}) copy-start(f32[1600,256]{1,0:T(8,128)} %get-tuple-element.34.shared_ref) | copy-start | bytes 4915204
  9.2 8.8 %copy-start.4 = (s32[16,256]{1,0:T(8,128)S(1)}, s32[16,256]{1,0:T(8,128)}, u32[]{:S(2)}) copy-start(s32[16,256]{1,0:T(8,128)} %get-tuple-element.48.table_ref) | copy-start | bytes 49156
  14.9 5.6 %collective-permute-start.2 = (bf16[4,1,592,128]{3,2,0,1:T(8,128)(2,1)S(1)}, bf16[4,1,592,128]{3,2,0,1:T(8,128)(2,1)S(1)}, u32[]{:S(2)}, u32[]{:S(2)}) collective-permute-start(bf16[4,1,592,128]{3,2,0,1:T(8,128)(2,1)S(1)} %bitcast.73), channel_id=1, source_target_pairs={{0,1},{1,0},{2,3},{3,2},{4,5},{5,4},{6,7},{7,6},{8,9},{9,8},{10,11... | collective-permute-start | bytes 1818632 | tf_op jit(solution)/shard_map/ppermute | solution.py:436
  15.1 7.8 %collective-permute-start.1 = (bf16[2,592,128]{2,1,0:T(8,128)(2,1)S(1)}, bf16[2,592,128]{2,1,0:T(8,128)(2,1)S(1)}, u32[]{:S(2)}, u32[]{:S(2)}) collective-permute-start(bf16[2,592,128]{2,1,0:T(8,128)(2,1)S(1)} %fusion), channel_id=1, source_target_pairs={{0,2},{1,5},{2,0},{3,7},{4,6},{5,1},{6,4},{7,3},{8,10},{9,13},{10,... | collective-permute-start | bytes 909320 | tf_op jit(solution)/shard_map/ppermute | solution.py:436
  20.6 9.2 %collective-permute-start.6 = (bf16[2,592,128]{2,1,0:T(8,128)(2,1)S(1)}, bf16[2,592,128]{2,1,0:T(8,128)(2,1)S(1)}, u32[]{:S(2)}, u32[]{:S(2)}) collective-permute-start(bf16[2,592,128]{2,1,0:T(8,128)(2,1)S(1)} %fusion.1), channel_id=1, source_target_pairs={{0,2},{1,5},{2,0},{3,7},{4,6},{5,1},{6,4},{7,3},{8,10},{9,13},{10,... | collective-permute-start | bytes 909320 | tf_op jit(solution)/shard_map/ppermute | solution.py:436
  21.1 12.4 %collective-permute-start.11 = (bf16[4,1,592,128]{3,2,0,1:T(8,128)(2,1)S(1)}, bf16[4,1,592,128]{3,2,0,1:T(8,128)(2,1)S(1)}, u32[]{:S(2)}, u32[]{:S(2)}) collective-permute-start(bf16[4,1,592,128]{3,2,0,1:T(8,128)(2,1)S(1)} %bitcast.71), channel_id=1, source_target_pairs={{0,1},{1,0},{2,3},{3,2},{4,5},{5,4},{6,7},{7,6},{8,9},{9,8},{10,11... | collective-permute-start | bytes 1818632 | tf_op jit(solution)/shard_map/ppermute | solution.py:436
  23.0 8.8 %collective-permute-start.8 = (bf16[592,128]{1,0:T(8,128)(2,1)S(1)}, bf16[592,128]{1,0:T(8,128)(2,1)S(1)}, u32[]{:S(2)}, u32[]{:S(2)}) collective-permute-start(bf16[592,128]{1,0:T(8,128)(2,1)S(1)} %fusion.12), channel_id=1, source_target_pairs={{0,4},{1,3},{2,6},{3,1},{4,0},{5,7},{6,2},{7,5},{8,12},{9,11},{10,... | collective-permute-start | bytes 454664 | tf_op jit(solution)/shard_map/ppermute | solution.py:436
  30.0 5.2 %collective-permute-start.3 = (bf16[4,1,592,128]{3,2,0,1:T(8,128)(2,1)S(1)}, bf16[4,1,592,128]{3,2,0,1:T(8,128)(2,1)S(1)}, u32[]{:S(2)}, u32[]{:S(2)}) collective-permute-start(bf16[4,1,592,128]{3,2,0,1:T(8,128)(2,1)S(1)} %bitcast.72), channel_id=1, source_target_pairs={{0,1},{1,0},{2,3},{3,2},{4,5},{5,4},{6,7},{7,6},{8,9},{9,8},{10,11... | collective-permute-start | bytes 1818632 | tf_op jit(solution)/shard_map/ppermute | solution.py:436
  30.1 5.8 %collective-permute-start.7 = (bf16[592,128]{1,0:T(8,128)(2,1)S(1)}, bf16[592,128]{1,0:T(8,128)(2,1)S(1)}, u32[]{:S(2)}, u32[]{:S(2)}) collective-permute-start(bf16[592,128]{1,0:T(8,128)(2,1)S(1)} %fusion.14), channel_id=1, source_target_pairs={{0,4},{1,3},{2,6},{3,1},{4,0},{5,7},{6,2},{7,5},{8,12},{9,11},{10,... | collective-permute-start | bytes 454664 | tf_op jit(solution)/shard_map/ppermute | solution.py:436
  31.9 6.1 %collective-permute-start.9 = (bf16[592,128]{1,0:T(8,128)(2,1)S(1)}, bf16[592,128]{1,0:T(8,128)(2,1)S(1)}, u32[]{:S(2)}, u32[]{:S(2)}) collective-permute-start(bf16[592,128]{1,0:T(8,128)(2,1)S(1)} %fusion.7), channel_id=1, source_target_pairs={{0,8},{8,0},{16,24},{24,16},{1,9},{9,1},{17,25},{25,17},{2,10},{10... | collective-permute-start | bytes 454664 | tf_op jit(solution)/shard_map/ppermute | solution.py:439
  33.6 7.4 %collective-permute-start.12 = (bf16[2,592,128]{2,1,0:T(8,128)(2,1)S(1)}, bf16[2,592,128]{2,1,0:T(8,128)(2,1)S(1)}, u32[]{:S(2)}, u32[]{:S(2)}) collective-permute-start(bf16[2,592,128]{2,1,0:T(8,128)(2,1)S(1)} %fusion.3), channel_id=1, source_target_pairs={{0,2},{1,5},{2,0},{3,7},{4,6},{5,1},{6,4},{7,3},{8,10},{9,13},{10,... | collective-permute-start | bytes 909320 | tf_op jit(solution)/shard_map/ppermute | solution.py:436
  35.2 9.0 %collective-permute-start.4 = (bf16[2,592,128]{2,1,0:T(8,128)(2,1)S(1)}, bf16[2,592,128]{2,1,0:T(8,128)(2,1)S(1)}, u32[]{:S(2)}, u32[]{:S(2)}) collective-permute-start(bf16[2,592,128]{2,1,0:T(8,128)(2,1)S(1)} %fusion.2), channel_id=1, source_target_pairs={{0,2},{1,5},{2,0},{3,7},{4,6},{5,1},{6,4},{7,3},{8,10},{9,13},{10,... | collective-permute-start | bytes 909320 | tf_op jit(solution)/shard_map/ppermute | solution.py:436
  38.0 12.7 %collective-permute-start.10 = (bf16[592,128]{1,0:T(8,128)(2,1)S(1)}, bf16[592,128]{1,0:T(8,128)(2,1)S(1)}, u32[]{:S(2)}, u32[]{:S(2)}) collective-permute-start(bf16[592,128]{1,0:T(8,128)(2,1)S(1)} %fusion.10), channel_id=1, source_target_pairs={{0,16},{8,24},{16,0},{24,8},{1,17},{9,25},{17,1},{25,9},{2,18},{10... | collective-permute-start | bytes 454664 | tf_op jit(solution)/shard_map/ppermute | solution.py:439
  41.1 6.4 %collective-permute-start.13 = (bf16[592,128]{1,0:T(8,128)(2,1)S(1)}, bf16[592,128]{1,0:T(8,128)(2,1)S(1)}, u32[]{:S(2)}, u32[]{:S(2)}) collective-permute-start(bf16[592,128]{1,0:T(8,128)(2,1)S(1)} %fusion.15), channel_id=1, source_target_pairs={{0,4},{1,3},{2,6},{3,1},{4,0},{5,7},{6,2},{7,5},{8,12},{9,11},{10,... | collective-permute-start | bytes 454664 | tf_op jit(solution)/shard_map/ppermute | solution.py:436
  44.3 6.4 %collective-permute-start.5 = (bf16[592,128]{1,0:T(8,128)(2,1)S(1)}, bf16[592,128]{1,0:T(8,128)(2,1)S(1)}, u32[]{:S(2)}, u32[]{:S(2)}) collective-permute-start(bf16[592,128]{1,0:T(8,128)(2,1)S(1)} %fusion.13), channel_id=1, source_target_pairs={{0,4},{1,3},{2,6},{3,1},{4,0},{5,7},{6,2},{7,5},{8,12},{9,11},{10,... | collective-permute-start | bytes 454664 | tf_op jit(solution)/shard_map/ppermute | solution.py:436
  47.6 5.3 %collective-permute-start.14 = (bf16[592,128]{1,0:T(8,128)(2,1)S(1)}, bf16[592,128]{1,0:T(8,128)(2,1)S(1)}, u32[]{:S(2)}, u32[]{:S(2)}) collective-permute-start(bf16[592,128]{1,0:T(8,128)(2,1)S(1)} %fusion.5), channel_id=1, source_target_pairs={{0,8},{8,0},{16,24},{24,16},{1,9},{9,1},{17,25},{25,17},{2,10},{10... | collective-permute-start | bytes 454664 | tf_op jit(solution)/shard_map/ppermute | solution.py:439
  52.9 5.7 %collective-permute-start.15 = (bf16[128,128]{1,0:T(8,128)(2,1)S(1)}, bf16[128,128]{1,0:T(8,128)(2,1)S(1)}, u32[]{:S(2)}, u32[]{:S(2)}) collective-permute-start(bf16[128,128]{1,0:T(8,128)(2,1)S(1)} %get-tuple-element.60), channel_id=1, source_target_pairs={{0,1},{1,2},{2,3},{3,4},{4,5},{5,6},{6,7},{7,0},{8,9},{9,10},{10,1... | collective-permute-start | bytes 98312 | tf_op jit(solution)/shard_map/ppermute | solution.py:503
  53.0 5.6 %collective-permute-start.16 = (bf16[128,128]{1,0:T(8,128)(2,1)S(1)}, bf16[128,128]{1,0:T(8,128)(2,1)S(1)}, u32[]{:S(2)}, u32[]{:S(2)}) collective-permute-start(bf16[128,128]{1,0:T(8,128)(2,1)S(1)} %get-tuple-element.61), channel_id=1, source_target_pairs={{0,2},{1,3},{2,4},{3,5},{4,6},{5,7},{6,0},{7,1},{8,10},{9,11},{10,... | collective-permute-start | bytes 98312 | tf_op jit(solution)/shard_map/ppermute | solution.py:503
  53.3 5.3 %collective-permute-start.17 = (bf16[128,128]{1,0:T(8,128)(2,1)S(1)}, bf16[128,128]{1,0:T(8,128)(2,1)S(1)}, u32[]{:S(2)}, u32[]{:S(2)}) collective-permute-start(bf16[128,128]{1,0:T(8,128)(2,1)S(1)} %get-tuple-element.62), channel_id=1, source_target_pairs={{0,3},{1,4},{2,5},{3,6},{4,7},{5,0},{6,1},{7,2},{8,11},{9,12},{10,... | collective-permute-start | bytes 98312 | tf_op jit(solution)/shard_map/ppermute | solution.py:503
  54.7 3.9 %collective-permute-start.18 = (bf16[64,128]{1,0:T(8,128)(2,1)S(1)}, bf16[64,128]{1,0:T(8,128)(2,1)S(1)}, u32[]{:S(2)}, u32[]{:S(2)}) collective-permute-start(bf16[64,128]{1,0:T(8,128)(2,1)S(1)} %get-tuple-element.63), channel_id=1, source_target_pairs={{0,4},{1,5},{2,6},{3,7},{4,0},{5,1},{6,2},{7,3},{8,12},{9,13},{10,... | collective-permute-start | bytes 49160 | tf_op jit(solution)/shard_map/ppermute | solution.py:503

commit v9 on v8

--- a/solution.py
+++ b/solution.py
@@ -464,6 +464,7 @@
             inputs = tuple(made) if made else inputs
             done = send
         elif slot == regions:
+            cores[0] = after(cores[0], seconds[2][1])
             done = both(cores[0], top)[:, 0].astype(BF16)
         k = regions - 1 - (slot - 3)
 
@@ -473,7 +474,7 @@
             return total[1].astype(BF16)
 
         if slot > regions and k > 0:
-            done = lowered(k - 1, done)
+            lowered(k - 1, done)
         if 0 <= k < regions:
             total = seconds[k][0] + after(seconds[k][1], done).astype(F32)
             if k:

time: 60.2 us -> 60.7 us (level)
    ppermute x12, starting transfers between devices: 15.3 us -> 11.9 us  [swap(): return lax.ppermute(value, 'tile', pairs)]
    ppermute x3, starting transfers between devices: 5.21 us -> 8.39 us  [across(): lax.ppermute(value.astype(BF16), 'region', [(r, r ^ k) for r in range(reg...]
    ppermute x3, waiting for transfers between devices: 4.22 us -> 2.09 us  [across(): lax.ppermute(value.astype(BF16), 'region', [(r, r ^ k) for r in range(reg...]
    ppermute x12, waiting for transfers between devices: 5.57 us -> 7.62 us  [swap(): return lax.ppermute(value, 'tile', pairs)]
  transfers between devices with their start and end apart: 19 -> 19, of which waited for: 6 -> 9; matrix products, arithmetic and copies ran while one was open for 2% -> 2% of each run, Pallas kernels for 21% -> 18%
where the time goes in v9:
time: 60.7 us; the launch traced here: 59.6 us
  starting transfers between devices  23.6 us (39%)
  Pallas kernels  19.6 us (32%)
  waiting for transfers between devices  12.4 us (20%)
  local copies, waits for them, and re-layouts  2.23 us (4%)
  other arithmetic  0.9 us (1%)
  between operations  0.83 us (1%)
    pallas_call x4, Pallas kernels, assemble(): pl.pallas_call(functools.partial(lead_kernel if lead else follow_kernel,...  18.7 us
    ppermute x12, starting transfers between devices, swap(): return lax.ppermute(value, 'tile', pairs)  11.9 us
    ppermute x3, starting transfers between devices, across(): lax.ppermute(value.astype(BF16), 'region', [(r, r ^ k) for r in range(reg...  8.39 us
    ppermute x12, waiting for transfers between devices, swap(): return lax.ppermute(value, 'tile', pairs)  7.62 us
    ppermute x4, starting transfers between devices, onward(): return lax.ppermute(value, 'tile', pairs)  3.28 us
    ppermute x4, waiting for transfers between devices, onward(): return lax.ppermute(value, 'tile', pairs)  2.71 us
    unnamed x12, local copies, waits for them, and re-layouts  2.16 us
    ppermute x3, waiting for transfers between devices, across(): lax.ppermute(value.astype(BF16), 'region', [(r, r ^ k) for r in range(reg...  2.09 us
  transfers between devices with their start and end apart: 19, of which 9 were waited for; matrix products, arithmetic and copies ran while one was open for 2% of the time, Pallas kernels for 18%

profile of v9, /device:TPU:0, one launch (start us, length us, event | category | flops | bytes accessed | tf_op | source)
XLA Modules:
  0.0 59.6 jit_solution(14074386805071790721)
XLA Ops:
  0.6 7.8 %assemble.4 = (bf16[4,1,592,128]{3,2,1,0:T(8,128)(2,1)}, bf16[4,1,592,128]{3,2,1,0:T(8,128)(2,1)}, f32[1600,256]{1,0:T(8,128)}, s32[16,256]{1,0:T(8,128)}) custom-call(s32[8]{0:T(128)} %refs_0_.1, s32[1,192]{1,0:T(1,128)} %bitcast.82, s32[1,192]{1,0:T(1,128)} %bitcast.83, bf16[160,192]{1,0:T(8,128)(2,1)} %bitcast.78, bf16[32,192]{1,0:T(8,128)(2,1)} %bitcast.80, ...), custom_call_target="tpu_custom_call" | custom-call | flops 1000000000 | bytes 4000000 | tf_op jit(solution)/shard_map/assemble/pallas_call | solution.py:321
  8.4 0.5 collective-permute-start
  9.0 1.4 %copy-done.1 = f32[1600,256]{1,0:T(8,128)S(1)} copy-done((f32[1600,256]{1,0:T(8,128)S(1)}, f32[1600,256]{1,0:T(8,128)}, u32[]{:S(2)}) %copy-start.1) | copy-done | bytes 1638424
  10.4 0.7 %copy-done.3 = s32[16,256]{1,0:T(8,128)S(1)} copy-done((s32[16,256]{1,0:T(8,128)S(1)}, s32[16,256]{1,0:T(8,128)}, u32[]{:S(2)}) %copy-start.3) | copy-done | bytes 16408
  11.1 2.9 %assemble.5 = (bf16[4,1,592,128]{3,2,1,0:T(8,128)(2,1)S(1)}, bf16[4,1,592,128]{3,2,1,0:T(8,128)(2,1)S(1)}) custom-call(f32[1600,256]{1,0:T(8,128)S(1)} %copy-done.1, s32[16,256]{1,0:T(8,128)S(1)} %copy-done.3, bf16[192,32,128]{2,1,0:T(8,128)(2,1)S(1)} %copy-done), custom_call_target="tpu_custom_call" | custom-call | flops 1000000000 | bytes 4000000 | tf_op jit(solution)/shard_map/assemble/pallas_call | solution.py:321
  14.0 0.1 collective-permute-start.2
  14.1 0.1 fusion
  14.2 1.6 %collective-permute-start.1 = (bf16[2,592,128]{2,1,0:T(8,128)(2,1)S(1)}, bf16[2,592,128]{2,1,0:T(8,128)(2,1)S(1)}, u32[]{:S(2)}, u32[]{:S(2)}) collective-permute-start(bf16[2,592,128]{2,1,0:T(8,128)(2,1)S(1)} %fusion), channel_id=1, source_target_pairs={{0,2},{1,5},{2,0},{3,7},{4,6},{5,1},{6,4},{7,3},{8,10},{9,13},{10,... | collective-permute-start | bytes 909320 | tf_op jit(solution)/shard_map/ppermute | solution.py:436
  15.8 2.4 %assemble.6 = (bf16[4,1,592,128]{3,2,1,0:T(8,128)(2,1)S(1)}, bf16[4,1,592,128]{3,2,1,0:T(8,128)(2,1)S(1)}) custom-call(f32[1600,256]{1,0:T(8,128)S(1)} %copy-done.2, s32[16,256]{1,0:T(8,128)S(1)} %copy-done.4, bf16[192,32,128]{2,1,0:T(8,128)(2,1)S(1)} %copy-done), custom_call_target="tpu_custom_call" | custom-call | flops 1000000000 | bytes 4000000 | tf_op jit(solution)/shard_map/assemble/pallas_call | solution.py:321
  18.2 0.0 collective-permute-done.2
  18.2 0.1 fusion.1
  18.3 1.0 %collective-permute-start.4 = (bf16[2,592,128]{2,1,0:T(8,128)(2,1)S(1)}, bf16[2,592,128]{2,1,0:T(8,128)(2,1)S(1)}, u32[]{:S(2)}, u32[]{:S(2)}) collective-permute-start(bf16[2,592,128]{2,1,0:T(8,128)(2,1)S(1)} %fusion.1), channel_id=1, source_target_pairs={{0,2},{1,5},{2,0},{3,7},{4,6},{5,1},{6,4},{7,3},{8,10},{9,13},{10,... | collective-permute-start | bytes 909320 | tf_op jit(solution)/shard_map/ppermute | solution.py:436
  19.3 1.0 %collective-permute-start.11 = (bf16[4,1,592,128]{3,2,0,1:T(8,128)(2,1)S(1)}, bf16[4,1,592,128]{3,2,0,1:T(8,128)(2,1)S(1)}, u32[]{:S(2)}, u32[]{:S(2)}) collective-permute-start(bf16[4,1,592,128]{3,2,0,1:T(8,128)(2,1)S(1)} %bitcast.71), channel_id=1, source_target_pairs={{0,1},{1,0},{2,3},{3,2},{4,5},{5,4},{6,7},{7,6},{8,9},{9,8},{10,11... | collective-permute-start | bytes 1818632 | tf_op jit(solution)/shard_map/ppermute | solution.py:436
  20.3 0.7 %collective-permute-done.1 = bf16[2,592,128]{2,1,0:T(8,128)(2,1)S(1)} collective-permute-done((bf16[2,592,128]{2,1,0:T(8,128)(2,1)S(1)}, bf16[2,592,128]{2,1,0:T(8,128)(2,1)S(1)}, u32[]{:S(2)}, u32[]{:S(2)}) %collective-permute-start.1) | collective-permute-done | bytes 303136 | tf_op jit(solution)/shard_map/ppermute | solution.py:436
  21.1 0.1 bitcast_add_fusion.3
  21.2 2.8 %collective-permute-start.8 = (bf16[592,128]{1,0:T(8,128)(2,1)S(1)}, bf16[592,128]{1,0:T(8,128)(2,1)S(1)}, u32[]{:S(2)}, u32[]{:S(2)}) collective-permute-start(bf16[592,128]{1,0:T(8,128)(2,1)S(1)} %fusion.12), channel_id=1, source_target_pairs={{0,4},{1,3},{2,6},{3,1},{4,0},{5,7},{6,2},{7,5},{8,12},{9,11},{10,... | collective-permute-start | bytes 454664 | tf_op jit(solution)/shard_map/ppermute | solution.py:436
  24.0 5.6 %assemble.7 = (bf16[4,1,592,128]{3,2,1,0:T(8,128)(2,1)S(1)}, bf16[4,1,592,128]{3,2,1,0:T(8,128)(2,1)S(1)}) custom-call(f32[1600,256]{1,0:T(8,128)S(1)} %copy-done.2, s32[16,256]{1,0:T(8,128)S(1)} %copy-done.4, bf16[192,32,128]{2,1,0:T(8,128)(2,1)S(1)} %copy-done), custom_call_target="tpu_custom_call" | custom-call | flops 1000000000 | bytes 4000000 | tf_op jit(solution)/shard_map/assemble/pallas_call | solution.py:321
  29.6 0.0 collective-permute-done.4
  29.6 0.1 bitcast_add_fusion.2
  29.7 0.1 collective-permute-start.3
  29.8 0.7 %collective-permute-start.5 = (bf16[592,128]{1,0:T(8,128)(2,1)S(1)}, bf16[592,128]{1,0:T(8,128)(2,1)S(1)}, u32[]{:S(2)}, u32[]{:S(2)}) collective-permute-start(bf16[592,128]{1,0:T(8,128)(2,1)S(1)} %fusion.13), channel_id=1, source_target_pairs={{0,4},{1,3},{2,6},{3,1},{4,0},{5,7},{6,2},{7,5},{8,12},{9,11},{10,... | collective-permute-start | bytes 454664 | tf_op jit(solution)/shard_map/ppermute | solution.py:436
  30.5 0.0 collective-permute-done.8
  30.6 2.9 %collective-permute-start.9 = (bf16[592,128]{1,0:T(8,128)(2,1)S(1)}, bf16[592,128]{1,0:T(8,128)(2,1)S(1)}, u32[]{:S(2)}, u32[]{:S(2)}) collective-permute-start(bf16[592,128]{1,0:T(8,128)(2,1)S(1)} %fusion.7), channel_id=1, source_target_pairs={{0,8},{8,0},{16,24},{24,16},{1,9},{9,1},{17,25},{25,17},{2,10},{10... | collective-permute-start | bytes 454664 | tf_op jit(solution)/shard_map/ppermute | solution.py:439
  33.5 0.1 fusion.3
  33.6 0.6 collective-permute-start.12
  34.1 1.0 %collective-permute-done.5 = bf16[592,128]{1,0:T(8,128)(2,1)S(1)} collective-permute-done((bf16[592,128]{1,0:T(8,128)(2,1)S(1)}, bf16[592,128]{1,0:T(8,128)(2,1)S(1)}, u32[]{:S(2)}, u32[]{:S(2)}) %collective-permute-start.5) | collective-permute-done | bytes 151584 | tf_op jit(solution)/shard_map/ppermute | solution.py:436
  35.1 0.1 fusion.2
  35.2 2.1 %collective-permute-start.6 = (bf16[2,592,128]{2,1,0:T(8,128)(2,1)S(1)}, bf16[2,592,128]{2,1,0:T(8,128)(2,1)S(1)}, u32[]{:S(2)}, u32[]{:S(2)}) collective-permute-start(bf16[2,592,128]{2,1,0:T(8,128)(2,1)S(1)} %fusion.2), channel_id=1, source_target_pairs={{0,2},{1,5},{2,0},{3,7},{4,6},{5,1},{6,4},{7,3},{8,10},{9,13},{10,... | collective-permute-start | bytes 909320 | tf_op jit(solution)/shard_map/ppermute | solution.py:436
  37.3 0.5 collective-permute-done.9
  37.8 0.1 fusion.10
  37.9 1.9 %collective-permute-start.10 = (bf16[592,128]{1,0:T(8,128)(2,1)S(1)}, bf16[592,128]{1,0:T(8,128)(2,1)S(1)}, u32[]{:S(2)}, u32[]{:S(2)}) collective-permute-start(bf16[592,128]{1,0:T(8,128)(2,1)S(1)} %fusion.10), channel_id=1, source_target_pairs={{0,16},{8,24},{16,0},{24,8},{1,17},{9,25},{17,1},{25,9},{2,18},{10... | collective-permute-start | bytes 454664 | tf_op jit(solution)/shard_map/ppermute | solution.py:439
  39.8 0.6 %collective-permute-done.12 = bf16[2,592,128]{2,1,0:T(8,128)(2,1)S(1)} collective-permute-done((bf16[2,592,128]{2,1,0:T(8,128)(2,1)S(1)}, bf16[2,592,128]{2,1,0:T(8,128)(2,1)S(1)}, u32[]{:S(2)}, u32[]{:S(2)}) %collective-permute-start.12) | collective-permute-done | bytes 303136 | tf_op jit(solution)/shard_map/ppermute | solution.py:436
  40.4 0.1 bitcast_add_fusion
  40.6 1.3 %collective-permute-start.13 = (bf16[592,128]{1,0:T(8,128)(2,1)S(1)}, bf16[592,128]{1,0:T(8,128)(2,1)S(1)}, u32[]{:S(2)}, u32[]{:S(2)}) collective-permute-start(bf16[592,128]{1,0:T(8,128)(2,1)S(1)} %fusion.15), channel_id=1, source_target_pairs={{0,4},{1,3},{2,6},{3,1},{4,0},{5,7},{6,2},{7,5},{8,12},{9,11},{10,... | collective-permute-start | bytes 454664 | tf_op jit(solution)/shard_map/ppermute | solution.py:436
  41.9 3.7 %collective-permute-done.6 = bf16[2,592,128]{2,1,0:T(8,128)(2,1)S(1)} collective-permute-done((bf16[2,592,128]{2,1,0:T(8,128)(2,1)S(1)}, bf16[2,592,128]{2,1,0:T(8,128)(2,1)S(1)}, u32[]{:S(2)}, u32[]{:S(2)}) %collective-permute-start.6) | collective-permute-done | bytes 303136 | tf_op jit(solution)/shard_map/ppermute | solution.py:436
  45.6 0.1 bitcast_add_fusion.1
  45.7 0.1 collective-permute-start.7
  45.8 0.1 collective-permute-done.13
  45.9 3.6 %collective-permute-start.14 = (bf16[592,128]{1,0:T(8,128)(2,1)S(1)}, bf16[592,128]{1,0:T(8,128)(2,1)S(1)}, u32[]{:S(2)}, u32[]{:S(2)}) collective-permute-start(bf16[592,128]{1,0:T(8,128)(2,1)S(1)} %fusion.5), channel_id=1, source_target_pairs={{0,8},{8,0},{16,24},{24,16},{1,9},{9,1},{17,25},{25,17},{2,10},{10... | collective-permute-start | bytes 454664 | tf_op jit(solution)/shard_map/ppermute | solution.py:439
  49.4 1.5 %collective-permute-done.7 = bf16[592,128]{1,0:T(8,128)(2,1)S(1)} collective-permute-done((bf16[592,128]{1,0:T(8,128)(2,1)S(1)}, bf16[592,128]{1,0:T(8,128)(2,1)S(1)}, u32[]{:S(2)}, u32[]{:S(2)}) %collective-permute-start.7) | collective-permute-done | bytes 151584 | tf_op jit(solution)/shard_map/ppermute | solution.py:436
  51.0 1.6 %collective-permute-done.14.refs_1_ = bf16[592,128]{1,0:T(8,128)(2,1)S(1)} collective-permute-done((bf16[592,128]{1,0:T(8,128)(2,1)S(1)}, bf16[592,128]{1,0:T(8,128)(2,1)S(1)}, u32[]{:S(2)}, u32[]{:S(2)}) %collective-permute-start.14) | collective-permute-done | bytes 151584 | tf_op jit(solution)/shard_map/ppermute | solution.py:439
  52.6 0.1 gather.1
  52.7 0.1 collective-permute-start.15
  52.7 0.1 collective-permute-start.16
  52.8 2.1 %collective-permute-start.17 = (bf16[128,128]{1,0:T(8,128)(2,1)S(1)}, bf16[128,128]{1,0:T(8,128)(2,1)S(1)}, u32[]{:S(2)}, u32[]{:S(2)}) collective-permute-start(bf16[128,128]{1,0:T(8,128)(2,1)S(1)} %get-tuple-element.64), channel_id=1, source_target_pairs={{0,3},{1,4},{2,5},{3,6},{4,7},{5,0},{6,1},{7,2},{8,11},{9,12},{10,... | collective-permute-start | bytes 98312 | tf_op jit(solution)/shard_map/ppermute | solution.py:504
  54.9 1.0 %collective-permute-start.18 = (bf16[64,128]{1,0:T(8,128)(2,1)S(1)}, bf16[64,128]{1,0:T(8,128)(2,1)S(1)}, u32[]{:S(2)}, u32[]{:S(2)}) collective-permute-start(bf16[64,128]{1,0:T(8,128)(2,1)S(1)} %get-tuple-element.65), channel_id=1, source_target_pairs={{0,4},{1,5},{2,6},{3,7},{4,0},{5,1},{6,2},{7,3},{8,12},{9,13},{10,... | collective-permute-start | bytes 49160 | tf_op jit(solution)/shard_map/ppermute | solution.py:504
  56.0 2.7 %collective-permute-done.18.e_ref = bf16[64,128]{1,0:T(8,128)(2,1)S(1)} collective-permute-done((bf16[64,128]{1,0:T(8,128)(2,1)S(1)}, bf16[64,128]{1,0:T(8,128)(2,1)S(1)}, u32[]{:S(2)}, u32[]{:S(2)}) %collective-permute-start.18) | collective-permute-done | bytes 16416 | tf_op jit(solution)/shard_map/ppermute | solution.py:504
  58.7 0.9 %finish.1 = (f32[128,1024]{1,0:T(8,128)}, f32[1,128]{1,0:T(1,128)}) custom-call(f32[592,128]{1,0:T(8,128)S(1)} %get-tuple-element.61.own_ref, bf16[128,128]{1,0:T(8,128)(2,1)S(1)} %collective-permute-done.15.r1_ref, bf16[128,128]{1,0:T(8,128)(2,1)S(1)} %collective-permute-done.16.r2_ref, bf16[128,128]{1,0:T(8,128)(2,1)S(1)} %collective-permute-done.17.r3_ref, ...), custom_call_target="tpu_custom_call" | custom-call | tf_op jit(solution)/shard_map/finish/pallas_call | solution.py:402
  (24 shorter events, 0.2 us)
Async XLA Ops:
  0.6 8.3 %copy-start = (bf16[192,32,128]{2,1,0:T(8,128)(2,1)S(1)}, bf16[192,32,128]{2,1,0:T(8,128)(2,1)}, u32[]{:S(2)}) copy-start(bf16[192,32,128]{2,1,0:T(8,128)(2,1)} %g_ref.5) | copy-start | bytes 4718596
  8.4 5.7 %collective-permute-start = (bf16[4,1,592,128]{3,2,0,1:T(8,128)(2,1)}, bf16[4,1,592,128]{3,2,0,1:T(8,128)(2,1)S(1)}, u32[]{:S(2)}, u32[]{:S(2)}) collective-permute-start(bf16[4,1,592,128]{3,2,0,1:T(8,128)(2,1)} %bitcast.76), channel_id=1, source_target_pairs={{0,1},{1,0},{2,3},{3,2},{4,5},{5,4},{6,7},{7,6},{8,9},{9,8},{10,11... | collective-permute-start | bytes 1818632 | tf_op jit(solution)/shard_map/ppermute | solution.py:436
  9.0 1.4 %copy-start.1 = (f32[1600,256]{1,0:T(8,128)S(1)}, f32[1600,256]{1,0:T(8,128)}, u32[]{:S(2)}) copy-start(f32[1600,256]{1,0:T(8,128)} %get-tuple-element.35.shared_ref) | copy-start | bytes 4915204
  10.4 0.7 %copy-start.3 = (s32[16,256]{1,0:T(8,128)S(1)}, s32[16,256]{1,0:T(8,128)}, u32[]{:S(2)}) copy-start(s32[16,256]{1,0:T(8,128)} %get-tuple-element.49.table_ref) | copy-start | bytes 49156
  11.1 3.0 %copy-start.5 = (bf16[4,1,592,128]{3,2,1,0:T(8,128)(2,1)S(1)}, bf16[4,1,592,128]{3,2,1,0:T(8,128)(2,1)}, u32[]{:S(2)}) copy-start(bf16[4,1,592,128]{3,2,1,0:T(8,128)(2,1)} %get-tuple-element.41) | copy-start | bytes 1818628
  11.1 4.7 %copy-start.2 = (f32[1600,256]{1,0:T(8,128)S(1)}, f32[1600,256]{1,0:T(8,128)}, u32[]{:S(2)}) copy-start(f32[1600,256]{1,0:T(8,128)} %get-tuple-element.35.shared_ref) | copy-start | bytes 4915204
  11.1 4.7 %copy-start.4 = (s32[16,256]{1,0:T(8,128)S(1)}, s32[16,256]{1,0:T(8,128)}, u32[]{:S(2)}) copy-start(s32[16,256]{1,0:T(8,128)} %get-tuple-element.49.table_ref) | copy-start | bytes 49156
  14.0 4.2 %collective-permute-start.2 = (bf16[4,1,592,128]{3,2,0,1:T(8,128)(2,1)S(1)}, bf16[4,1,592,128]{3,2,0,1:T(8,128)(2,1)S(1)}, u32[]{:S(2)}, u32[]{:S(2)}) collective-permute-start(bf16[4,1,592,128]{3,2,0,1:T(8,128)(2,1)S(1)} %bitcast.73), channel_id=1, source_target_pairs={{0,1},{1,0},{2,3},{3,2},{4,5},{5,4},{6,7},{7,6},{8,9},{9,8},{10,11... | collective-permute-start | bytes 1818632 | tf_op jit(solution)/shard_map/ppermute | solution.py:436
  14.2 6.9 %collective-permute-start.1 = (bf16[2,592,128]{2,1,0:T(8,128)(2,1)S(1)}, bf16[2,592,128]{2,1,0:T(8,128)(2,1)S(1)}, u32[]{:S(2)}, u32[]{:S(2)}) collective-permute-start(bf16[2,592,128]{2,1,0:T(8,128)(2,1)S(1)} %fusion), channel_id=1, source_target_pairs={{0,2},{1,5},{2,0},{3,7},{4,6},{5,1},{6,4},{7,3},{8,10},{9,13},{10,... | collective-permute-start | bytes 909320 | tf_op jit(solution)/shard_map/ppermute | solution.py:436
  18.3 11.3 %collective-permute-start.4 = (bf16[2,592,128]{2,1,0:T(8,128)(2,1)S(1)}, bf16[2,592,128]{2,1,0:T(8,128)(2,1)S(1)}, u32[]{:S(2)}, u32[]{:S(2)}) collective-permute-start(bf16[2,592,128]{2,1,0:T(8,128)(2,1)S(1)} %fusion.1), channel_id=1, source_target_pairs={{0,2},{1,5},{2,0},{3,7},{4,6},{5,1},{6,4},{7,3},{8,10},{9,13},{10,... | collective-permute-start | bytes 909320 | tf_op jit(solution)/shard_map/ppermute | solution.py:436
  19.3 14.1 %collective-permute-start.11 = (bf16[4,1,592,128]{3,2,0,1:T(8,128)(2,1)S(1)}, bf16[4,1,592,128]{3,2,0,1:T(8,128)(2,1)S(1)}, u32[]{:S(2)}, u32[]{:S(2)}) collective-permute-start(bf16[4,1,592,128]{3,2,0,1:T(8,128)(2,1)S(1)} %bitcast.71), channel_id=1, source_target_pairs={{0,1},{1,0},{2,3},{3,2},{4,5},{5,4},{6,7},{7,6},{8,9},{9,8},{10,11... | collective-permute-start | bytes 1818632 | tf_op jit(solution)/shard_map/ppermute | solution.py:436
  21.2 9.3 %collective-permute-start.8 = (bf16[592,128]{1,0:T(8,128)(2,1)S(1)}, bf16[592,128]{1,0:T(8,128)(2,1)S(1)}, u32[]{:S(2)}, u32[]{:S(2)}) collective-permute-start(bf16[592,128]{1,0:T(8,128)(2,1)S(1)} %fusion.12), channel_id=1, source_target_pairs={{0,4},{1,3},{2,6},{3,1},{4,0},{5,7},{6,2},{7,5},{8,12},{9,11},{10,... | collective-permute-start | bytes 454664 | tf_op jit(solution)/shard_map/ppermute | solution.py:436
  29.7 5.4 %collective-permute-start.3 = (bf16[4,1,592,128]{3,2,0,1:T(8,128)(2,1)S(1)}, bf16[4,1,592,128]{3,2,0,1:T(8,128)(2,1)S(1)}, u32[]{:S(2)}, u32[]{:S(2)}) collective-permute-start(bf16[4,1,592,128]{3,2,0,1:T(8,128)(2,1)S(1)} %bitcast.72), channel_id=1, source_target_pairs={{0,1},{1,0},{2,3},{3,2},{4,5},{5,4},{6,7},{7,6},{8,9},{9,8},{10,11... | collective-permute-start | bytes 1818632 | tf_op jit(solution)/shard_map/ppermute | solution.py:436
  29.8 5.3 %collective-permute-start.5 = (bf16[592,128]{1,0:T(8,128)(2,1)S(1)}, bf16[592,128]{1,0:T(8,128)(2,1)S(1)}, u32[]{:S(2)}, u32[]{:S(2)}) collective-permute-start(bf16[592,128]{1,0:T(8,128)(2,1)S(1)} %fusion.13), channel_id=1, source_target_pairs={{0,4},{1,3},{2,6},{3,1},{4,0},{5,7},{6,2},{7,5},{8,12},{9,11},{10,... | collective-permute-start | bytes 454664 | tf_op jit(solution)/shard_map/ppermute | solution.py:436
  30.6 7.2 %collective-permute-start.9 = (bf16[592,128]{1,0:T(8,128)(2,1)S(1)}, bf16[592,128]{1,0:T(8,128)(2,1)S(1)}, u32[]{:S(2)}, u32[]{:S(2)}) collective-permute-start(bf16[592,128]{1,0:T(8,128)(2,1)S(1)} %fusion.7), channel_id=1, source_target_pairs={{0,8},{8,0},{16,24},{24,16},{1,9},{9,1},{17,25},{25,17},{2,10},{10... | collective-permute-start | bytes 454664 | tf_op jit(solution)/shard_map/ppermute | solution.py:439
  33.6 6.9 %collective-permute-start.12 = (bf16[2,592,128]{2,1,0:T(8,128)(2,1)S(1)}, bf16[2,592,128]{2,1,0:T(8,128)(2,1)S(1)}, u32[]{:S(2)}, u32[]{:S(2)}) collective-permute-start(bf16[2,592,128]{2,1,0:T(8,128)(2,1)S(1)} %fusion.3), channel_id=1, source_target_pairs={{0,2},{1,5},{2,0},{3,7},{4,6},{5,1},{6,4},{7,3},{8,10},{9,13},{10,... | collective-permute-start | bytes 909320 | tf_op jit(solution)/shard_map/ppermute | solution.py:436
  35.2 10.4 %collective-permute-start.6 = (bf16[2,592,128]{2,1,0:T(8,128)(2,1)S(1)}, bf16[2,592,128]{2,1,0:T(8,128)(2,1)S(1)}, u32[]{:S(2)}, u32[]{:S(2)}) collective-permute-start(bf16[2,592,128]{2,1,0:T(8,128)(2,1)S(1)} %fusion.2), channel_id=1, source_target_pairs={{0,2},{1,5},{2,0},{3,7},{4,6},{5,1},{6,4},{7,3},{8,10},{9,13},{10,... | collective-permute-start | bytes 909320 | tf_op jit(solution)/shard_map/ppermute | solution.py:436
  37.9 13.1 %collective-permute-start.10 = (bf16[592,128]{1,0:T(8,128)(2,1)S(1)}, bf16[592,128]{1,0:T(8,128)(2,1)S(1)}, u32[]{:S(2)}, u32[]{:S(2)}) collective-permute-start(bf16[592,128]{1,0:T(8,128)(2,1)S(1)} %fusion.10), channel_id=1, source_target_pairs={{0,16},{8,24},{16,0},{24,8},{1,17},{9,25},{17,1},{25,9},{2,18},{10... | collective-permute-start | bytes 454664 | tf_op jit(solution)/shard_map/ppermute | solution.py:439
  40.6 5.3 %collective-permute-start.13 = (bf16[592,128]{1,0:T(8,128)(2,1)S(1)}, bf16[592,128]{1,0:T(8,128)(2,1)S(1)}, u32[]{:S(2)}, u32[]{:S(2)}) collective-permute-start(bf16[592,128]{1,0:T(8,128)(2,1)S(1)} %fusion.15), channel_id=1, source_target_pairs={{0,4},{1,3},{2,6},{3,1},{4,0},{5,7},{6,2},{7,5},{8,12},{9,11},{10,... | collective-permute-start | bytes 454664 | tf_op jit(solution)/shard_map/ppermute | solution.py:436
  45.7 5.3 %collective-permute-start.7 = (bf16[592,128]{1,0:T(8,128)(2,1)S(1)}, bf16[592,128]{1,0:T(8,128)(2,1)S(1)}, u32[]{:S(2)}, u32[]{:S(2)}) collective-permute-start(bf16[592,128]{1,0:T(8,128)(2,1)S(1)} %fusion.14), channel_id=1, source_target_pairs={{0,4},{1,3},{2,6},{3,1},{4,0},{5,7},{6,2},{7,5},{8,12},{9,11},{10,... | collective-permute-start | bytes 454664 | tf_op jit(solution)/shard_map/ppermute | solution.py:436
  45.9 6.7 %collective-permute-start.14 = (bf16[592,128]{1,0:T(8,128)(2,1)S(1)}, bf16[592,128]{1,0:T(8,128)(2,1)S(1)}, u32[]{:S(2)}, u32[]{:S(2)}) collective-permute-start(bf16[592,128]{1,0:T(8,128)(2,1)S(1)} %fusion.5), channel_id=1, source_target_pairs={{0,8},{8,0},{16,24},{24,16},{1,9},{9,1},{17,25},{25,17},{2,10},{10... | collective-permute-start | bytes 454664 | tf_op jit(solution)/shard_map/ppermute | solution.py:439
  52.7 6.0 %collective-permute-start.15 = (bf16[128,128]{1,0:T(8,128)(2,1)S(1)}, bf16[128,128]{1,0:T(8,128)(2,1)S(1)}, u32[]{:S(2)}, u32[]{:S(2)}) collective-permute-start(bf16[128,128]{1,0:T(8,128)(2,1)S(1)} %get-tuple-element.62), channel_id=1, source_target_pairs={{0,1},{1,2},{2,3},{3,4},{4,5},{5,6},{6,7},{7,0},{8,9},{9,10},{10,1... | collective-permute-start | bytes 98312 | tf_op jit(solution)/shard_map/ppermute | solution.py:504
  52.7 5.9 %collective-permute-start.16 = (bf16[128,128]{1,0:T(8,128)(2,1)S(1)}, bf16[128,128]{1,0:T(8,128)(2,1)S(1)}, u32[]{:S(2)}, u32[]{:S(2)}) collective-permute-start(bf16[128,128]{1,0:T(8,128)(2,1)S(1)} %get-tuple-element.63), channel_id=1, source_target_pairs={{0,2},{1,3},{2,4},{3,5},{4,6},{5,7},{6,0},{7,1},{8,10},{9,11},{10,... | collective-permute-start | bytes 98312 | tf_op jit(solution)/shard_map/ppermute | solution.py:504
  52.8 5.9 %collective-permute-start.17 = (bf16[128,128]{1,0:T(8,128)(2,1)S(1)}, bf16[128,128]{1,0:T(8,128)(2,1)S(1)}, u32[]{:S(2)}, u32[]{:S(2)}) collective-permute-start(bf16[128,128]{1,0:T(8,128)(2,1)S(1)} %get-tuple-element.64), channel_id=1, source_target_pairs={{0,3},{1,4},{2,5},{3,6},{4,7},{5,0},{6,1},{7,2},{8,11},{9,12},{10,... | collective-permute-start | bytes 98312 | tf_op jit(solution)/shard_map/ppermute | solution.py:504
  54.9 3.8 %collective-permute-start.18 = (bf16[64,128]{1,0:T(8,128)(2,1)S(1)}, bf16[64,128]{1,0:T(8,128)(2,1)S(1)}, u32[]{:S(2)}, u32[]{:S(2)}) collective-permute-start(bf16[64,128]{1,0:T(8,128)(2,1)S(1)} %get-tuple-element.65), channel_id=1, source_target_pairs={{0,4},{1,5},{2,6},{3,7},{4,0},{5,1},{6,2},{7,3},{8,12},{9,13},{10,... | collective-permute-start | bytes 49160 | tf_op jit(solution)/shard_map/ppermute | solution.py:504
